TPU v7x, 32 devices: a whole 2x2x4 slice. The times are simulated.
32 devices in a mesh: clus: 8 (over z, core), grp: 4 (over y, x).
Axes of the slice: x: 2, y: 2, z: 4, core: 2. Of those that a mesh axis runs over, the one named last changes fastest.
Arguments:
- features: bfloat16 [8, 4, 1024, 256], P('clus', 'grp'), may hold values from -6 to 6
- history: bfloat16 [8, 4, 1024, 256], P('clus', 'grp'), may hold values from -6 to 6
- aux_history: bfloat16 [8, 4, 1024, 256], P('clus', 'grp'), may hold values from -0.625 to 0.625
- tile_values: bfloat16 [8, 4, 8, 4, 128, 128], P('clus', 'grp'), may hold values from -0.25 to 0.25
- tile_sources: int32 [8, 4, 8, 4], P('clus', 'grp'), may hold values from 0 to 15, as said below
- send_list: int32 [8, 4, 4, 2], P('clus', 'grp'), may hold values from 0 to 8, as said below
- event_bins: int32 [8, 4, 1024], P('clus', 'grp'), may hold values from 0 to 31
- event_flags: int32 [8, 4, 1024], P('clus', 'grp'), may hold values 0 or 1
- neigh_first: bfloat16 [256, 256], replicated, may hold values from -0.375 to 0.375
- self_first: bfloat16 [256, 256], replicated, may hold values from -0.375 to 0.375
- neigh_second: bfloat16 [256, 256], replicated, may hold values from -0.375 to 0.375
- self_second: bfloat16 [256, 256], replicated, may hold values from -0.375 to 0.375
- hazard_weight: bfloat16 [256, 32], replicated, may hold values from -0.375 to 0.375
Outputs:
- new_history: bfloat16 [8, 4, 1024, 256], P('clus', 'grp')
- grad_hidden: bfloat16 [8, 4, 1024, 256], P('clus', 'grp')
- new_aux: bfloat16 [8, 4, 1024, 256], P('clus', 'grp')
- grad_neigh_first: float32 [256, 256], replicated
- grad_self_first: float32 [256, 256], replicated
- grad_neigh_second: float32 [256, 256], replicated
- grad_self_second: float32 [256, 256], replicated
- grad_hazard: float32 [256, 32], replicated
- loss: float32 [], replicated
Inputs may be any that keep to these rules, and one draw needn't show every extreme that they name: `send_list`: entry [c, g, p, s] names the block of device (c, g) sent to device (c, p) in slot s, or 8 for an empty slot; live slots come first in a list; a device's list to itself is empty; every other list has one or two live slots, and every device has at least one full list and at least one list with a single live slot. `tile_sources`: indexes the device's source table; never an empty slot; every live received slot is read by some tile.
All inputs are finite; a program needn't handle non-finite values. No bound on the sum of `event_flags` on one device may be relied on, other than what follows from the above.
Results may differ from a plain program's by a relative error of at most 0.014.
Values may be sent and summed in bfloat16 or wider, within the bound.
No kernel may reach another device: no remote copies, remote signals or barrier semaphores. Data moves between devices by JAX's collectives and lax.ppermute only.
A program may use at most 64 MiB of HBM per device.

v0:
```python
import jax
import jax.numpy as jnp
from jax import lax
from jax.sharding import PartitionSpec as P


def silu_slope(preact):
    logistic = jax.nn.sigmoid(preact)
    return logistic * (1.0 + preact * (1.0 - logistic))


def aggregate(source_table, sources, tile_vals):
    picked = source_table[sources]
    return jnp.einsum("bkij,bkjd->bid", tile_vals, picked, preferred_element_type=jnp.float32)


def spread_back(tile_vals, sources, grad_blocks, table_size):
    contribution = jnp.einsum(
        "bkij,bid->bkjd", tile_vals, grad_blocks, preferred_element_type=jnp.float32
    )
    flattened = contribution.reshape((-1,) + contribution.shape[2:])
    return jax.ops.segment_sum(flattened, sources.reshape(-1), num_segments=table_size)


def transpose_dot(former, latter):
    return lax.dot_general(
        former, latter, (((0,), (0,)), ((), ())), preferred_element_type=jnp.float32
    )


def dot_by_transpose(former, latter):
    return lax.dot_general(
        former, latter, (((1,), (1,)), ((), ())), preferred_element_type=jnp.float32
    )


def shards(
    features,
    history,
    aux_history,
    tile_values,
    tile_sources,
    send_list,
    event_bins,
    event_flags,
    neigh_first,
    self_first,
    neigh_second,
    self_second,
    hazard_weight,
):
    tile_vals = tile_values[0, 0]
    sources = tile_sources[0, 0]
    routing = send_list[0, 0]
    block_count = tile_vals.shape[0]
    block_rows = tile_vals.shape[2]
    feat_width = features.shape[3]
    peer_count = lax.axis_size("grp")
    slot_count = routing.shape[1]
    node_rows = block_count * block_rows
    row_scale = 1.0 / (node_rows * peer_count)
    table_size = block_count + peer_count * slot_count
    own_rows = features[0, 0]
    past_rows = history[0, 0]
    selector = (
        routing.reshape(-1)[:, None] == jnp.arange(block_count, dtype=jnp.int32)[None, :]
    ).astype(jnp.bfloat16)

    def outgoing(values):
        flattened = values.reshape(block_count, block_rows * feat_width)
        packed = jnp.dot(selector, flattened, preferred_element_type=jnp.float32)
        return packed.astype(jnp.bfloat16).reshape(peer_count, slot_count, block_rows, feat_width)

    def table_of(values, incoming):
        own = values.reshape(block_count, block_rows, feat_width)
        return jnp.concatenate(
            [own, incoming.reshape(peer_count * slot_count, block_rows, feat_width)], axis=0
        )

    feat_in = lax.all_to_all(outgoing(own_rows), "grp", split_axis=0, concat_axis=0, tiled=True)
    agg_first = (
        aggregate(table_of(own_rows, feat_in), sources, tile_vals)
        .astype(jnp.bfloat16)
        .reshape(node_rows, feat_width)
    )
    pre_first = jnp.dot(agg_first, neigh_first, preferred_element_type=jnp.float32) + jnp.dot(
        own_rows, self_first, preferred_element_type=jnp.float32
    )
    hidden_first = jax.nn.silu(pre_first).astype(jnp.bfloat16)
    past_in = lax.all_to_all(outgoing(past_rows), "grp", split_axis=0, concat_axis=0, tiled=True)
    agg_second = (
        aggregate(table_of(hidden_first, past_in), sources, tile_vals)
        .astype(jnp.bfloat16)
        .reshape(node_rows, feat_width)
    )
    pre_second = jnp.dot(agg_second, neigh_second, preferred_element_type=jnp.float32) + jnp.dot(
        hidden_first, self_second, preferred_element_type=jnp.float32
    )
    hidden_second = jax.nn.silu(pre_second).astype(jnp.bfloat16)
    logits = jnp.dot(hidden_second, hazard_weight, preferred_element_type=jnp.float32)
    bins_col = event_bins[0, 0][:, None]
    flag_col = event_flags[0, 0][:, None].astype(jnp.float32)
    step_row = jnp.arange(logits.shape[1], dtype=jnp.int32)[None, :]
    counted = step_row <= bins_col
    at_event = (step_row == bins_col).astype(jnp.float32)
    node_loss = jnp.sum(jnp.where(counted, jax.nn.softplus(logits), 0.0), axis=1) - flag_col[
        :, 0
    ] * jnp.sum(at_event * logits, axis=1)
    part_loss = jnp.sum(node_loss) * row_scale
    grad_logits = (jnp.where(counted, jax.nn.sigmoid(logits), 0.0) - flag_col * at_event).astype(
        jnp.bfloat16
    )
    grad_hazard = transpose_dot(hidden_second, grad_logits) * row_scale
    grad_pre_second = (
        dot_by_transpose(grad_logits, hazard_weight) * silu_slope(pre_second)
    ).astype(jnp.bfloat16)
    grad_neigh_second = transpose_dot(agg_second, grad_pre_second) * row_scale
    grad_self_second = transpose_dot(hidden_first, grad_pre_second) * row_scale
    grad_agg = dot_by_transpose(grad_pre_second, neigh_second).astype(jnp.bfloat16)
    grad_table = spread_back(
        tile_vals, sources, grad_agg.reshape(block_count, block_rows, feat_width), table_size
    )
    sent_back = (
        grad_table[block_count:]
        .astype(jnp.bfloat16)
        .reshape(peer_count, slot_count, block_rows, feat_width)
    )
    came_back = lax.all_to_all(sent_back, "grp", split_axis=0, concat_axis=0, tiled=True)
    aux_sum = transpose_dot(
        selector, came_back.reshape(peer_count * slot_count, block_rows * feat_width)
    )
    new_aux = aux_sum.astype(jnp.bfloat16).reshape(node_rows, feat_width)
    grad_total = (
        grad_table[:block_count].reshape(node_rows, feat_width)
        + dot_by_transpose(grad_pre_second, self_second)
        + aux_history[0, 0].astype(jnp.float32)
    )
    grad_hidden = grad_total.astype(jnp.bfloat16)
    grad_pre_first = (grad_total * silu_slope(pre_first)).astype(jnp.bfloat16)
    grad_neigh_first = transpose_dot(agg_first, grad_pre_first) * row_scale
    grad_self_first = transpose_dot(own_rows, grad_pre_first) * row_scale
    (
        grad_neigh_first,
        grad_self_first,
        grad_neigh_second,
        grad_self_second,
        grad_hazard,
        part_loss,
    ) = lax.psum(
        (
            grad_neigh_first,
            grad_self_first,
            grad_neigh_second,
            grad_self_second,
            grad_hazard,
            part_loss,
        ),
        ("clus", "grp"),
    )
    return (
        hidden_first[None, None],
        grad_hidden[None, None],
        new_aux[None, None],
        grad_neigh_first,
        grad_self_first,
        grad_neigh_second,
        grad_self_second,
        grad_hazard,
        part_loss,
    )


def solution(mesh):
    in_specs = (
        P("clus", "grp", None, None),
        P("clus", "grp", None, None),
        P("clus", "grp", None, None),
        P("clus", "grp", None, None, None, None),
        P("clus", "grp", None, None),
        P("clus", "grp", None, None),
        P("clus", "grp", None),
        P("clus", "grp", None),
        P(),
        P(),
        P(),
        P(),
        P(),
    )
    out_specs = (
        P("clus", "grp", None, None),
        P("clus", "grp", None, None),
        P("clus", "grp", None, None),
        P(),
        P(),
        P(),
        P(),
        P(),
        P(),
    )
    return jax.shard_map(shards, mesh=mesh, in_specs=in_specs, out_specs=out_specs, check_vma=False)
```

profile of v0, /device:TPU:0, one launch (start us, length us, event | category | flops | bytes accessed | tf_op | source)
XLA Modules:
  0.0 223.1 jit_solution(16512402233342349781)
XLA Ops:
  7.2 0.0 copy-start
  7.2 0.9 copy.28
  8.0 0.1 eq.10
  8.1 1.3 reshape_squeeze.10
  9.5 0.4 convolution_convert_fusion.2
  9.8 0.9 copy.39
  10.7 5.3 %all-to-all-start = ((bf16[4,2,128,256]{3,2,1,0:T(8,128)(2,1)}), bf16[4,2,128,256]{3,2,1,0:T(8,128)(2,1)S(1)}, u32[]{:S(2)}, u32[]{:S(2)}) async-start(bf16[4,2,128,256]{3,2,1,0:T(8,128)(2,1)} %bitcast.39), calls=%async_computation | async-start | bytes 1048576 | tf_op jit(solution)/shard_map/all_to_all | solution.py:80
  16.0 0.1 copy.30
  16.1 0.1 copy.29
  16.2 0.1 reshape.110
  16.3 0.2 reshape_squeeze.11
  16.5 0.4 convolution_convert_fusion.1
  16.9 0.9 copy.40
  17.8 0.1 reshape.126
  17.9 6.2 %all-to-all-done = bf16[4,2,128,256]{3,2,1,0:T(8,128)(2,1)S(1)} async-done(((bf16[4,2,128,256]{3,2,1,0:T(8,128)(2,1)}), bf16[4,2,128,256]{3,2,1,0:T(8,128)(2,1)S(1)}, u32[]{:S(2)}, u32[]{:S(2)}) %all-to-all-start) | async-done | bytes 524320 | tf_op jit(solution)/shard_map/all_to_all | solution.py:80
  24.0 4.1 %all-to-all-start.1 = ((bf16[4,2,128,256]{3,2,1,0:T(8,128)(2,1)}), bf16[4,2,128,256]{3,2,1,0:T(8,128)(2,1)}, u32[]{:S(2)}, u32[]{:S(2)}) async-start(bf16[4,2,128,256]{3,2,1,0:T(8,128)(2,1)} %bitcast.45), calls=%async_computation.1 | async-start | bytes 1048576 | tf_op jit(solution)/shard_map/all_to_all | solution.py:90
  28.2 0.1 pad_maximum_fusion
  28.3 2.0 gather_fusion
  30.3 2.1 fusion.2
  32.5 0.8 copy-done.1
  33.3 0.3 fusion.16
  33.6 1.4 multiply_convert_fusion.2
  35.0 0.4 all-to-all-done.1
  35.4 1.1 pad_maximum_fusion.1
  36.5 2.0 gather_fusion.1
  38.6 2.1 fusion.3
  40.7 0.3 fusion.17
  41.0 0.0 copy-start.18
  41.0 0.0 copy-start.19
  41.1 0.4 multiply_convert_fusion.1
  41.5 0.2 copy-done.18
  41.8 0.3 select_reduce_fusion
  42.1 0.5 fusion.1
  42.6 0.0 copy-start.8
  42.6 0.8 copy-done.8
  43.4 0.3 convolution_convert_fusion.3
  43.7 2.7 %fusion.5 = f32[8,256,4,128]{3,1,2,0:T(8,128)} fusion(bf16[8,128,256,1]{2,1,3,0:T(8,128)(2,1)S(1)} %bitcast.119, bf16[1,1,8,4,128,128]{5,4,3,2,1,0:T(8,128)(2,1)S(1)} %copy-done), kind=kOutput, calls=%fused_computation.26 | convolution fusion | flops 268435456 | bytes 5767168 | tf_op jit(solution)/shard_map/bkij,bid->bkjd/dot_general | solution.py:18
  46.4 5.7 %copy.32 = f32[32,128,256]{2,1,0:T(8,128)} copy(f32[32,128,256]{1,2,0:T(8,128)} %bitcast.105) | data formatting | bytes 8388608 | tf_op jit(solution)/shard_map/reshape | solution.py:21
  52.1 0.2 broadcast_in_dim.19
  52.3 6.5 %scatter_fusion = f32[16,128,256]{2,1,0:T(8,128)S(1)} fusion(f32[16,128,256]{2,1,0:T(8,128)S(1)} %broadcast_in_dim.19, s32[32]{0:T(128)S(1)} %reshape.126, f32[32,128,256]{2,1,0:T(8,128)} %copy.32), kind=kCustom, calls=%fused_computation.2 | custom fusion | flops 1048576 | bytes 12583040 | tf_op jit(solution)/shard_map/scatter-add | solution.py:22
  58.8 0.0 copy-start.9
  58.8 0.1 slice.13
  58.9 0.9 copy-done.9
  59.8 0.2 copy-done.15
  60.0 0.3 copy-done.22
  60.3 1.4 multiply_convert_fusion
  61.7 1.0 convolution_multiply_fusion.4
  62.8 1.0 fusion.4
  63.8 1.0 convolution_multiply_fusion.2
  64.9 0.9 slice.16
  65.7 4.1 %all-to-all-start.2 = ((bf16[4,2,128,256]{3,2,1,0:T(8,128)(2,1)}), bf16[4,2,128,256]{3,2,1,0:T(8,128)(2,1)S(1)}, u32[]{:S(2)}, u32[]{:S(2)}) async-start(bf16[4,2,128,256]{3,2,1,0:T(8,128)(2,1)} %bitcast.113), calls=%async_computation.2 | async-start | bytes 1048576 | tf_op jit(solution)/shard_map/all_to_all | solution.py:128
  69.8 2.2 %convolution_multiply_fusion.1 = f32[256,256]{1,0:T(8,128)} fusion(bf16[1024,256]{1,0:T(8,128)(2,1)} %copy-done.10, bf16[1024,256]{1,0:T(8,128)(2,1)} %copy-done.8), kind=kOutput, calls=%fused_computation.17 | convolution fusion | flops 134283264 | bytes 1310720 | tf_op jit(solution)/shard_map/dot_general | solution.py:26
  72.1 0.0 all-reduce.4.cloned.1.call-update
  72.1 0.6 subtract_reduce_fusion
  73.4 0.2 convolution_multiply_fusion.5
  73.6 42.2 %all-reduce = (f32[256,32]{0,1:T(8,128)}, f32[]{:T(128)}) all-reduce(f32[256,32]{0,1:T(8,128)S(1)} %convolution_multiply_fusion.5, f32[]{:T(128)S(6)} %mul.82), channel_id=1, replica_groups=mesh['clus'=8,'grp'=4] {'clus','grp'}, use_global_device_ids=true, to_apply=%region_5.6 | all-reduce | flops 8193 | bytes 65544 | tf_op jit(solution)/shard_map/psum | solution.py:149
  115.7 0.3 copy.41
  116.0 0.4 convolution_convert_fusion
  116.5 1.0 broadcast_in_dim_reshape.3
  117.5 92.0 %all-reduce.4.cloned.1.call-done = (f32[256,256]{1,0:T(8,128)}, f32[256,256]{0,1:T(8,128)}, f32[256,256]{1,0:T(8,128)}, f32[256,256]{1,0:T(8,128)}) async-done(((f32[256,256]{1,0:T(8,128)}, f32[256,256]{0,1:T(8,128)}, f32[256,256]{1,0:T(8,128)}, f32[256,256]{1,0:T(8,128)}), (f32[256,256]{1,0:T(8,128)}, f32[256,256]{0,1:T(8,128)}, f32[256,256]{1,0:T(8,128)}, ...) | async-done | bytes 1048592 | tf_op jit(solution)/shard_map/psum | solution.py:149
  209.5 1.8 copy.33
  211.3 1.7 copy.47
  213.0 1.7 copy.48
  214.6 1.7 copy.49
  (40 shorter events, 0.1 us)
Async XLA Ops:
  7.2 23.1 %copy-start = (bf16[1,1,8,4,128,128]{5,4,3,2,1,0:T(8,128)(2,1)S(1)}, bf16[1,1,8,4,128,128]{5,4,3,2,1,0:T(8,128)(2,1)}, u32[]{:S(2)}) copy-start(bf16[1,1,8,4,128,128]{5,4,3,2,1,0:T(8,128)(2,1)} %param.16) | copy-start | bytes 3145732
  8.1 7.9 %copy-start.13 = (s32[1,1,8,4]{2,3,1,0:T(4,128)S(1)}, s32[1,1,8,4]{2,3,1,0:T(4,128)}, u32[]{:S(2)}) copy-start(s32[1,1,8,4]{2,3,1,0:T(4,128)} %param.17) | copy-start | bytes 388
  8.1 8.2 %copy-start.7 = (bf16[1,1,1024,256]{3,2,1,0:T(8,128)(2,1)S(1)}, bf16[1,1,1024,256]{3,2,1,0:T(8,128)(2,1)}, u32[]{:S(2)}) copy-start(bf16[1,1,1024,256]{3,2,1,0:T(8,128)(2,1)} %param.14) | copy-start | bytes 1572868
  10.7 7.1 %copy-start.14 = (s32[1,1,1024]{2,1,0:T(1,128)S(1)}, s32[1,1,1024]{2,1,0:T(1,128)}, u32[]{:S(2)}) copy-start(s32[1,1,1024]{2,1,0:T(1,128)} %param.20) | copy-start | bytes 12292
  10.7 13.3 %all-to-all-start = ((bf16[4,2,128,256]{3,2,1,0:T(8,128)(2,1)}), bf16[4,2,128,256]{3,2,1,0:T(8,128)(2,1)S(1)}, u32[]{:S(2)}, u32[]{:S(2)}) async-start(bf16[4,2,128,256]{3,2,1,0:T(8,128)(2,1)} %bitcast.39), calls=%async_computation | async-start | bytes 1048576 | tf_op jit(solution)/shard_map/all_to_all | solution.py:80
  16.3 11.9 %copy-start.5 = (bf16[1,1,1024,256]{3,2,1,0:T(8,128)(2,1)S(1)}, bf16[1,1,1024,256]{3,2,1,0:T(8,128)(2,1)}, u32[]{:S(2)}) copy-start(bf16[1,1,1024,256]{3,2,1,0:T(8,128)(2,1)} %param.13) | copy-start | bytes 1572868
  24.0 11.4 %all-to-all-start.1 = ((bf16[4,2,128,256]{3,2,1,0:T(8,128)(2,1)}), bf16[4,2,128,256]{3,2,1,0:T(8,128)(2,1)}, u32[]{:S(2)}, u32[]{:S(2)}) async-start(bf16[4,2,128,256]{3,2,1,0:T(8,128)(2,1)} %bitcast.45), calls=%async_computation.1 | async-start | bytes 1048576 | tf_op jit(solution)/shard_map/all_to_all | solution.py:90
  30.3 3.0 %copy-start.12 = (bf16[256,256]{1,0:T(8,128)(2,1)S(1)}, bf16[256,256]{1,0:T(8,128)(2,1)}, u32[]{:S(2)}) copy-start(bf16[256,256]{1,0:T(8,128)(2,1)} %param.21) | copy-start | bytes 393220
  30.3 3.3 %copy-start.16 = (bf16[256,256]{1,0:T(8,128)(2,1)S(1)}, bf16[256,256]{1,0:T(8,128)(2,1)}, u32[]{:S(2)}) copy-start(bf16[256,256]{1,0:T(8,128)(2,1)} %param.22) | copy-start | bytes 393220
  32.5 0.8 copy-start.1
  35.0 6.0 %copy-start.10 = (bf16[1024,256]{1,0:T(8,128)(2,1)}, bf16[1024,256]{1,0:T(8,128)(2,1)S(1)}, u32[]{:S(2)}) copy-start(bf16[1024,256]{1,0:T(8,128)(2,1)S(1)} %get-tuple-element.37) | copy-start | bytes 1572868
  38.5 2.2 copy-start.11
  38.6 2.5 %copy-start.17 = (bf16[256,256]{1,0:T(8,128)(2,1)S(1)}, bf16[256,256]{1,0:T(8,128)(2,1)}, u32[]{:S(2)}) copy-start(bf16[256,256]{1,0:T(8,128)(2,1)} %param.24) | copy-start | bytes 393220
  40.7 0.8 copy-start.3
  41.0 0.7 copy-start.18
  41.0 0.7 copy-start.19
  41.5 1.1 copy-start.20
  42.6 0.8 copy-start.8
  58.8 1.0 copy-start.9
  58.8 1.2 copy-start.15
  58.8 1.5 copy-start.22
  60.3 1.4 copy-start.2
  60.3 2.4 %copy-start.6 = (bf16[1,1,1024,256]{3,2,1,0:T(8,128)(2,1)S(1)}, bf16[1,1,1024,256]{3,2,1,0:T(8,128)(2,1)}, u32[]{:S(2)}) copy-start(bf16[1,1,1024,256]{3,2,1,0:T(8,128)(2,1)} %param.13) | copy-start | bytes 1572868
  61.7 2.1 copy-start.4
  65.7 7.6 %copy-start.21 = (bf16[1024,256]{1,0:T(8,128)(2,1)S(1)}, bf16[1024,256]{1,0:T(8,128)(2,1)}, u32[]{:S(2)}) copy-start(bf16[1024,256]{1,0:T(8,128)(2,1)} %copy-done.20) | copy-start | bytes 1572868
  65.7 50.0 %all-to-all-start.2 = ((bf16[4,2,128,256]{3,2,1,0:T(8,128)(2,1)}), bf16[4,2,128,256]{3,2,1,0:T(8,128)(2,1)S(1)}, u32[]{:S(2)}, u32[]{:S(2)}) async-start(bf16[4,2,128,256]{3,2,1,0:T(8,128)(2,1)} %bitcast.113), calls=%async_computation.2 | async-start | bytes 1048576 | tf_op jit(solution)/shard_map/all_to_all | solution.py:128
  69.8 139.7 %all-reduce.4.cloned.1.call-start = ((), (), s32[]{:S(2)}) async-start(), calls=%async_computation.3 | async-start | bytes 2097152 | tf_op jit(solution)/shard_map/psum | solution.py:149
Sparse Core Ops, SparseCore 0:
  76.8 132.6 all-reduce.3
where the time goes:
time: 224 us; the launch traced here: 223 us
  waiting for transfers between devices  98.6 us (44%)
  blocking collectives  42.2 us (19%)
  local copies, waits for them, and re-layouts  26.9 us (12%)
  matrix products  18.7 us (8%)
  between operations  15 us (7%)
  starting transfers between devices  13.6 us (6%)
  other arithmetic  8.3 us (4%)
    psum x1, waiting for transfers between devices, shards(): lax.psum((grad_neigh_first, grad_self_first, grad_neigh_second, grad_self...  92 us
    psum x1, blocking collectives, shards(): lax.psum((grad_neigh_first, grad_self_first, grad_neigh_second, grad_self...  42.2 us
    unnamed x55, local copies, waits for them, and re-layouts  13.2 us
    scatter-add x1, other arithmetic, spread_back(): jax.ops.segment_sum(flattened, sources.reshape(-1), num_segments=table_size)  6.46 us
    all_to_all x1, waiting for transfers between devices, shards(): lax.all_to_all(outgoing(own_rows), 'grp', split_axis=0, concat_axis=0, ti...  6.16 us
    dot_general x6, matrix products, transpose_dot(): lax.dot_general(former, latter, (((0,), (0,)), ((), ())), preferred_eleme...  5.99 us
    reshape x1, local copies, waits for them, and re-layouts, spread_back(): flattened = contribution.reshape((-1,) + contribution.shape[2:])  5.67 us
    all_to_all x1, starting transfers between devices, shards(): lax.all_to_all(outgoing(own_rows), 'grp', split_axis=0, concat_axis=0, ti...  5.3 us
  transfers between devices with their start and end apart: 4, of which 3 were waited for; matrix products, arithmetic and copies ran while one was open for 6% of the time, Pallas kernels for 0%

commit v1 on v0

v1 whole, which is shorter than its diff:
```python
import functools

import jax
import jax.numpy as jnp
from jax import lax
from jax.experimental import pallas as pl
from jax.experimental.pallas import tpu as pltpu
from jax.sharding import PartitionSpec as P

BF16 = jnp.bfloat16
F32 = jnp.float32
VMEM = pl.BlockSpec(memory_space=pltpu.VMEM)
SMEM = pl.BlockSpec(memory_space=pltpu.SMEM)
ANY = pl.BlockSpec(memory_space=pl.ANY)
CORES = 2


def dot(former, latter):
    return jnp.dot(former, latter, preferred_element_type=F32)


def transpose_dot(former, latter):
    return lax.dot_general(former, latter, (((0,), (0,)), ((), ())), preferred_element_type=F32)


def dot_by_transpose(former, latter):
    return lax.dot_general(former, latter, (((1,), (1,)), ((), ())), preferred_element_type=F32)


def partner(index, step, count):
    if count & (count - 1) == 0:
        return index ^ step, index ^ step
    return (index + step) % count, (index + count - step) % count


def pack_kernel(peers, slots, blocks, send, feat, past, *refs):
    outs, sems = refs[:-1], refs[-1]
    g = lax.axis_index("grp")
    copies = []
    for step in range(1, peers):
        peer, _ = partner(g, step, peers)
        for s in range(slots):
            block = jnp.minimum(send[s, peer], blocks - 1)
            for which, values in enumerate((feat, past)):
                copies.append(
                    pltpu.make_async_copy(
                        values.at[block],
                        outs[which * (peers - 1) + step - 1].at[s],
                        sems.at[len(copies)],
                    )
                )
    for copy in copies:
        copy.start()
    for copy in copies:
        copy.wait()


def main_kernel(dims, sources, *refs):
    peers, slots, blocks, picks, rows, width, bins_count, devices, clus_count, pay_rows = dims
    inc = peers - 1
    (feat, tiles, aux, bins, flags, wn1, ws1, wn2, ws2, hw), refs = refs[:10], refs[10:]
    feat_in, past_in, refs = refs[:inc], refs[inc : 2 * inc], refs[2 * inc :]
    (hidden_out, grad_hidden_out, keep, send), refs = refs[:4], refs[4:]
    back_out, refs = refs[:inc], refs[inc:]
    (table1, table2, agg1, agg2, slope1, gps, gagg, gtab, gpf, pay, sems) = refs
    g = lax.axis_index("grp")
    core = lax.axis_index("clus") % CORES
    device = lax.axis_index("clus") * peers + g
    nodes = blocks * rows
    scale = 1.0 / (nodes * peers)
    copies = []
    for step in range(1, peers):
        _, origin = partner(g, step, peers)
        slot = pl.ds(blocks + origin * slots, slots)
        copies.append(pltpu.make_async_copy(feat_in[step - 1], table1.at[slot], sems.at[2 * step - 2]))
        copies.append(pltpu.make_async_copy(past_in[step - 1], table2.at[slot], sems.at[2 * step - 1]))
    for copy in copies:
        copy.start()
    table1[pl.ds(0, blocks)] = feat[...]
    for copy in copies:
        copy.wait()

    def gathered(table, b):
        return jnp.concatenate([table[sources[k, b]] for k in range(picks)], axis=0)

    def tile_row(b):
        return jnp.concatenate([tiles[b, k] for k in range(picks)], axis=1)

    pair = 2
    span = pair * rows

    def aggregate(table, result):
        @pl.loop(0, blocks)
        def _(b):
            result[b] = dot(tile_row(b), gathered(table, b)).astype(BF16)

    def two(ref, i):
        return ref[pl.ds(i * pair, pair)].reshape(span, width)

    aggregate(table1, agg1)

    @pl.loop(0, blocks // pair)
    def _(i):
        both = jnp.concatenate([two(agg1, i), two(table1, i)], axis=1)
        pre = dot(both, jnp.concatenate([wn1[...], ws1[...]], axis=0))
        gate = 0.5 * jnp.tanh(0.5 * pre) + 0.5
        value = pre * gate
        slope1[pl.ds(i * span, span)] = gate + value * (1.0 - gate)
        hidden = value.astype(BF16).reshape(pair, rows, width)
        table2[pl.ds(i * pair, pair)] = hidden
        hidden_out[pl.ds(i * pair, pair)] = hidden

    aggregate(table2, agg2)
    head = hw[...]
    step_col = lax.broadcasted_iota(jnp.int32, (bins_count, span), 0)

    def second(i, carry):
        loss, ghw = carry
        both = jnp.concatenate([two(agg2, i), two(table2, i)], axis=1)
        pre = dot(both, jnp.concatenate([wn2[...], ws2[...]], axis=0))
        gate = 0.5 * jnp.tanh(0.5 * pre) + 0.5
        value = pre * gate
        slope = gate + value * (1.0 - gate)
        hidden = value.astype(BF16)
        logits = dot_by_transpose(head, hidden)
        bin_row = bins[i]
        flag_row = flags[i].astype(F32)
        counted = step_col <= bin_row
        event = jnp.where(step_col == bin_row, flag_row, 0.0)
        tail = jnp.exp(-jnp.abs(logits))
        soft = jnp.maximum(logits, 0.0) + jnp.log1p(tail)
        loss = loss + jnp.where(counted, soft, 0.0) - event * logits
        chance = jnp.where(logits >= 0.0, 1.0, tail) / (1.0 + tail)
        glog = (jnp.where(counted, chance, 0.0) - event).astype(BF16)
        ghw = ghw + dot(glog, hidden)
        grad_pre = (transpose_dot(glog, head) * slope).astype(BF16)
        gps[pl.ds(i * span, span)] = grad_pre
        gagg[pl.ds(i * pair, pair)] = (
            dot_by_transpose(grad_pre, wn2[...]).astype(BF16).reshape(pair, rows, width)
        )
        own = dot_by_transpose(grad_pre, ws2[...]) + two(aux, i).astype(F32)
        gtab[pl.ds(i * pair, pair)] = own.reshape(pair, rows, width)
        return loss, ghw

    loss, ghw = lax.fori_loop(
        0,
        blocks // pair,
        second,
        (jnp.zeros((bins_count, span), F32), jnp.zeros((bins_count, width), F32)),
    )
    gtab[pl.ds(blocks, peers * slots)] = jnp.zeros((peers * slots, rows, width), F32)

    @pl.loop(0, blocks)
    def _(b):
        spread = transpose_dot(tile_row(b), gagg[b])
        for k in range(picks):
            gtab[sources[k, b]] += spread[k * rows : (k + 1) * rows]

    for step in range(1, peers):
        _, origin = partner(g, step, peers)
        for s in range(slots):
            back_out[step - 1][s] = gtab[blocks + origin * slots + s].astype(BF16)

    @pl.loop(0, blocks // pair)
    def _(i):
        total = gtab[pl.ds(i * pair, pair)]
        grad_hidden_out[pl.ds(i * pair, pair)] = total.astype(BF16)
        gpf[pl.ds(i * span, span)] = (
            total.reshape(span, width) * slope1[pl.ds(i * span, span)]
        ).astype(BF16)

    def weight_grads(at, left, right, grads):
        pay[pl.ds(at, width)] = (
            transpose_dot(left.reshape(nodes, width), grads[...]) * scale
        ).astype(BF16)
        pay[pl.ds(at + width, width)] = (
            transpose_dot(right.reshape(nodes, width), grads[...]) * scale
        ).astype(BF16)

    weight_grads(0, agg1[...], table1[pl.ds(0, blocks)], gpf)
    weight_grads(2 * width, agg2[...], table2[pl.ds(0, blocks)], gps)
    part = jnp.sum(loss) * scale
    high = part.astype(BF16).astype(F32)
    tail_rows = pay_rows - 4 * width - bins_count
    lane = lax.broadcasted_iota(jnp.int32, (tail_rows, width), 0) * width + lax.broadcasted_iota(
        jnp.int32, (tail_rows, width), 1
    )
    loss_rows = jnp.where(lane == 2 * device, high, 0.0) + jnp.where(
        lane == 2 * device + 1, part - high, 0.0
    )
    pay[pl.ds(4 * width, bins_count)] = (ghw * scale).astype(BF16)
    pay[pl.ds(4 * width + bins_count, tail_rows)] = loss_rows.astype(BF16)
    half = pay_rows // CORES
    keep[...] = pay[pl.ds(pl.multiple_of(core * half, 16), half)]
    send[...] = pay[pl.ds(pl.multiple_of((1 - core) * half, 16), half)]


def split_kernel(peers, kept, came, own, *outs):
    g = lax.axis_index("grp")

    def chunk(p):
        return (kept[p].astype(F32) + came[p].astype(F32)).astype(BF16)

    own[...] = chunk(g)
    for step in range(1, peers):
        peer, _ = partner(g, step, peers)
        outs[step - 1][...] = chunk(peer)


def add_kernel(*refs):
    total = refs[0][...].astype(F32)
    for ref in refs[1:-1]:
        total = total + ref[...].astype(F32)
    refs[-1][...] = total.astype(BF16)


def join_kernel(peers, own, *refs):
    out = refs[-1]
    g = lax.axis_index("grp")
    out[g] = own[...]
    for step in range(1, peers):
        _, origin = partner(g, step, peers)
        out[origin] = refs[step - 1][...]


def finish_kernel(dims, mine, other, *outs):
    width, bins_count, devices, pay_rows = dims
    pay = outs[-1]
    half = pay_rows // CORES
    core = lax.axis_index("clus") % CORES
    pay[pl.ds(pl.multiple_of(core * half, 16), half)] = mine[...]
    pay[pl.ds(pl.multiple_of((1 - core) * half, 16), half)] = other[...]
    for i in range(4):
        outs[i][...] = pay[pl.ds(i * width, width)].astype(F32)
    outs[4][...] = pay[pl.ds(4 * width, bins_count)].astype(F32)
    loss_rows = pay[pl.ds(4 * width + bins_count, pay_rows - 4 * width - bins_count)].astype(F32)
    outs[5][0, 0] = jnp.sum(loss_rows)


def add_aux_kernel(peers, slots, blocks, terms, send, *refs):
    add_kernel(*refs[:terms], refs[-3])
    back, out, total = refs[terms:-3], refs[-2], refs[-1]
    g = lax.axis_index("grp")
    total[...] = jnp.zeros_like(total)
    for step in range(1, peers):
        peer, _ = partner(g, step, peers)
        for s in range(slots):
            total[send[s, peer]] += back[step - 1][s].astype(F32)
    out[...] = total[pl.ds(0, blocks)].astype(BF16)


def shards(
    clus_count,
    peers,
    features,
    history,
    aux_history,
    tile_values,
    tile_sources,
    send_list,
    event_bins,
    event_flags,
    neigh_first,
    self_first,
    neigh_second,
    self_second,
    hazard_weight,
):
    blocks, picks, rows = tile_values.shape[2:5]
    width = features.shape[3]
    slots = send_list.shape[3]
    bins_count = hazard_weight.shape[1]
    devices = clus_count * peers
    chips_z = clus_count // CORES
    inc = peers - 1
    used = 4 * width + bins_count + -(-2 * devices // width)
    pay_rows = -(-used // (16 * CORES * peers)) * 16 * CORES * peers
    half = pay_rows // CORES
    chunk = half // peers
    block_shape = (blocks, rows, width)
    slot_shape = (slots, rows, width)
    routing = send_list[0, 0].T
    feat = features.reshape(block_shape)
    past = history.reshape(block_shape)
    params = pltpu.CompilerParams(vmem_limit_bytes=20 << 20)
    small = pltpu.CompilerParams(vmem_limit_bytes=4 << 20)

    def shape(dims, dtype=BF16):
        return jax.ShapeDtypeStruct(dims, dtype)

    def grp_pairs(step):
        return [(i, partner(i, step, peers)[0]) for i in range(peers)]

    def over_grp(value, step):
        return lax.ppermute(value, "grp", grp_pairs(step))

    def over_z(value, step):
        pairs = [
            (z * CORES + c, partner(z, step, chips_z)[0] * CORES + c)
            for z in range(chips_z)
            for c in range(CORES)
        ]
        return lax.ppermute(value, "clus", pairs)

    def over_core(value):
        return lax.ppermute(value, "clus", [(i, i ^ 1) for i in range(clus_count)])

    packed = pl.pallas_call(
        functools.partial(pack_kernel, peers, slots, blocks),
        out_shape=[shape(slot_shape)] * (2 * inc),
        in_specs=[SMEM, ANY, ANY],
        out_specs=[VMEM] * (2 * inc),
        scratch_shapes=[pltpu.SemaphoreType.DMA((2 * inc * slots,))],
        compiler_params=small,
        name="pack",
    )(routing, feat, past)
    feat_in = [over_grp(packed[i], i + 1) for i in range(inc)]
    past_in = [over_grp(packed[inc + i], i + 1) for i in range(inc)]

    pair_shape = (blocks // 2, 1, 2 * rows)
    dims = (peers, slots, blocks, picks, rows, width, bins_count, devices, clus_count, pay_rows)
    nodes = blocks * rows
    table = blocks + peers * slots
    outs = pl.pallas_call(
        functools.partial(main_kernel, dims),
        out_shape=[shape(block_shape), shape(block_shape), shape((half, width)), shape((half, width))]
        + [shape(slot_shape)] * inc,
        in_specs=[SMEM] + [VMEM] * 10 + [ANY] * (2 * inc),
        out_specs=[VMEM] * (4 + inc),
        scratch_shapes=[
            pltpu.VMEM((table, rows, width), BF16),
            pltpu.VMEM((table, rows, width), BF16),
            pltpu.VMEM(block_shape, BF16),
            pltpu.VMEM(block_shape, BF16),
            pltpu.VMEM((nodes, width), F32),
            pltpu.VMEM((nodes, width), BF16),
            pltpu.VMEM(block_shape, BF16),
            pltpu.VMEM((table, rows, width), F32),
            pltpu.VMEM((nodes, width), BF16),
            pltpu.VMEM((pay_rows, width), BF16),
            pltpu.SemaphoreType.DMA((2 * inc,)),
        ],
        compiler_params=params,
        name="network",
    )(
        tile_sources[0, 0].T,
        feat,
        tile_values[0, 0],
        aux_history.reshape(block_shape),
        event_bins.reshape(pair_shape),
        event_flags.reshape(pair_shape),
        neigh_first,
        self_first,
        neigh_second,
        self_second,
        hazard_weight.T,
        *feat_in,
        *past_in,
    )
    hidden_first, grad_hidden, kept, sent = outs[:4]
    back = outs[4:]

    came = over_core(sent)
    parts = pl.pallas_call(
        functools.partial(split_kernel, peers),
        out_shape=[shape((chunk, width))] * peers,
        in_specs=[VMEM, VMEM],
        out_specs=[VMEM] * peers,
        compiler_params=small,
        name="split",
    )(kept.reshape(peers, chunk, width), came.reshape(peers, chunk, width))
    from_grp = [over_grp(parts[i], i) for i in range(1, peers)]
    came_back = [over_grp(back[i], i + 1) for i in range(inc)]

    def add(*values):
        return pl.pallas_call(
            add_kernel,
            out_shape=shape((chunk, width)),
            in_specs=[VMEM] * len(values),
            out_specs=VMEM,
            compiler_params=small,
            name="add",
        )(*values)

    mine = add(parts[0], *from_grp)
    terms = [mine] + [over_z(mine, i) for i in range(1, chips_z)]
    mine, new_aux = pl.pallas_call(
        functools.partial(add_aux_kernel, peers, slots, blocks, len(terms)),
        out_shape=[shape((chunk, width)), shape(block_shape)],
        in_specs=[SMEM] + [VMEM] * (len(terms) + inc),
        out_specs=[VMEM] * 2,
        scratch_shapes=[pltpu.VMEM((blocks + 1, rows, width), F32)],
        compiler_params=small,
        name="add_aux",
    )(routing, *terms, *came_back)
    others = [over_grp(mine, i) for i in range(1, peers)]
    joined = pl.pallas_call(
        functools.partial(join_kernel, peers),
        out_shape=shape((peers, chunk, width)),
        in_specs=[VMEM] * peers,
        out_specs=VMEM,
        compiler_params=small,
        name="join",
    )(mine, *others).reshape(half, width)
    other_half = over_core(joined)
    square = shape((width, width), F32)
    grads = pl.pallas_call(
        functools.partial(finish_kernel, (width, bins_count, devices, pay_rows)),
        out_shape=[square] * 4 + [shape((bins_count, width), F32), shape((1, 1), F32)],
        in_specs=[VMEM, VMEM],
        out_specs=[VMEM] * 5 + [SMEM],
        scratch_shapes=[pltpu.VMEM((pay_rows, width), BF16)],
        compiler_params=small,
        name="finish",
    )(joined, other_half)
    return (
        hidden_first.reshape(features.shape),
        grad_hidden.reshape(features.shape),
        new_aux.reshape(features.shape),
        *grads[:4],
        grads[4].T,
        grads[5][0, 0],
    )


def solution(mesh):
    split = P("clus", "grp")
    whole = P()
    return jax.shard_map(
        functools.partial(shards, mesh.shape["clus"], mesh.shape["grp"]),
        mesh=mesh,
        in_specs=(split,) * 8 + (whole,) * 5,
        out_specs=(split,) * 3 + (whole,) * 6,
        check_vma=False,
    )
```

time: 224 us -> 73.7 us (0.33)
  waiting for transfers between devices: 98.6 us -> 20.3 us
  blocking collectives: 42.2 us -> 0 us
  matrix products: 18.7 us -> 0 us
  local copies, waits for them, and re-layouts: 26.9 us -> 8.96 us
  Pallas kernels: 0 us -> 17.8 us
  between operations: 15 us -> 0.75 us
  starting transfers between devices: 13.6 us -> 25.5 us
  other arithmetic: 8.3 us -> 0 us
    psum x1 -> x0, waiting for transfers between devices: 92 us -> none  [shards(): lax.psum((grad_neigh_first, grad_self_first, grad_neigh_second, grad_self...]
    psum x1 -> x0, blocking collectives: 42.2 us -> none  [shards(): lax.psum((grad_neigh_first, grad_self_first, grad_neigh_second, grad_self...]
    ppermute x0 -> x20, starting transfers between devices: none -> 25.5 us  [the longest x15 20.9 us: over_grp(): return lax.ppermute(value, 'grp', grp_pairs(step))]
    ppermute x0 -> x20, waiting for transfers between devices: none -> 20.3 us  [the longest x15 12.7 us: over_grp(): return lax.ppermute(value, 'grp', grp_pairs(step))]
    dot_general x19 -> x0, matrix products: 18.7 us -> none  [the longest x6 5.99 us: transpose_dot(): lax.dot_general(former, latter, (((0,), (0,)), ((), ())), preferred_eleme...]
    pallas_call x0 -> x7, Pallas kernels: none -> 17.8 us  [the longest x1 13.3 us: shards(): pl.pallas_call(functools.partial(main_kernel, dims), out_shape=[shape(blo...]
    all_to_all x3 -> x0, starting transfers between devices: 13.6 us -> none  [the longest x1 5.3 us: shards(): lax.all_to_all(outgoing(own_rows), 'grp', split_axis=0, concat_axis=0, ti...]
    all_to_all x3 -> x0, waiting for transfers between devices: 6.53 us -> none  [the longest x1 6.16 us: shards(): lax.all_to_all(outgoing(own_rows), 'grp', split_axis=0, concat_axis=0, ti...]
  transfers between devices with their start and end apart: 4 -> 20, of which waited for: 3 -> 11; matrix products, arithmetic and copies ran while one was open for 6% -> 0% of each run, Pallas kernels for 0% -> 0%
where the time goes in v1:
time: 73.7 us; the launch traced here: 73.3 us
  starting transfers between devices  25.5 us (35%)
  waiting for transfers between devices  20.3 us (28%)
  Pallas kernels  17.8 us (24%)
  local copies, waits for them, and re-layouts  8.96 us (12%)
  between operations  0.75 us (1%)
    ppermute x15, starting transfers between devices, over_grp(): return lax.ppermute(value, 'grp', grp_pairs(step))  20.9 us
    pallas_call x1, Pallas kernels, shards(): pl.pallas_call(functools.partial(main_kernel, dims), out_shape=[shape(blo...  13.3 us
    ppermute x15, waiting for transfers between devices, over_grp(): return lax.ppermute(value, 'grp', grp_pairs(step))  12.7 us
    unnamed x28, local copies, waits for them, and re-layouts  8.96 us
    ppermute x3, waiting for transfers between devices, over_z(): return lax.ppermute(value, 'clus', pairs)  4.46 us
    ppermute x3, starting transfers between devices, over_z(): return lax.ppermute(value, 'clus', pairs)  4.45 us
    ppermute x2, waiting for transfers between devices, over_core(): return lax.ppermute(value, 'clus', [(i, i ^ 1) for i in range(clus_count)])  3.14 us
    pallas_call x1, Pallas kernels, shards(): pl.pallas_call(functools.partial(pack_kernel, peers, slots, blocks), out_...  1.71 us
  transfers between devices with their start and end apart: 20, of which 11 were waited for; matrix products, arithmetic and copies ran while one was open for 0% of the time, Pallas kernels for 0%

profile of v1, /device:TPU:0, one launch (start us, length us, event | category | flops | bytes accessed | tf_op | source)
XLA Modules:
  0.0 73.3 jit_solution(1602532883718515672)
XLA Ops:
  0.6 0.0 copy-start.12
  0.7 0.7 copy-done.12
  1.3 0.0 copy-start
  1.3 1.0 %copy-done = bf16[1,1,1024,256]{3,2,1,0:T(8,128)(2,1)S(1)} copy-done((bf16[1,1,1024,256]{3,2,1,0:T(8,128)(2,1)S(1)}, bf16[1,1,1024,256]{3,2,1,0:T(8,128)(2,1)}, u32[]{:S(2)}) %copy-start) | copy-done | bytes 524312
  2.4 0.0 copy-start.3
  2.4 1.0 %copy-done.3 = bf16[1,1,1024,256]{3,2,1,0:T(8,128)(2,1)S(1)} copy-done((bf16[1,1,1024,256]{3,2,1,0:T(8,128)(2,1)S(1)}, bf16[1,1,1024,256]{3,2,1,0:T(8,128)(2,1)}, u32[]{:S(2)}) %copy-start.3) | copy-done | bytes 524312
  3.4 0.0 copy-start.1
  3.4 1.7 %pack.1 = (bf16[2,128,256]{2,1,0:T(8,128)(2,1)S(1)}, bf16[2,128,256]{2,1,0:T(8,128)(2,1)S(1)}, bf16[2,128,256]{2,1,0:T(8,128)(2,1)S(1)}, bf16[2,128,256]{2,1,0:T...) custom-call(s32[2,4]{1,0:T(2,128)S(1)} %bitcast.33, ...), custom_call_target="tpu_custom_call" | custom-call | tf_op jit(solution)/shard_map/pack/pallas_call | solution.py:308
  5.1 0.0 copy-start.9
  5.1 3.0 %collective-permute-start = (bf16[2,128,256]{2,1,0:T(8,128)(2,1)S(1)}, bf16[2,128,256]{2,1,0:T(8,128)(2,1)S(1)}, u32[]{:S(2)}, u32[]{:S(2)}) collective-permute-start(bf16[2,128,256]{2,1,0:T(8,128)(2,1)S(1)} %get-tuple-element.34), channel_id=1, source_target_pairs={{0,1},{1,0},{2,3},{3,2},{4,5},{5,4},{6,7},{7,6},{8,9},{9,8},{10,11... | collective-permute-start | bytes 393224 | tf_op jit(solution)/shard_map/ppermute | solution.py:295
  8.1 1.5 %collective-permute-start.1 = (bf16[2,128,256]{2,1,0:T(8,128)(2,1)S(1)}, bf16[2,128,256]{2,1,0:T(8,128)(2,1)S(1)}, u32[]{:S(2)}, u32[]{:S(2)}) collective-permute-start(bf16[2,128,256]{2,1,0:T(8,128)(2,1)S(1)} %get-tuple-element.35), channel_id=1, source_target_pairs={{0,2},{1,3},{2,0},{3,1},{4,6},{5,7},{6,4},{7,5},{8,10},{9,11},{10,... | collective-permute-start | bytes 393224 | tf_op jit(solution)/shard_map/ppermute | solution.py:295
  9.7 0.0 collective-permute-start.2
  9.7 1.9 %collective-permute-start.3 = (bf16[2,128,256]{2,1,0:T(8,128)(2,1)S(1)}, bf16[2,128,256]{2,1,0:T(8,128)(2,1)S(1)}, u32[]{:S(2)}, u32[]{:S(2)}) collective-permute-start(bf16[2,128,256]{2,1,0:T(8,128)(2,1)S(1)} %get-tuple-element.37), channel_id=1, source_target_pairs={{0,1},{1,0},{2,3},{3,2},{4,5},{5,4},{6,7},{7,6},{8,9},{9,8},{10,11... | collective-permute-start | bytes 393224 | tf_op jit(solution)/shard_map/ppermute | solution.py:295
  11.6 1.5 %collective-permute-start.4 = (bf16[2,128,256]{2,1,0:T(8,128)(2,1)S(1)}, bf16[2,128,256]{2,1,0:T(8,128)(2,1)S(1)}, u32[]{:S(2)}, u32[]{:S(2)}) collective-permute-start(bf16[2,128,256]{2,1,0:T(8,128)(2,1)S(1)} %get-tuple-element.38), channel_id=1, source_target_pairs={{0,2},{1,3},{2,0},{3,1},{4,6},{5,7},{6,4},{7,5},{8,10},{9,11},{10,... | collective-permute-start | bytes 393224 | tf_op jit(solution)/shard_map/ppermute | solution.py:295
  13.2 0.0 collective-permute-done.refs_10_
  13.2 2.3 %collective-permute-start.5 = (bf16[2,128,256]{2,1,0:T(8,128)(2,1)S(1)}, bf16[2,128,256]{2,1,0:T(8,128)(2,1)S(1)}, u32[]{:S(2)}, u32[]{:S(2)}) collective-permute-start(bf16[2,128,256]{2,1,0:T(8,128)(2,1)S(1)} %get-tuple-element.39), channel_id=1, source_target_pairs={{0,3},{1,2},{2,1},{3,0},{4,7},{5,6},{6,5},{7,4},{8,11},{9,10},{10,... | collective-permute-start | bytes 393224 | tf_op jit(solution)/shard_map/ppermute | solution.py:295
  15.5 1.9 %collective-permute-done.1.refs_11_ = bf16[2,128,256]{2,1,0:T(8,128)(2,1)S(1)} collective-permute-done((bf16[2,128,256]{2,1,0:T(8,128)(2,1)S(1)}, bf16[2,128,256]{2,1,0:T(8,128)(2,1)S(1)}, u32[]{:S(2)}, u32[]{:S(2)}) %collective-permute-start.1) | collective-permute-done | bytes 131104 | tf_op jit(solution)/shard_map/ppermute | solution.py:295
  17.4 0.0 collective-permute-done.2.refs_12_
  17.4 1.3 %collective-permute-done.3.refs_13_ = bf16[2,128,256]{2,1,0:T(8,128)(2,1)S(1)} collective-permute-done((bf16[2,128,256]{2,1,0:T(8,128)(2,1)S(1)}, bf16[2,128,256]{2,1,0:T(8,128)(2,1)S(1)}, u32[]{:S(2)}, u32[]{:S(2)}) %collective-permute-start.3) | collective-permute-done | bytes 131104 | tf_op jit(solution)/shard_map/ppermute | solution.py:295
  18.7 2.8 %collective-permute-done.4.refs_14_ = bf16[2,128,256]{2,1,0:T(8,128)(2,1)S(1)} collective-permute-done((bf16[2,128,256]{2,1,0:T(8,128)(2,1)S(1)}, bf16[2,128,256]{2,1,0:T(8,128)(2,1)S(1)}, u32[]{:S(2)}, u32[]{:S(2)}) %collective-permute-start.4) | collective-permute-done | bytes 131104 | tf_op jit(solution)/shard_map/ppermute | solution.py:295
  21.5 0.0 collective-permute-done.5.refs_15_
  21.5 0.0 copy-done.1
  21.6 0.0 copy-done.4
  21.6 0.0 copy-done.9
  21.6 0.7 copy-done.10
  22.2 0.0 copy-done.13
  22.2 1.2 %copy-done.2 = bf16[1,1,8,4,128,128]{5,4,3,2,1,0:T(8,128)(2,1)S(1)} copy-done((bf16[1,1,8,4,128,128]{5,4,3,2,1,0:T(8,128)(2,1)S(1)}, bf16[1,1,8,4,128,128]{5,4,3,2,1,0:T(8,128)(2,1)}, u32[]{:S(2)}) %copy-start.2) | copy-done | bytes 1048600
  23.5 0.9 %copy-done.5 = bf16[256,256]{1,0:T(8,128)(2,1)S(1)} copy-done((bf16[256,256]{1,0:T(8,128)(2,1)S(1)}, bf16[256,256]{1,0:T(8,128)(2,1)}, u32[]{:S(2)}) %copy-start.5) | copy-done | bytes 131096
  24.4 0.9 %copy-done.6 = bf16[256,256]{1,0:T(8,128)(2,1)S(1)} copy-done((bf16[256,256]{1,0:T(8,128)(2,1)S(1)}, bf16[256,256]{1,0:T(8,128)(2,1)}, u32[]{:S(2)}) %copy-start.6) | copy-done | bytes 131096
  25.3 0.9 %copy-done.7 = bf16[256,256]{1,0:T(8,128)(2,1)S(1)} copy-done((bf16[256,256]{1,0:T(8,128)(2,1)S(1)}, bf16[256,256]{1,0:T(8,128)(2,1)}, u32[]{:S(2)}) %copy-start.7) | copy-done | bytes 131096
  26.2 0.9 %copy-done.8 = bf16[256,256]{1,0:T(8,128)(2,1)S(1)} copy-done((bf16[256,256]{1,0:T(8,128)(2,1)S(1)}, bf16[256,256]{1,0:T(8,128)(2,1)}, u32[]{:S(2)}) %copy-start.8) | copy-done | bytes 131096
  27.1 0.7 copy-done.11
  27.8 13.3 %network.1 = (bf16[8,128,256]{2,1,0:T(8,128)(2,1)}, bf16[8,128,256]{2,1,0:T(8,128)(2,1)}, bf16[576,256]{1,0:T(8,128)(2,1)S(1)}, bf16[576,256]{1,0:T(8,128)(2,1)S...) custom-call(s32[4,8]{1,0:T(4,128)S(1)} %bitcast.35, ...), custom_call_target="tpu_custom_call" | custom-call | tf_op jit(solution)/shard_map/network/pallas_call | solution.py:324
  41.1 0.1 collective-permute-start.6
  41.2 1.6 %collective-permute-done.6 = bf16[576,256]{1,0:T(8,128)(2,1)S(1)} collective-permute-done((bf16[576,256]{1,0:T(8,128)(2,1)S(1)}, bf16[576,256]{1,0:T(8,128)(2,1)S(1)}, u32[]{:S(2)}, u32[]{:S(2)}) %collective-permute-start.6) | collective-permute-done | bytes 294944 | tf_op jit(solution)/shard_map/ppermute | solution.py:306
  42.8 0.1 split.1
  42.9 1.3 %collective-permute-start.7 = (bf16[144,256]{1,0:T(8,128)(2,1)S(1)}, bf16[144,256]{1,0:T(8,128)(2,1)S(1)}, u32[]{:S(2)}, u32[]{:S(2)}) collective-permute-start(bf16[144,256]{1,0:T(8,128)(2,1)S(1)} %get-tuple-element.45), channel_id=1, source_target_pairs={{0,1},{1,0},{2,3},{3,2},{4,5},{5,4},{6,7},{7,6},{8,9},{9,8},{10,11... | collective-permute-start | bytes 221192 | tf_op jit(solution)/shard_map/ppermute | solution.py:295
  44.1 0.8 %collective-permute-start.13 = (bf16[2,128,256]{2,1,0:T(8,128)(2,1)S(1)}, bf16[2,128,256]{2,1,0:T(8,128)(2,1)S(1)}, u32[]{:S(2)}, u32[]{:S(2)}) collective-permute-start(bf16[2,128,256]{2,1,0:T(8,128)(2,1)S(1)} %get-tuple-element.48), channel_id=1, source_target_pairs={{0,1},{1,0},{2,3},{3,2},{4,5},{5,4},{6,7},{7,6},{8,9},{9,8},{10,11... | collective-permute-start | bytes 393224 | tf_op jit(solution)/shard_map/ppermute | solution.py:295
  44.9 1.5 %collective-permute-start.8 = (bf16[144,256]{1,0:T(8,128)(2,1)S(1)}, bf16[144,256]{1,0:T(8,128)(2,1)S(1)}, u32[]{:S(2)}, u32[]{:S(2)}) collective-permute-start(bf16[144,256]{1,0:T(8,128)(2,1)S(1)} %get-tuple-element.46), channel_id=1, source_target_pairs={{0,2},{1,3},{2,0},{3,1},{4,6},{5,7},{6,4},{7,5},{8,10},{9,11},{10,... | collective-permute-start | bytes 221192 | tf_op jit(solution)/shard_map/ppermute | solution.py:295
  46.5 1.1 %collective-permute-start.9 = (bf16[144,256]{1,0:T(8,128)(2,1)S(1)}, bf16[144,256]{1,0:T(8,128)(2,1)S(1)}, u32[]{:S(2)}, u32[]{:S(2)}) collective-permute-start(bf16[144,256]{1,0:T(8,128)(2,1)S(1)} %get-tuple-element.47), channel_id=1, source_target_pairs={{0,3},{1,2},{2,1},{3,0},{4,7},{5,6},{6,5},{7,4},{8,11},{9,10},{10,... | collective-permute-start | bytes 221192 | tf_op jit(solution)/shard_map/ppermute | solution.py:295
  47.6 0.8 %collective-permute-start.14 = (bf16[2,128,256]{2,1,0:T(8,128)(2,1)S(1)}, bf16[2,128,256]{2,1,0:T(8,128)(2,1)S(1)}, u32[]{:S(2)}, u32[]{:S(2)}) collective-permute-start(bf16[2,128,256]{2,1,0:T(8,128)(2,1)S(1)} %get-tuple-element.49), channel_id=1, source_target_pairs={{0,2},{1,3},{2,0},{3,1},{4,6},{5,7},{6,4},{7,5},{8,10},{9,11},{10,... | collective-permute-start | bytes 393224 | tf_op jit(solution)/shard_map/ppermute | solution.py:295
  48.4 0.0 collective-permute-done.7.refs_1_
  48.5 1.4 %collective-permute-start.15 = (bf16[2,128,256]{2,1,0:T(8,128)(2,1)S(1)}, bf16[2,128,256]{2,1,0:T(8,128)(2,1)S(1)}, u32[]{:S(2)}, u32[]{:S(2)}) collective-permute-start(bf16[2,128,256]{2,1,0:T(8,128)(2,1)S(1)} %get-tuple-element.50), channel_id=1, source_target_pairs={{0,3},{1,2},{2,1},{3,0},{4,7},{5,6},{6,5},{7,4},{8,11},{9,10},{10,... | collective-permute-start | bytes 393224 | tf_op jit(solution)/shard_map/ppermute | solution.py:295
  49.9 0.0 collective-permute-done.8.refs_2_
  49.9 3.6 %collective-permute-done.9.refs_3_ = bf16[144,256]{1,0:T(8,128)(2,1)S(1)} collective-permute-done((bf16[144,256]{1,0:T(8,128)(2,1)S(1)}, bf16[144,256]{1,0:T(8,128)(2,1)S(1)}, u32[]{:S(2)}, u32[]{:S(2)}) %collective-permute-start.9) | collective-permute-done | bytes 73760 | tf_op jit(solution)/shard_map/ppermute | solution.py:295
  53.5 3.7 %collective-permute-start.12 = (bf16[144,256]{1,0:T(8,128)(2,1)S(1)}, bf16[144,256]{1,0:T(8,128)(2,1)S(1)}, u32[]{:S(2)}, u32[]{:S(2)}) collective-permute-start(bf16[144,256]{1,0:T(8,128)(2,1)S(1)} %add.1.refs_0_), channel_id=1, source_target_pairs={{0,24},{4,28},{8,16},{12,20},{16,8},{20,12},{24,0},{28,4},{1,25},{... | collective-permute-start | bytes 221192 | tf_op jit(solution)/shard_map/ppermute | solution.py:303
  57.2 0.0 collective-permute-start.11
  57.2 0.0 collective-permute-done.13.refs_4_
  57.2 0.8 %collective-permute-start.10 = (bf16[144,256]{1,0:T(8,128)(2,1)S(1)}, bf16[144,256]{1,0:T(8,128)(2,1)S(1)}, u32[]{:S(2)}, u32[]{:S(2)}) collective-permute-start(bf16[144,256]{1,0:T(8,128)(2,1)S(1)} %add.1.refs_0_), channel_id=1, source_target_pairs={{0,8},{4,12},{8,0},{12,4},{16,24},{20,28},{24,16},{28,20},{1,9},{5... | collective-permute-start | bytes 221192 | tf_op jit(solution)/shard_map/ppermute | solution.py:303
  58.0 0.0 collective-permute-done.14.refs_5_
  58.0 0.0 collective-permute-done.15.refs_6_
  58.0 1.9 %collective-permute-done.12.refs_3_ = bf16[144,256]{1,0:T(8,128)(2,1)S(1)} collective-permute-done((bf16[144,256]{1,0:T(8,128)(2,1)S(1)}, bf16[144,256]{1,0:T(8,128)(2,1)S(1)}, u32[]{:S(2)}, u32[]{:S(2)}) %collective-permute-start.12) | collective-permute-done | bytes 73760 | tf_op jit(solution)/shard_map/ppermute | solution.py:303
  59.9 2.6 %collective-permute-done.11.refs_2_ = bf16[144,256]{1,0:T(8,128)(2,1)S(1)} collective-permute-done((bf16[144,256]{1,0:T(8,128)(2,1)S(1)}, bf16[144,256]{1,0:T(8,128)(2,1)S(1)}, u32[]{:S(2)}, u32[]{:S(2)}) %collective-permute-start.11) | collective-permute-done | bytes 73760 | tf_op jit(solution)/shard_map/ppermute | solution.py:303
  62.5 0.0 collective-permute-done.10.refs_1_
  62.5 1.6 %add_aux.1 = (bf16[144,256]{1,0:T(8,128)(2,1)S(1)}, bf16[8,128,256]{2,1,0:T(8,128)(2,1)}) custom-call(s32[2,4]{1,0:T(2,128)S(1)} %bitcast.34, bf16[144,256]{1,0:T(8,128)(2,1)S(1)} %add.1.refs_0_, bf16[144,256]{1,0:T(8,128)(2,1)S(1)} %collective-permute-done.10.refs_1_, bf16[144,256]{1,0:T(8,128)(2,1)S(1)} %collective-permute-done.11.refs_2_, ...), custom_call_target="tpu_custom_call" | custom-call | tf_op jit(solution)/shard_map/add_aux/pallas_call | solution.py:387
  64.0 1.2 %collective-permute-start.18 = (bf16[144,256]{1,0:T(8,128)(2,1)S(1)}, bf16[144,256]{1,0:T(8,128)(2,1)S(1)}, u32[]{:S(2)}, u32[]{:S(2)}) collective-permute-start(bf16[144,256]{1,0:T(8,128)(2,1)S(1)} %get-tuple-element.52.own), channel_id=1, source_target_pairs={{0,3},{1,2},{2,1},{3,0},{4,7},{5,6},{6,5},{7,4},{8,11},{9,10},{10,... | collective-permute-start | bytes 221192 | tf_op jit(solution)/shard_map/ppermute | solution.py:295
  65.2 1.0 %collective-permute-start.17 = (bf16[144,256]{1,0:T(8,128)(2,1)S(1)}, bf16[144,256]{1,0:T(8,128)(2,1)S(1)}, u32[]{:S(2)}, u32[]{:S(2)}) collective-permute-start(bf16[144,256]{1,0:T(8,128)(2,1)S(1)} %get-tuple-element.52.own), channel_id=1, source_target_pairs={{0,2},{1,3},{2,0},{3,1},{4,6},{5,7},{6,4},{7,5},{8,10},{9,11},{10,... | collective-permute-start | bytes 221192 | tf_op jit(solution)/shard_map/ppermute | solution.py:295
  66.2 1.3 %collective-permute-start.16 = (bf16[144,256]{1,0:T(8,128)(2,1)S(1)}, bf16[144,256]{1,0:T(8,128)(2,1)S(1)}, u32[]{:S(2)}, u32[]{:S(2)}) collective-permute-start(bf16[144,256]{1,0:T(8,128)(2,1)S(1)} %get-tuple-element.52.own), channel_id=1, source_target_pairs={{0,1},{1,0},{2,3},{3,2},{4,5},{5,4},{6,7},{7,6},{8,9},{9,8},{10,11... | collective-permute-start | bytes 221192 | tf_op jit(solution)/shard_map/ppermute | solution.py:295
  67.5 1.8 %collective-permute-done.18.refs_2_ = bf16[144,256]{1,0:T(8,128)(2,1)S(1)} collective-permute-done((bf16[144,256]{1,0:T(8,128)(2,1)S(1)}, bf16[144,256]{1,0:T(8,128)(2,1)S(1)}, u32[]{:S(2)}, u32[]{:S(2)}) %collective-permute-start.18) | collective-permute-done | bytes 73760 | tf_op jit(solution)/shard_map/ppermute | solution.py:295
  69.3 0.7 %collective-permute-done.17.refs_1_ = bf16[144,256]{1,0:T(8,128)(2,1)S(1)} collective-permute-done((bf16[144,256]{1,0:T(8,128)(2,1)S(1)}, bf16[144,256]{1,0:T(8,128)(2,1)S(1)}, u32[]{:S(2)}, u32[]{:S(2)}) %collective-permute-start.17) | collective-permute-done | bytes 73760 | tf_op jit(solution)/shard_map/ppermute | solution.py:295
  70.1 0.5 collective-permute-done.16.refs_0_
  70.6 0.1 collective-permute-start.19
  70.7 1.6 %collective-permute-done.19.other = bf16[576,256]{1,0:T(8,128)(2,1)S(1)} collective-permute-done((bf16[576,256]{1,0:T(8,128)(2,1)S(1)}, bf16[576,256]{1,0:T(8,128)(2,1)S(1)}, u32[]{:S(2)}, u32[]{:S(2)}) %collective-permute-start.19) | collective-permute-done | bytes 294944 | tf_op jit(solution)/shard_map/ppermute | solution.py:306
  72.2 1.0 %finish.1 = (f32[256,256]{1,0:T(8,128)}, f32[256,256]{1,0:T(8,128)}, f32[256,256]{1,0:T(8,128)}, f32[256,256]{1,0:T(8,128)}, f32[32,256]{1,0:T(8,128)}, /*index=5*/f32[1,1]{1,0:T(1,128)}) custom-call(bf16[576,256]{1,0:T(8,128)(2,1)S(1)} %bitcast.24, bf16[576,256]{1,0:T(8,128)(2,1)S(1)} %collective-permute-done.19.other), custom_call_target="tpu_custom_call" | custom-call | tf_op jit(solution)/shard_map/finish/pallas_call | solution.py:407
  (11 shorter events, 0.1 us)
Async XLA Ops:
  0.6 0.7 copy-start.12
  1.3 1.0 %copy-start = (bf16[1,1,1024,256]{3,2,1,0:T(8,128)(2,1)S(1)}, bf16[1,1,1024,256]{3,2,1,0:T(8,128)(2,1)}, u32[]{:S(2)}) copy-start(bf16[1,1,1024,256]{3,2,1,0:T(8,128)(2,1)} %param.13) | copy-start | bytes 1572868
  2.4 1.0 %copy-start.3 = (bf16[1,1,1024,256]{3,2,1,0:T(8,128)(2,1)S(1)}, bf16[1,1,1024,256]{3,2,1,0:T(8,128)(2,1)}, u32[]{:S(2)}) copy-start(bf16[1,1,1024,256]{3,2,1,0:T(8,128)(2,1)} %param.14) | copy-start | bytes 1572868
  3.4 18.1 %copy-start.1 = (bf16[1,1,1024,256]{3,2,1,0:T(8,128)(2,1)S(1)}, bf16[1,1,1024,256]{3,2,1,0:T(8,128)(2,1)}, u32[]{:S(2)}) copy-start(bf16[1,1,1024,256]{3,2,1,0:T(8,128)(2,1)} %param.13) | copy-start | bytes 1572868
  3.4 18.1 %copy-start.4 = (bf16[1,1,1024,256]{3,2,1,0:T(8,128)(2,1)S(1)}, bf16[1,1,1024,256]{3,2,1,0:T(8,128)(2,1)}, u32[]{:S(2)}) copy-start(bf16[1,1,1024,256]{3,2,1,0:T(8,128)(2,1)} %param.15) | copy-start | bytes 1572868
  5.1 16.4 %copy-start.9 = (bf16[256,32]{0,1:T(8,128)(2,1)S(1)}, bf16[256,32]{0,1:T(8,128)(2,1)}, u32[]{:S(2)}) copy-start(bf16[256,32]{0,1:T(8,128)(2,1)} %param.25) | copy-start | bytes 49156
  5.1 8.0 %collective-permute-start = (bf16[2,128,256]{2,1,0:T(8,128)(2,1)S(1)}, bf16[2,128,256]{2,1,0:T(8,128)(2,1)S(1)}, u32[]{:S(2)}, u32[]{:S(2)}) collective-permute-start(bf16[2,128,256]{2,1,0:T(8,128)(2,1)S(1)} %get-tuple-element.34), channel_id=1, source_target_pairs={{0,1},{1,0},{2,3},{3,2},{4,5},{5,4},{6,7},{7,6},{8,9},{9,8},{10,11... | collective-permute-start | bytes 393224 | tf_op jit(solution)/shard_map/ppermute | solution.py:295
  8.1 9.2 %collective-permute-start.1 = (bf16[2,128,256]{2,1,0:T(8,128)(2,1)S(1)}, bf16[2,128,256]{2,1,0:T(8,128)(2,1)S(1)}, u32[]{:S(2)}, u32[]{:S(2)}) collective-permute-start(bf16[2,128,256]{2,1,0:T(8,128)(2,1)S(1)} %get-tuple-element.35), channel_id=1, source_target_pairs={{0,2},{1,3},{2,0},{3,1},{4,6},{5,7},{6,4},{7,5},{8,10},{9,11},{10,... | collective-permute-start | bytes 393224 | tf_op jit(solution)/shard_map/ppermute | solution.py:295
  9.7 7.7 %collective-permute-start.2 = (bf16[2,128,256]{2,1,0:T(8,128)(2,1)S(1)}, bf16[2,128,256]{2,1,0:T(8,128)(2,1)S(1)}, u32[]{:S(2)}, u32[]{:S(2)}) collective-permute-start(bf16[2,128,256]{2,1,0:T(8,128)(2,1)S(1)} %get-tuple-element.36), channel_id=1, source_target_pairs={{0,3},{1,2},{2,1},{3,0},{4,7},{5,6},{6,5},{7,4},{8,11},{9,10},{10,... | collective-permute-start | bytes 393224 | tf_op jit(solution)/shard_map/ppermute | solution.py:295
  9.7 9.0 %collective-permute-start.3 = (bf16[2,128,256]{2,1,0:T(8,128)(2,1)S(1)}, bf16[2,128,256]{2,1,0:T(8,128)(2,1)S(1)}, u32[]{:S(2)}, u32[]{:S(2)}) collective-permute-start(bf16[2,128,256]{2,1,0:T(8,128)(2,1)S(1)} %get-tuple-element.37), channel_id=1, source_target_pairs={{0,1},{1,0},{2,3},{3,2},{4,5},{5,4},{6,7},{7,6},{8,9},{9,8},{10,11... | collective-permute-start | bytes 393224 | tf_op jit(solution)/shard_map/ppermute | solution.py:295
  11.6 9.9 %collective-permute-start.4 = (bf16[2,128,256]{2,1,0:T(8,128)(2,1)S(1)}, bf16[2,128,256]{2,1,0:T(8,128)(2,1)S(1)}, u32[]{:S(2)}, u32[]{:S(2)}) collective-permute-start(bf16[2,128,256]{2,1,0:T(8,128)(2,1)S(1)} %get-tuple-element.38), channel_id=1, source_target_pairs={{0,2},{1,3},{2,0},{3,1},{4,6},{5,7},{6,4},{7,5},{8,10},{9,11},{10,... | collective-permute-start | bytes 393224 | tf_op jit(solution)/shard_map/ppermute | solution.py:295
  13.2 8.4 %collective-permute-start.5 = (bf16[2,128,256]{2,1,0:T(8,128)(2,1)S(1)}, bf16[2,128,256]{2,1,0:T(8,128)(2,1)S(1)}, u32[]{:S(2)}, u32[]{:S(2)}) collective-permute-start(bf16[2,128,256]{2,1,0:T(8,128)(2,1)S(1)} %get-tuple-element.39), channel_id=1, source_target_pairs={{0,3},{1,2},{2,1},{3,0},{4,7},{5,6},{6,5},{7,4},{8,11},{9,10},{10,... | collective-permute-start | bytes 393224 | tf_op jit(solution)/shard_map/ppermute | solution.py:295
  21.5 0.7 copy-start.10
  21.5 0.7 copy-start.13
  22.2 1.2 %copy-start.2 = (bf16[1,1,8,4,128,128]{5,4,3,2,1,0:T(8,128)(2,1)S(1)}, bf16[1,1,8,4,128,128]{5,4,3,2,1,0:T(8,128)(2,1)}, u32[]{:S(2)}) copy-start(bf16[1,1,8,4,128,128]{5,4,3,2,1,0:T(8,128)(2,1)} %param.16) | copy-start | bytes 3145732
  23.5 0.9 %copy-start.5 = (bf16[256,256]{1,0:T(8,128)(2,1)S(1)}, bf16[256,256]{1,0:T(8,128)(2,1)}, u32[]{:S(2)}) copy-start(bf16[256,256]{1,0:T(8,128)(2,1)} %refs_5_.1) | copy-start | bytes 393220
  24.4 0.9 %copy-start.6 = (bf16[256,256]{1,0:T(8,128)(2,1)S(1)}, bf16[256,256]{1,0:T(8,128)(2,1)}, u32[]{:S(2)}) copy-start(bf16[256,256]{1,0:T(8,128)(2,1)} %refs_6_.1) | copy-start | bytes 393220
  25.3 0.9 %copy-start.7 = (bf16[256,256]{1,0:T(8,128)(2,1)S(1)}, bf16[256,256]{1,0:T(8,128)(2,1)}, u32[]{:S(2)}) copy-start(bf16[256,256]{1,0:T(8,128)(2,1)} %refs_7_.1) | copy-start | bytes 393220
  26.2 0.9 %copy-start.8 = (bf16[256,256]{1,0:T(8,128)(2,1)S(1)}, bf16[256,256]{1,0:T(8,128)(2,1)}, u32[]{:S(2)}) copy-start(bf16[256,256]{1,0:T(8,128)(2,1)} %refs_8_.1) | copy-start | bytes 393220
  27.1 0.7 copy-start.11
  41.1 1.6 %collective-permute-start.6 = (bf16[576,256]{1,0:T(8,128)(2,1)S(1)}, bf16[576,256]{1,0:T(8,128)(2,1)S(1)}, u32[]{:S(2)}, u32[]{:S(2)}) collective-permute-start(bf16[576,256]{1,0:T(8,128)(2,1)S(1)} %get-tuple-element.43), channel_id=1, source_target_pairs={{0,4},{4,0},{8,12},{12,8},{16,20},{20,16},{24,28},{28,24},{1,5},{5... | collective-permute-start | bytes 884744 | tf_op jit(solution)/shard_map/ppermute | solution.py:306
  42.9 5.6 %collective-permute-start.7 = (bf16[144,256]{1,0:T(8,128)(2,1)S(1)}, bf16[144,256]{1,0:T(8,128)(2,1)S(1)}, u32[]{:S(2)}, u32[]{:S(2)}) collective-permute-start(bf16[144,256]{1,0:T(8,128)(2,1)S(1)} %get-tuple-element.45), channel_id=1, source_target_pairs={{0,1},{1,0},{2,3},{3,2},{4,5},{5,4},{6,7},{7,6},{8,9},{9,8},{10,11... | collective-permute-start | bytes 221192 | tf_op jit(solution)/shard_map/ppermute | solution.py:295
  44.1 13.1 %collective-permute-start.13 = (bf16[2,128,256]{2,1,0:T(8,128)(2,1)S(1)}, bf16[2,128,256]{2,1,0:T(8,128)(2,1)S(1)}, u32[]{:S(2)}, u32[]{:S(2)}) collective-permute-start(bf16[2,128,256]{2,1,0:T(8,128)(2,1)S(1)} %get-tuple-element.48), channel_id=1, source_target_pairs={{0,1},{1,0},{2,3},{3,2},{4,5},{5,4},{6,7},{7,6},{8,9},{9,8},{10,11... | collective-permute-start | bytes 393224 | tf_op jit(solution)/shard_map/ppermute | solution.py:295
  44.9 5.0 %collective-permute-start.8 = (bf16[144,256]{1,0:T(8,128)(2,1)S(1)}, bf16[144,256]{1,0:T(8,128)(2,1)S(1)}, u32[]{:S(2)}, u32[]{:S(2)}) collective-permute-start(bf16[144,256]{1,0:T(8,128)(2,1)S(1)} %get-tuple-element.46), channel_id=1, source_target_pairs={{0,2},{1,3},{2,0},{3,1},{4,6},{5,7},{6,4},{7,5},{8,10},{9,11},{10,... | collective-permute-start | bytes 221192 | tf_op jit(solution)/shard_map/ppermute | solution.py:295
  46.5 7.0 %collective-permute-start.9 = (bf16[144,256]{1,0:T(8,128)(2,1)S(1)}, bf16[144,256]{1,0:T(8,128)(2,1)S(1)}, u32[]{:S(2)}, u32[]{:S(2)}) collective-permute-start(bf16[144,256]{1,0:T(8,128)(2,1)S(1)} %get-tuple-element.47), channel_id=1, source_target_pairs={{0,3},{1,2},{2,1},{3,0},{4,7},{5,6},{6,5},{7,4},{8,11},{9,10},{10,... | collective-permute-start | bytes 221192 | tf_op jit(solution)/shard_map/ppermute | solution.py:295
  47.6 10.4 %collective-permute-start.14 = (bf16[2,128,256]{2,1,0:T(8,128)(2,1)S(1)}, bf16[2,128,256]{2,1,0:T(8,128)(2,1)S(1)}, u32[]{:S(2)}, u32[]{:S(2)}) collective-permute-start(bf16[2,128,256]{2,1,0:T(8,128)(2,1)S(1)} %get-tuple-element.49), channel_id=1, source_target_pairs={{0,2},{1,3},{2,0},{3,1},{4,6},{5,7},{6,4},{7,5},{8,10},{9,11},{10,... | collective-permute-start | bytes 393224 | tf_op jit(solution)/shard_map/ppermute | solution.py:295
  48.5 9.6 %collective-permute-start.15 = (bf16[2,128,256]{2,1,0:T(8,128)(2,1)S(1)}, bf16[2,128,256]{2,1,0:T(8,128)(2,1)S(1)}, u32[]{:S(2)}, u32[]{:S(2)}) collective-permute-start(bf16[2,128,256]{2,1,0:T(8,128)(2,1)S(1)} %get-tuple-element.50), channel_id=1, source_target_pairs={{0,3},{1,2},{2,1},{3,0},{4,7},{5,6},{6,5},{7,4},{8,11},{9,10},{10,... | collective-permute-start | bytes 393224 | tf_op jit(solution)/shard_map/ppermute | solution.py:295
  53.5 6.4 %collective-permute-start.12 = (bf16[144,256]{1,0:T(8,128)(2,1)S(1)}, bf16[144,256]{1,0:T(8,128)(2,1)S(1)}, u32[]{:S(2)}, u32[]{:S(2)}) collective-permute-start(bf16[144,256]{1,0:T(8,128)(2,1)S(1)} %add.1.refs_0_), channel_id=1, source_target_pairs={{0,24},{4,28},{8,16},{12,20},{16,8},{20,12},{24,0},{28,4},{1,25},{... | collective-permute-start | bytes 221192 | tf_op jit(solution)/shard_map/ppermute | solution.py:303
  57.2 5.3 %collective-permute-start.11 = (bf16[144,256]{1,0:T(8,128)(2,1)S(1)}, bf16[144,256]{1,0:T(8,128)(2,1)S(1)}, u32[]{:S(2)}, u32[]{:S(2)}) collective-permute-start(bf16[144,256]{1,0:T(8,128)(2,1)S(1)} %add.1.refs_0_), channel_id=1, source_target_pairs={{0,16},{4,20},{8,24},{12,28},{16,0},{20,4},{24,8},{28,12},{1,17},{... | collective-permute-start | bytes 221192 | tf_op jit(solution)/shard_map/ppermute | solution.py:303
  57.2 5.2 %collective-permute-start.10 = (bf16[144,256]{1,0:T(8,128)(2,1)S(1)}, bf16[144,256]{1,0:T(8,128)(2,1)S(1)}, u32[]{:S(2)}, u32[]{:S(2)}) collective-permute-start(bf16[144,256]{1,0:T(8,128)(2,1)S(1)} %add.1.refs_0_), channel_id=1, source_target_pairs={{0,8},{4,12},{8,0},{12,4},{16,24},{20,28},{24,16},{28,20},{1,9},{5... | collective-permute-start | bytes 221192 | tf_op jit(solution)/shard_map/ppermute | solution.py:303
  64.0 5.3 %collective-permute-start.18 = (bf16[144,256]{1,0:T(8,128)(2,1)S(1)}, bf16[144,256]{1,0:T(8,128)(2,1)S(1)}, u32[]{:S(2)}, u32[]{:S(2)}) collective-permute-start(bf16[144,256]{1,0:T(8,128)(2,1)S(1)} %get-tuple-element.52.own), channel_id=1, source_target_pairs={{0,3},{1,2},{2,1},{3,0},{4,7},{5,6},{6,5},{7,4},{8,11},{9,10},{10,... | collective-permute-start | bytes 221192 | tf_op jit(solution)/shard_map/ppermute | solution.py:295
  65.2 4.9 %collective-permute-start.17 = (bf16[144,256]{1,0:T(8,128)(2,1)S(1)}, bf16[144,256]{1,0:T(8,128)(2,1)S(1)}, u32[]{:S(2)}, u32[]{:S(2)}) collective-permute-start(bf16[144,256]{1,0:T(8,128)(2,1)S(1)} %get-tuple-element.52.own), channel_id=1, source_target_pairs={{0,2},{1,3},{2,0},{3,1},{4,6},{5,7},{6,4},{7,5},{8,10},{9,11},{10,... | collective-permute-start | bytes 221192 | tf_op jit(solution)/shard_map/ppermute | solution.py:295
  66.2 4.4 %collective-permute-start.16 = (bf16[144,256]{1,0:T(8,128)(2,1)S(1)}, bf16[144,256]{1,0:T(8,128)(2,1)S(1)}, u32[]{:S(2)}, u32[]{:S(2)}) collective-permute-start(bf16[144,256]{1,0:T(8,128)(2,1)S(1)} %get-tuple-element.52.own), channel_id=1, source_target_pairs={{0,1},{1,0},{2,3},{3,2},{4,5},{5,4},{6,7},{7,6},{8,9},{9,8},{10,11... | collective-permute-start | bytes 221192 | tf_op jit(solution)/shard_map/ppermute | solution.py:295
  70.6 1.6 %collective-permute-start.19 = (bf16[576,256]{1,0:T(8,128)(2,1)S(1)}, bf16[576,256]{1,0:T(8,128)(2,1)S(1)}, u32[]{:S(2)}, u32[]{:S(2)}) collective-permute-start(bf16[576,256]{1,0:T(8,128)(2,1)S(1)} %bitcast.23), channel_id=1, source_target_pairs={{0,4},{4,0},{8,12},{12,8},{16,20},{20,16},{24,28},{28,24},{1,5},{5... | collective-permute-start | bytes 884744 | tf_op jit(solution)/shard_map/ppermute | solution.py:306

commit v2 on v1

v2 whole, which is shorter than its diff:
```python
import functools

import jax
import jax.numpy as jnp
from jax import lax
from jax.experimental import pallas as pl
from jax.experimental.pallas import tpu as pltpu
from jax.sharding import PartitionSpec as P

BF16 = jnp.bfloat16
F32 = jnp.float32
VMEM = pl.BlockSpec(memory_space=pltpu.VMEM)
SMEM = pl.BlockSpec(memory_space=pltpu.SMEM)
HBM = pl.BlockSpec(memory_space=pltpu.HBM)
CORES = 2
PACK_LIMIT = 40 << 20
PREP_LIMIT = 4 << 20
AUX_FLOPS = 10**6


def dot(former, latter):
    return jnp.dot(former, latter, preferred_element_type=F32)


def transpose_dot(former, latter):
    return lax.dot_general(former, latter, (((0,), (0,)), ((), ())), preferred_element_type=F32)


def dot_by_transpose(former, latter):
    return lax.dot_general(former, latter, (((1,), (1,)), ((), ())), preferred_element_type=F32)


def partner(index, step, count):
    if count & (count - 1) == 0:
        return index ^ step, index ^ step
    return (index + step) % count, (index + count - step) % count


def pack_kernel(peers, slots, blocks, send, feat_in, past_in, *refs):
    outs, (token, lists, feat, past, sems) = refs[:-5], refs[-5:]
    g = lax.axis_index("grp")
    pairs = ((send, lists), (feat_in, feat), (past_in, past))
    copies = [pltpu.make_async_copy(src, dst, sems.at[i]) for i, (src, dst) in enumerate(pairs)]
    for copy in copies:
        copy.start()
    token[...] = jnp.zeros_like(token)
    copies[0].wait()
    for which, values in enumerate((feat, past)):
        copies[1 + which].wait()
        for step in range(1, peers):
            peer, _ = partner(g, step, peers)
            for s in range(slots):
                block = jnp.minimum(lists[s, peer], blocks - 1)
                outs[which * (peers - 1) + step - 1][s] = values[block]


def prepare_kernel(dims, feat_in, tiles_in, token, tiles, tiles_t, feat, feat_t, sems):
    blocks, picks, rows = dims
    whole = pltpu.make_async_copy(feat_in, feat, sems.at[0])
    copies = [
        pltpu.make_async_copy(tiles_in.at[b], tiles.at[b], sems.at[1 + b]) for b in range(blocks)
    ]
    for copy in [whole] + copies:
        copy.start()
    whole.wait()
    for b in range(blocks):
        feat_t[:, b * rows : (b + 1) * rows] = feat[b].T
    for b in range(blocks):
        copies[b].wait()
        for k in range(picks):
            tiles_t[b, k * rows : (k + 1) * rows] = tiles[b, k].T


def gathered(table, sources, b, picks):
    return jnp.concatenate([table[sources[k, b]] for k in range(picks)], axis=0)


def gate_of(pre):
    gate = 0.5 * jnp.tanh(0.5 * pre) + 0.5
    value = pre * gate
    return value, gate + value * (1.0 - gate)


def first_kernel(dims, sources_in, wn_in, ws_in, feat, tiles, *refs):
    peers, slots, blocks, picks, rows, width = dims
    inc = peers - 1
    feat_in, refs = refs[:inc], refs[inc:]
    (hidden_out, own2, slope1, agg_t, hidden_t), refs = refs[:5], refs[5:]
    table, sources, wn, ws, sems, out_sem = refs
    g = lax.axis_index("grp")
    listed = pltpu.make_async_copy(sources_in, sources, sems.at[0])
    weights = [
        pltpu.make_async_copy(wn_in, wn, sems.at[1]),
        pltpu.make_async_copy(ws_in, ws, sems.at[2]),
    ]
    for copy in [listed] + weights:
        copy.start()
    table[pl.ds(0, blocks)] = feat[...]
    for step in range(1, peers):
        _, origin = partner(g, step, peers)
        table[pl.ds(blocks + origin * slots, slots)] = feat_in[step - 1][...]
    listed.wait()
    aggs = []
    for b in range(blocks):
        row = jnp.concatenate([tiles[b, k] for k in range(picks)], axis=1)
        agg = dot(row, gathered(table, sources, b, picks)).astype(BF16)
        aggs.append(agg)
        agg_t[:, b * rows : (b + 1) * rows] = agg.T
    for copy in weights:
        copy.wait()
    both_w = jnp.concatenate([wn[...], ws[...]], axis=0)
    pair = 2
    span = pair * rows
    for i in range(blocks // pair):
        at = pl.ds(i * span, span)
        nodes_feat = table[pl.ds(i * pair, pair)].reshape(span, width)
        both = jnp.concatenate(
            [jnp.concatenate(aggs[i * pair : (i + 1) * pair], axis=0), nodes_feat], axis=1
        )
        value, slope = gate_of(dot(both, both_w))
        slope1[at] = slope
        hidden = value.astype(BF16)
        own2[pl.ds(i * pair, pair)] = hidden.reshape(pair, rows, width)
        hidden_t[:, at] = hidden.T
    out = pltpu.make_async_copy(own2, hidden_out, out_sem)
    out.start()
    out.wait()


def second_kernel(dims, *refs):
    peers, slots, blocks, picks, rows, width, bins_count, pay_rows = dims
    inc = peers - 1
    hbm_in, refs = refs[:7], refs[7:]
    (own2, slope1, tiles, tiles_t, agg1_t, feat_t, hidden_t), refs = refs[:7], refs[7:]
    past_in, refs = refs[:inc], refs[inc:]
    (grad_hidden_out, keep, send, back), refs = refs[:4], refs[4:]
    loaded, refs = refs[:7], refs[7:]
    table, agg_t, gtab, grad_hidden, pay, sems, out_sem = refs
    sources, wn, ws, hw, bins, flags, aux = loaded
    g = lax.axis_index("grp")
    core = lax.axis_index("clus") % CORES
    device = lax.axis_index("clus") * peers + g
    nodes = blocks * rows
    scale = 1.0 / (nodes * peers)
    loads = [
        pltpu.make_async_copy(src, dst, sems.at[i])
        for i, (src, dst) in enumerate(zip(hbm_in, loaded))
    ]
    for load in loads:
        load.start()
    table[pl.ds(0, blocks)] = own2[...]
    for step in range(1, peers):
        _, origin = partner(g, step, peers)
        table[pl.ds(blocks + origin * slots, slots)] = past_in[step - 1][...]
    back[...] = jnp.zeros(back.shape, F32)
    loads[0].wait()
    aggs = []
    for b in range(blocks):
        row = jnp.concatenate([tiles[b, k] for k in range(picks)], axis=1)
        agg = dot(row, gathered(table, sources, b, picks)).astype(BF16)
        aggs.append(agg)
        agg_t[:, b * rows : (b + 1) * rows] = agg.T
    for load in loads[1:]:
        load.wait()
    pair = 2
    span = pair * rows
    head = hw[...]
    step_col = lax.broadcasted_iota(jnp.int32, (bins_count, span), 0)
    both_w = jnp.concatenate([wn[...], ws[...]], axis=0)
    loss = jnp.zeros((bins_count, span), F32)
    ghw = jnp.zeros((bins_count, width), F32)
    grad_pres, grad_aggs = [], []
    for i in range(blocks // pair):
        at = pl.ds(i * pair, pair)
        both = jnp.concatenate(
            [
                jnp.concatenate(aggs[i * pair : (i + 1) * pair], axis=0),
                table[at].reshape(span, width),
            ],
            axis=1,
        )
        value, slope = gate_of(dot(both, both_w))
        hidden = value.astype(BF16)
        logits = dot_by_transpose(head, hidden)
        counted = step_col <= bins[i]
        event = jnp.where(step_col == bins[i], flags[i].astype(F32), 0.0)
        tail = jnp.exp(-jnp.abs(logits))
        soft = jnp.maximum(logits, 0.0) + jnp.log1p(tail)
        loss = loss + jnp.where(counted, soft, 0.0) - event * logits
        chance = jnp.where(logits >= 0.0, 1.0, tail) / (1.0 + tail)
        glog = (jnp.where(counted, chance, 0.0) - event).astype(BF16)
        ghw = ghw + dot(glog, hidden)
        grad_pre = (transpose_dot(glog, head) * slope).astype(BF16)
        grad_pres.append(grad_pre)
        grad_aggs.append(dot_by_transpose(grad_pre, wn[...]).astype(BF16))
        own = dot_by_transpose(grad_pre, ws[...]) + aux[at].reshape(span, width).astype(F32)
        gtab[at] = own.reshape(pair, rows, width)
    remote = pl.ds(blocks, peers * slots)
    gtab[remote] = jnp.zeros((peers * slots, rows, width), F32)
    for b in range(blocks):
        part = grad_aggs[b // pair][(b % pair) * rows : (b % pair + 1) * rows]
        spread = dot(tiles_t[b], part)
        for k in range(picks):
            gtab[sources[k, b]] += spread[k * rows : (k + 1) * rows]
    back[...] = gtab[remote]
    total = gtab[pl.ds(0, blocks)]
    grad_hidden[...] = total.astype(BF16)
    out = pltpu.make_async_copy(grad_hidden, grad_hidden_out, out_sem)
    out.start()
    grad_first = (total.reshape(nodes, width) * slope1[...]).astype(BF16)
    grad_second = jnp.concatenate(grad_pres, axis=0)
    terms = (
        (agg1_t, grad_first),
        (feat_t, grad_first),
        (agg_t, grad_second),
        (hidden_t, grad_second),
    )
    for n, (left, grads) in enumerate(terms):
        pay[pl.ds(n * width, width)] = (dot(left[...], grads) * scale).astype(BF16)
    part = jnp.sum(loss) * scale
    high = part.astype(BF16).astype(F32)
    tail_rows = pay_rows - 4 * width - bins_count
    lane = lax.broadcasted_iota(jnp.int32, (tail_rows, width), 0) * width + lax.broadcasted_iota(
        jnp.int32, (tail_rows, width), 1
    )
    loss_rows = jnp.where(lane == 2 * device, high, 0.0) + jnp.where(
        lane == 2 * device + 1, part - high, 0.0
    )
    pay[pl.ds(4 * width, bins_count)] = (ghw * scale).astype(BF16)
    pay[pl.ds(4 * width + bins_count, tail_rows)] = loss_rows.astype(BF16)
    half = pay_rows // CORES
    keep[...] = pay[pl.ds(pl.multiple_of(core * half, 16), half)]
    send[...] = pay[pl.ds(pl.multiple_of((1 - core) * half, 16), half)]
    out.wait()


def split_kernel(peers, kept, came, own, *outs):
    g = lax.axis_index("grp")

    def chunk(p):
        return (kept[p].astype(F32) + came[p].astype(F32)).astype(BF16)

    own[...] = chunk(g)
    for step in range(1, peers):
        peer, _ = partner(g, step, peers)
        outs[step - 1][...] = chunk(peer)


def add_kernel(*refs):
    total = refs[0][...].astype(F32)
    for ref in refs[1:-1]:
        if ref.shape == total.shape:
            total = total + ref[...].astype(F32)
    refs[-1][...] = total.astype(BF16)


def join_kernel(peers, own, *refs):
    out = refs[-1]
    g = lax.axis_index("grp")
    out[g] = own[...]
    for step in range(1, peers):
        _, origin = partner(g, step, peers)
        out[origin] = refs[step - 1][...]


def finish_kernel(dims, mine, other, *outs):
    width, bins_count, pay_rows = dims
    pay = outs[-1]
    half = pay_rows // CORES
    core = lax.axis_index("clus") % CORES
    pay[pl.ds(pl.multiple_of(core * half, 16), half)] = mine[...]
    pay[pl.ds(pl.multiple_of((1 - core) * half, 16), half)] = other[...]
    for i in range(4):
        outs[i][...] = pay[pl.ds(i * width, width)].astype(F32)
    outs[4][...] = pay[pl.ds(4 * width, bins_count)].astype(F32)
    loss_rows = pay[pl.ds(4 * width + bins_count, pay_rows - 4 * width - bins_count)].astype(F32)
    outs[5][0, 0] = jnp.sum(loss_rows)


def back_kernel(peers, slots, blocks, back, after, *outs):
    g = lax.axis_index("grp")
    for step in range(1, peers):
        _, origin = partner(g, step, peers)
        outs[step - 1][...] = back[pl.ds(origin * slots, slots)].astype(BF16)


def aux_kernel(peers, slots, blocks, send, *refs):
    back, out, token, total, lists, sem = refs[:-5], *refs[-5:]
    g = lax.axis_index("grp")
    listed = pltpu.make_async_copy(send, lists, sem)
    listed.start()
    total[...] = jnp.zeros_like(total)
    token[...] = jnp.zeros_like(token)
    listed.wait()
    for step in range(1, peers):
        peer, _ = partner(g, step, peers)
        for s in range(slots):
            total[lists[s, peer]] += back[step - 1][s].astype(F32)
    out[...] = total[pl.ds(0, blocks)].astype(BF16)


def shards(
    clus_count,
    peers,
    features,
    history,
    aux_history,
    tile_values,
    tile_sources,
    send_list,
    event_bins,
    event_flags,
    neigh_first,
    self_first,
    neigh_second,
    self_second,
    hazard_weight,
):
    blocks, picks, rows = tile_values.shape[2:5]
    width = features.shape[3]
    slots = send_list.shape[3]
    bins_count = hazard_weight.shape[1]
    devices = clus_count * peers
    chips_z = clus_count // CORES
    inc = peers - 1
    used = 4 * width + bins_count + -(-2 * devices // width)
    pay_rows = -(-used // (16 * CORES * peers)) * 16 * CORES * peers
    half = pay_rows // CORES
    chunk = half // peers
    block_shape = (blocks, rows, width)
    slot_shape = (slots, rows, width)
    routing = send_list[0, 0].T
    feat = features.reshape(block_shape)
    past = history.reshape(block_shape)
    params = pltpu.CompilerParams(vmem_limit_bytes=20 << 20)
    small = pltpu.CompilerParams(vmem_limit_bytes=4 << 20)

    def shape(dims, dtype=BF16):
        return jax.ShapeDtypeStruct(dims, dtype)

    def grp_pairs(step):
        return [(i, partner(i, step, peers)[0]) for i in range(peers)]

    def over_grp(value, step):
        return lax.ppermute(value, "grp", grp_pairs(step))

    def over_z(value, step):
        pairs = [
            (z * CORES + c, partner(z, step, chips_z)[0] * CORES + c)
            for z in range(chips_z)
            for c in range(CORES)
        ]
        return lax.ppermute(value, "clus", pairs)

    def over_core(value):
        return lax.ppermute(value, "clus", [(i, i ^ 1) for i in range(clus_count)])

    lists = (slots, peers)
    nodes = blocks * rows
    table = blocks + peers * slots
    tiles = tile_values[0, 0]
    sources = tile_sources[0, 0].T
    square = (width, width)
    turned = (width, nodes)
    packed = pl.pallas_call(
        functools.partial(pack_kernel, peers, slots, blocks),
        out_shape=[shape(slot_shape)] * (2 * inc) + [shape((8, 128), F32)],
        in_specs=[HBM] * 3,
        out_specs=[VMEM] * (2 * inc + 1),
        scratch_shapes=[
            pltpu.SMEM(lists, jnp.int32),
            pltpu.VMEM(block_shape, BF16),
            pltpu.VMEM(block_shape, BF16),
            pltpu.SemaphoreType.DMA((3,)),
        ],
        compiler_params=pltpu.CompilerParams(vmem_limit_bytes=PACK_LIMIT),
        name="pack",
    )(routing, feat, past)
    feat_in = [over_grp(packed[i], i + 1) for i in range(inc)]
    past_in = [over_grp(packed[inc + i], i + 1) for i in range(inc)]
    tiles, tiles_t, feat, feat_t = pl.pallas_call(
        functools.partial(prepare_kernel, (blocks, picks, rows)),
        out_shape=[
            shape(tiles.shape),
            shape((blocks, picks * rows, rows)),
            shape(block_shape),
            shape(turned),
        ],
        in_specs=[HBM] * 2 + [VMEM],
        out_specs=[VMEM] * 4,
        scratch_shapes=[pltpu.SemaphoreType.DMA((1 + blocks,))],
        compiler_params=pltpu.CompilerParams(vmem_limit_bytes=PREP_LIMIT),
        cost_estimate=pl.CostEstimate(flops=10**9, bytes_accessed=10**7, transcendentals=0),
        name="prepare",
    )(feat, tiles, packed[2 * inc])

    pair_shape = (blocks // 2, 1, 2 * rows)
    first = pl.pallas_call(
        functools.partial(first_kernel, (peers, slots, blocks, picks, rows, width)),
        out_shape=[
            shape(block_shape),
            shape(block_shape),
            shape((nodes, width), F32),
            shape(turned),
            shape(turned),
        ],
        in_specs=[HBM] * 3 + [VMEM] * (2 + inc),
        out_specs=[HBM] + [VMEM] * 4,
        scratch_shapes=[
            pltpu.VMEM((table, rows, width), BF16),
            pltpu.SMEM((picks, blocks), jnp.int32),
            pltpu.VMEM(square, BF16),
            pltpu.VMEM(square, BF16),
            pltpu.SemaphoreType.DMA((3,)),
            pltpu.SemaphoreType.DMA,
        ],
        compiler_params=params,
        name="first_layer",
    )(sources, neigh_first, self_first, feat, tiles, *feat_in)
    hidden_first = first[0]
    grad_hidden, kept, sent, gtab_back = pl.pallas_call(
        functools.partial(
            second_kernel, (peers, slots, blocks, picks, rows, width, bins_count, pay_rows)
        ),
        out_shape=[
            shape(block_shape),
            shape((half, width)),
            shape((half, width)),
            shape((peers * slots, rows, width), F32),
        ],
        in_specs=[HBM] * 7 + [VMEM] * (7 + inc),
        out_specs=[HBM] + [VMEM] * 3,
        scratch_shapes=[
            pltpu.SMEM((picks, blocks), jnp.int32),
            pltpu.VMEM(square, BF16),
            pltpu.VMEM(square, BF16),
            pltpu.VMEM((bins_count, width), BF16),
            pltpu.VMEM(pair_shape, jnp.int32),
            pltpu.VMEM(pair_shape, jnp.int32),
            pltpu.VMEM(block_shape, BF16),
            pltpu.VMEM((table, rows, width), BF16),
            pltpu.VMEM(turned, BF16),
            pltpu.VMEM((table, rows, width), F32),
            pltpu.VMEM(block_shape, BF16),
            pltpu.VMEM((pay_rows, width), BF16),
            pltpu.SemaphoreType.DMA((7,)),
            pltpu.SemaphoreType.DMA,
        ],
        compiler_params=params,
        name="second_layer",
    )(
        sources,
        neigh_second,
        self_second,
        hazard_weight.T,
        event_bins.reshape(pair_shape),
        event_flags.reshape(pair_shape),
        aux_history.reshape(block_shape),
        first[1],
        first[2],
        tiles,
        tiles_t,
        first[3],
        feat_t,
        first[4],
        *past_in,
    )

    came = over_core(sent)
    parts = pl.pallas_call(
        functools.partial(split_kernel, peers),
        out_shape=[shape((chunk, width))] * peers,
        in_specs=[VMEM, VMEM],
        out_specs=[VMEM] * peers,
        compiler_params=small,
        name="split",
    )(kept.reshape(peers, chunk, width), came.reshape(peers, chunk, width))
    from_grp = [over_grp(parts[i], i) for i in range(1, peers)]

    def add(*values):
        return pl.pallas_call(
            add_kernel,
            out_shape=shape((chunk, width)),
            in_specs=[VMEM] * len(values),
            out_specs=VMEM,
            compiler_params=small,
            name="add",
        )(*values)

    mine = add(parts[0], *from_grp)
    back = pl.pallas_call(
        functools.partial(back_kernel, peers, slots, blocks),
        out_shape=[shape(slot_shape)] * inc,
        in_specs=[VMEM, VMEM],
        out_specs=[VMEM] * inc,
        compiler_params=small,
        name="back",
    )(gtab_back, parts[0])
    came_back = [over_grp(back[i], i + 1) for i in range(inc)]
    new_aux, token = pl.pallas_call(
        functools.partial(aux_kernel, peers, slots, blocks),
        out_shape=[shape(block_shape), shape((8, 128), F32)],
        in_specs=[HBM] + [VMEM] * inc,
        out_specs=[VMEM] * 2,
        scratch_shapes=[
            pltpu.VMEM((blocks + 1, rows, width), F32),
            pltpu.SMEM(lists, jnp.int32),
            pltpu.SemaphoreType.DMA,
        ],
        compiler_params=small,
        cost_estimate=pl.CostEstimate(flops=AUX_FLOPS, bytes_accessed=10**6, transcendentals=0),
        name="aux",
    )(routing, *came_back)
    mine = add(mine, *[over_z(mine, i) for i in range(1, chips_z)])
    others = [over_grp(mine, i) for i in range(1, peers)]
    joined = pl.pallas_call(
        functools.partial(join_kernel, peers),
        out_shape=shape((peers, chunk, width)),
        in_specs=[VMEM] * (peers + 1),
        out_specs=VMEM,
        compiler_params=small,
        name="join",
    )(mine, *others, token).reshape(half, width)
    other_half = over_core(joined)
    grads = pl.pallas_call(
        functools.partial(finish_kernel, (width, bins_count, pay_rows)),
        out_shape=[shape(square, F32)] * 4 + [shape((bins_count, width), F32), shape((1, 1), F32)],
        in_specs=[VMEM] * 2,
        out_specs=[VMEM] * 5 + [SMEM],
        scratch_shapes=[pltpu.VMEM((pay_rows, width), BF16)],
        compiler_params=small,
        name="finish",
    )(joined, other_half)
    return (
        hidden_first.reshape(features.shape),
        grad_hidden.reshape(features.shape),
        new_aux.reshape(features.shape),
        *grads[:4],
        grads[4].T,
        grads[5][0, 0],
    )


def solution(mesh):
    split = P("clus", "grp")
    whole = P()
    return jax.shard_map(
        functools.partial(shards, mesh.shape["clus"], mesh.shape["grp"]),
        mesh=mesh,
        in_specs=(split,) * 8 + (whole,) * 5,
        out_specs=(split,) * 3 + (whole,) * 6,
        check_vma=False,
    )
```

time: 73.7 us -> 57.7 us (0.78)
  waiting for transfers between devices: 20.3 us -> 12.5 us
  local copies, waits for them, and re-layouts: 8.96 us -> 3.79 us
  Pallas kernels: 17.8 us -> 14.2 us
    ppermute x15, waiting for transfers between devices: 12.7 us -> 5.84 us  [over_grp(): return lax.ppermute(value, 'grp', grp_pairs(step))]
    unnamed x28 -> x26, local copies, waits for them, and re-layouts: 8.96 us -> 3.79 us
    pallas_call x3 -> x6, Pallas kernels: 16 us -> 13.4 us  [the longest x1 5.85 us: shards(): pl.pallas_call(functools.partial(second_kernel, (peers, slots, blocks, pi...]
    pallas_call x1, Pallas kernels: 1.71 us -> 0.64 us  [shards(): pl.pallas_call(functools.partial(pack_kernel, peers, slots, blocks), out_...]
    ppermute x3, waiting for transfers between devices: 4.46 us -> 3.53 us  [over_z(): return lax.ppermute(value, 'clus', pairs)]
  transfers between devices with their start and end apart: 20 -> 20, of which waited for: 11 -> 9; matrix products, arithmetic and copies ran while one was open for 0% -> 0% of each run, Pallas kernels for 0% -> 11%
where the time goes in v2:
time: 57.7 us; the launch traced here: 57.4 us
  starting transfers between devices  26 us (45%)
  Pallas kernels  14.2 us (25%)
  waiting for transfers between devices  12.5 us (22%)
  local copies, waits for them, and re-layouts  3.79 us (7%)
  between operations  0.85 us (1%)
    ppermute x15, starting transfers between devices, over_grp(): return lax.ppermute(value, 'grp', grp_pairs(step))  21.4 us
    pallas_call x1, Pallas kernels, shards(): pl.pallas_call(functools.partial(second_kernel, (peers, slots, blocks, pi...  5.85 us
    ppermute x15, waiting for transfers between devices, over_grp(): return lax.ppermute(value, 'grp', grp_pairs(step))  5.84 us
    ppermute x3, starting transfers between devices, over_z(): return lax.ppermute(value, 'clus', pairs)  4.48 us
    unnamed x26, local copies, waits for them, and re-layouts  3.79 us
    ppermute x3, waiting for transfers between devices, over_z(): return lax.ppermute(value, 'clus', pairs)  3.53 us
    ppermute x2, waiting for transfers between devices, over_core(): return lax.ppermute(value, 'clus', [(i, i ^ 1) for i in range(clus_count)])  3.14 us
    pallas_call x1, Pallas kernels, shards(): pl.pallas_call(functools.partial(first_kernel, (peers, slots, blocks, pic...  2.58 us
  transfers between devices with their start and end apart: 20, of which 9 were waited for; matrix products, arithmetic and copies ran while one was open for 0% of the time, Pallas kernels for 11%

profile of v2, /device:TPU:0, one launch (start us, length us, event | category | flops | bytes accessed | tf_op | source)
XLA Modules:
  0.0 57.4 jit_solution(13452649947308838317)
XLA Ops:
  0.6 0.0 copy-start.11
  0.7 0.7 %copy-done.11 = s32[1,1,4,2]{2,3,1,0:T(2,128)S(1)} copy-done((s32[1,1,4,2]{2,3,1,0:T(2,128)S(1)}, s32[1,1,4,2]{2,3,1,0:T(2,128)}, u32[]{:S(2)}) %copy-start.11) | copy-done | bytes 56
  1.3 1.0 %copy-done.1 = bf16[1,1,1024,256]{3,2,1,0:T(8,128)(2,1)S(1)} copy-done((bf16[1,1,1024,256]{3,2,1,0:T(8,128)(2,1)S(1)}, bf16[1,1,1024,256]{3,2,1,0:T(8,128)(2,1)}, u32[]{:S(2)}) %copy-start.1) | copy-done | bytes 524312
  2.4 1.0 %copy-done.2 = bf16[1,1,1024,256]{3,2,1,0:T(8,128)(2,1)S(1)} copy-done((bf16[1,1,1024,256]{3,2,1,0:T(8,128)(2,1)S(1)}, bf16[1,1,1024,256]{3,2,1,0:T(8,128)(2,1)}, u32[]{:S(2)}) %copy-start.2) | copy-done | bytes 524312
  3.4 0.6 %pack.1 = (bf16[2,128,256]{2,1,0:T(8,128)(2,1)S(1)}, bf16[2,128,256]{2,1,0:T(8,128)(2,1)S(1)}, bf16[2,128,256]{2,1,0:T(8,128)(2,1)S(1)}, bf16[2,128,256]{2,1,0:T...) custom-call(s32[2,4]{1,0:T(2,128)S(1)} %bitcast.34, ...), custom_call_target="tpu_custom_call" | custom-call | tf_op jit(solution)/shard_map/pack/pallas_call | solution.py:365
  4.1 3.0 %collective-permute-start = (bf16[2,128,256]{2,1,0:T(8,128)(2,1)S(1)}, bf16[2,128,256]{2,1,0:T(8,128)(2,1)S(1)}, u32[]{:S(2)}, u32[]{:S(2)}) collective-permute-start(bf16[2,128,256]{2,1,0:T(8,128)(2,1)S(1)} %get-tuple-element.47), channel_id=1, source_target_pairs={{0,1},{1,0},{2,3},{3,2},{4,5},{5,4},{6,7},{7,6},{8,9},{9,8},{10,11... | collective-permute-start | bytes 393224 | tf_op jit(solution)/shard_map/ppermute | solution.py:345
  7.1 1.5 %collective-permute-start.1 = (bf16[2,128,256]{2,1,0:T(8,128)(2,1)S(1)}, bf16[2,128,256]{2,1,0:T(8,128)(2,1)S(1)}, u32[]{:S(2)}, u32[]{:S(2)}) collective-permute-start(bf16[2,128,256]{2,1,0:T(8,128)(2,1)S(1)} %get-tuple-element.48), channel_id=1, source_target_pairs={{0,2},{1,3},{2,0},{3,1},{4,6},{5,7},{6,4},{7,5},{8,10},{9,11},{10,... | collective-permute-start | bytes 393224 | tf_op jit(solution)/shard_map/ppermute | solution.py:345
  8.6 0.0 collective-permute-start.2
  8.6 1.9 %collective-permute-start.3 = (bf16[2,128,256]{2,1,0:T(8,128)(2,1)S(1)}, bf16[2,128,256]{2,1,0:T(8,128)(2,1)S(1)}, u32[]{:S(2)}, u32[]{:S(2)}) collective-permute-start(bf16[2,128,256]{2,1,0:T(8,128)(2,1)S(1)} %get-tuple-element.57), channel_id=1, source_target_pairs={{0,1},{1,0},{2,3},{3,2},{4,5},{5,4},{6,7},{7,6},{8,9},{9,8},{10,11... | collective-permute-start | bytes 393224 | tf_op jit(solution)/shard_map/ppermute | solution.py:345
  10.5 1.5 %collective-permute-start.4 = (bf16[2,128,256]{2,1,0:T(8,128)(2,1)S(1)}, bf16[2,128,256]{2,1,0:T(8,128)(2,1)S(1)}, u32[]{:S(2)}, u32[]{:S(2)}) collective-permute-start(bf16[2,128,256]{2,1,0:T(8,128)(2,1)S(1)} %get-tuple-element.58), channel_id=1, source_target_pairs={{0,2},{1,3},{2,0},{3,1},{4,6},{5,7},{6,4},{7,5},{8,10},{9,11},{10,... | collective-permute-start | bytes 393224 | tf_op jit(solution)/shard_map/ppermute | solution.py:345
  12.1 0.0 collective-permute-done.refs_0_
  12.1 2.3 %collective-permute-start.5 = (bf16[2,128,256]{2,1,0:T(8,128)(2,1)S(1)}, bf16[2,128,256]{2,1,0:T(8,128)(2,1)S(1)}, u32[]{:S(2)}, u32[]{:S(2)}) collective-permute-start(bf16[2,128,256]{2,1,0:T(8,128)(2,1)S(1)} %get-tuple-element.59), channel_id=1, source_target_pairs={{0,3},{1,2},{2,1},{3,0},{4,7},{5,6},{6,5},{7,4},{8,11},{9,10},{10,... | collective-permute-start | bytes 393224 | tf_op jit(solution)/shard_map/ppermute | solution.py:345
  14.4 0.0 copy-done.12
  14.4 2.4 %prepare.1 = (bf16[8,4,128,128]{3,2,1,0:T(8,128)(2,1)S(1)}, bf16[8,512,128]{2,1,0:T(8,128)(2,1)S(1)}, bf16[8,128,256]{2,1,0:T(8,128)(2,1)S(1)}, bf16[256,1024]{1,0:T(8,128)(2,1)S(1)}) custom-call(bf16[8,128,256]{2,1,0:T(8,128)(2,1)S(1)} %bitcast.26, bf16[8,4,128,128]{3,2,1,0:T(8,128)(2,1)S(1)} %bitcast.36, f32[8,128]{1,0:T(8,128)S(1)} %get-tuple-element.44.token), custom_call_target="tpu_custom_call" | custom-call | flops 1000000000 | bytes 10000000 | tf_op jit(solution)/shard_map/prepare/pallas_call | solution.py:381
  16.8 0.0 collective-permute-done.1.refs_1_
  16.8 0.0 collective-permute-done.2.refs_2_
  16.8 0.0 copy-start.8
  16.8 0.0 copy-done.3
  16.8 0.0 copy-done.4
  16.9 0.7 %copy-done.8 = s32[1,1,8,4]{2,3,1,0:T(4,128)S(1)} copy-done((s32[1,1,8,4]{2,3,1,0:T(4,128)S(1)}, s32[1,1,8,4]{2,3,1,0:T(4,128)}, u32[]{:S(2)}) %copy-start.8) | copy-done | bytes 152
  17.5 0.0 copy-start.10
  17.5 2.6 %first_layer.1 = (bf16[8,128,256]{2,1,0:T(8,128)(2,1)}, bf16[8,128,256]{2,1,0:T(8,128)(2,1)S(1)}, f32[1024,256]{1,0:T(8,128)S(1)}, bf16[256,1024]{1,0:T(8,128)(2,1)S(1)}, bf16[256,1024]{1,0:T(8,128)(2,1)S(1)}) custom-call(s32[4,8]{1,0:T(4,128)S(1)} %bitcast.30, bf16[256,256]{1,0:T(8,128)(2,1)S(1)} %copy-done.3, bf16[256,256]{1,0:T(8,128)(2,1)S(1)} %copy-done.4, ...), custom_call_target="tpu_custom_call" | custom-call | tf_op jit(solution)/shard_map/first_layer/pallas_call | solution.py:398
  20.1 0.0 copy-start.7
  20.1 0.0 collective-permute-done.3.refs_14_
  20.1 0.3 collective-permute-done.4.refs_15_
  20.5 0.0 collective-permute-done.5.refs_16_
  20.5 0.0 copy-done
  20.5 0.0 copy-done.5
  20.5 0.0 copy-done.6
  20.5 0.0 copy-done.9
  20.5 0.0 copy-done.10
  20.5 0.3 copy-done.7
  20.8 5.9 %second_layer.1 = (bf16[8,128,256]{2,1,0:T(8,128)(2,1)}, bf16[576,256]{1,0:T(8,128)(2,1)S(1)}, bf16[576,256]{1,0:T(8,128)(2,1)S(1)}, f32[8,128,256]{2,1,0:T(8,128)S(1)}) custom-call(s32[4,8]{1,0:T(4,128)S(1)} %bitcast.31, bf16[256,256]{1,0:T(8,128)(2,1)S(1)} %copy-done.5, bf16[256,256]{1,0:T(8,128)(2,1)S(1)} %copy-done.6, bf16[32,256]{1,0:T(8,128)(2,1)S(1)} %bitcast.29, ...), custom_call_target="tpu_custom_call" | custom-call | tf_op jit(solution)/shard_map/second_layer/pallas_call | solution.py:421
  26.7 0.1 collective-permute-start.6
  26.8 1.6 %collective-permute-done.6 = bf16[576,256]{1,0:T(8,128)(2,1)S(1)} collective-permute-done((bf16[576,256]{1,0:T(8,128)(2,1)S(1)}, bf16[576,256]{1,0:T(8,128)(2,1)S(1)}, u32[]{:S(2)}, u32[]{:S(2)}) %collective-permute-start.6) | collective-permute-done | bytes 294944 | tf_op jit(solution)/shard_map/ppermute | solution.py:356
  28.3 0.1 split.1
  28.4 1.0 %collective-permute-start.10 = (bf16[144,256]{1,0:T(8,128)(2,1)S(1)}, bf16[144,256]{1,0:T(8,128)(2,1)S(1)}, u32[]{:S(2)}, u32[]{:S(2)}) collective-permute-start(bf16[144,256]{1,0:T(8,128)(2,1)S(1)} %get-tuple-element.69), channel_id=1, source_target_pairs={{0,1},{1,0},{2,3},{3,2},{4,5},{5,4},{6,7},{7,6},{8,9},{9,8},{10,11... | collective-permute-start | bytes 221192 | tf_op jit(solution)/shard_map/ppermute | solution.py:345
  29.4 1.6 %collective-permute-start.11 = (bf16[144,256]{1,0:T(8,128)(2,1)S(1)}, bf16[144,256]{1,0:T(8,128)(2,1)S(1)}, u32[]{:S(2)}, u32[]{:S(2)}) collective-permute-start(bf16[144,256]{1,0:T(8,128)(2,1)S(1)} %get-tuple-element.70), channel_id=1, source_target_pairs={{0,2},{1,3},{2,0},{3,1},{4,6},{5,7},{6,4},{7,5},{8,10},{9,11},{10,... | collective-permute-start | bytes 221192 | tf_op jit(solution)/shard_map/ppermute | solution.py:345
  31.0 1.4 %collective-permute-start.12 = (bf16[144,256]{1,0:T(8,128)(2,1)S(1)}, bf16[144,256]{1,0:T(8,128)(2,1)S(1)}, u32[]{:S(2)}, u32[]{:S(2)}) collective-permute-start(bf16[144,256]{1,0:T(8,128)(2,1)S(1)} %get-tuple-element.71), channel_id=1, source_target_pairs={{0,3},{1,2},{2,1},{3,0},{4,7},{5,6},{6,5},{7,4},{8,11},{9,10},{10,... | collective-permute-start | bytes 221192 | tf_op jit(solution)/shard_map/ppermute | solution.py:345
  32.4 0.4 collective-permute-done.10.refs_1_
  32.8 1.0 %collective-permute-done.11.refs_2_ = bf16[144,256]{1,0:T(8,128)(2,1)S(1)} collective-permute-done((bf16[144,256]{1,0:T(8,128)(2,1)S(1)}, bf16[144,256]{1,0:T(8,128)(2,1)S(1)}, u32[]{:S(2)}, u32[]{:S(2)}) %collective-permute-start.11) | collective-permute-done | bytes 73760 | tf_op jit(solution)/shard_map/ppermute | solution.py:345
  33.8 2.4 %collective-permute-done.12.refs_3_ = bf16[144,256]{1,0:T(8,128)(2,1)S(1)} collective-permute-done((bf16[144,256]{1,0:T(8,128)(2,1)S(1)}, bf16[144,256]{1,0:T(8,128)(2,1)S(1)}, u32[]{:S(2)}, u32[]{:S(2)}) %collective-permute-start.12) | collective-permute-done | bytes 73760 | tf_op jit(solution)/shard_map/ppermute | solution.py:345
  36.3 0.9 %collective-permute-start.13 = (bf16[144,256]{1,0:T(8,128)(2,1)S(1)}, bf16[144,256]{1,0:T(8,128)(2,1)S(1)}, u32[]{:S(2)}, u32[]{:S(2)}) collective-permute-start(bf16[144,256]{1,0:T(8,128)(2,1)S(1)} %add.2.refs_0_), channel_id=1, source_target_pairs={{0,8},{4,12},{8,0},{12,4},{16,24},{20,28},{24,16},{28,20},{1,9},{5... | collective-permute-start | bytes 221192 | tf_op jit(solution)/shard_map/ppermute | solution.py:353
  37.2 1.9 %collective-permute-start.7 = (bf16[2,128,256]{2,1,0:T(8,128)(2,1)S(1)}, bf16[2,128,256]{2,1,0:T(8,128)(2,1)S(1)}, u32[]{:S(2)}, u32[]{:S(2)}) collective-permute-start(bf16[2,128,256]{2,1,0:T(8,128)(2,1)S(1)} %get-tuple-element.65), channel_id=1, source_target_pairs={{0,1},{1,0},{2,3},{3,2},{4,5},{5,4},{6,7},{7,6},{8,9},{9,8},{10,11... | collective-permute-start | bytes 393224 | tf_op jit(solution)/shard_map/ppermute | solution.py:345
  39.2 2.6 %collective-permute-start.14 = (bf16[144,256]{1,0:T(8,128)(2,1)S(1)}, bf16[144,256]{1,0:T(8,128)(2,1)S(1)}, u32[]{:S(2)}, u32[]{:S(2)}) collective-permute-start(bf16[144,256]{1,0:T(8,128)(2,1)S(1)} %add.2.refs_0_), channel_id=1, source_target_pairs={{0,16},{4,20},{8,24},{12,28},{16,0},{20,4},{24,8},{28,12},{1,17},{... | collective-permute-start | bytes 221192 | tf_op jit(solution)/shard_map/ppermute | solution.py:353
  41.8 1.0 %collective-permute-start.15 = (bf16[144,256]{1,0:T(8,128)(2,1)S(1)}, bf16[144,256]{1,0:T(8,128)(2,1)S(1)}, u32[]{:S(2)}, u32[]{:S(2)}) collective-permute-start(bf16[144,256]{1,0:T(8,128)(2,1)S(1)} %add.2.refs_0_), channel_id=1, source_target_pairs={{0,24},{4,28},{8,16},{12,20},{16,8},{20,12},{24,0},{28,4},{1,25},{... | collective-permute-start | bytes 221192 | tf_op jit(solution)/shard_map/ppermute | solution.py:353
  42.8 0.5 collective-permute-start.8
  43.3 0.0 collective-permute-done.13.refs_1_
  43.3 1.1 %collective-permute-start.9 = (bf16[2,128,256]{2,1,0:T(8,128)(2,1)S(1)}, bf16[2,128,256]{2,1,0:T(8,128)(2,1)S(1)}, u32[]{:S(2)}, u32[]{:S(2)}) collective-permute-start(bf16[2,128,256]{2,1,0:T(8,128)(2,1)S(1)} %get-tuple-element.67), channel_id=1, source_target_pairs={{0,3},{1,2},{2,1},{3,0},{4,7},{5,6},{6,5},{7,4},{8,11},{9,10},{10,... | collective-permute-start | bytes 393224 | tf_op jit(solution)/shard_map/ppermute | solution.py:345
  44.4 1.6 %collective-permute-done.14.refs_2_ = bf16[144,256]{1,0:T(8,128)(2,1)S(1)} collective-permute-done((bf16[144,256]{1,0:T(8,128)(2,1)S(1)}, bf16[144,256]{1,0:T(8,128)(2,1)S(1)}, u32[]{:S(2)}, u32[]{:S(2)}) %collective-permute-start.14) | collective-permute-done | bytes 73760 | tf_op jit(solution)/shard_map/ppermute | solution.py:353
  46.0 1.9 %collective-permute-done.15.refs_3_ = bf16[144,256]{1,0:T(8,128)(2,1)S(1)} collective-permute-done((bf16[144,256]{1,0:T(8,128)(2,1)S(1)}, bf16[144,256]{1,0:T(8,128)(2,1)S(1)}, u32[]{:S(2)}, u32[]{:S(2)}) %collective-permute-start.15) | collective-permute-done | bytes 73760 | tf_op jit(solution)/shard_map/ppermute | solution.py:353
  48.0 0.2 collective-permute-start.16
  48.2 1.2 %collective-permute-start.17 = (bf16[144,256]{1,0:T(8,128)(2,1)S(1)}, bf16[144,256]{1,0:T(8,128)(2,1)S(1)}, u32[]{:S(2)}, u32[]{:S(2)}) collective-permute-start(bf16[144,256]{1,0:T(8,128)(2,1)S(1)} %add.3.own), channel_id=1, source_target_pairs={{0,2},{1,3},{2,0},{3,1},{4,6},{5,7},{6,4},{7,5},{8,10},{9,11},{10,... | collective-permute-start | bytes 221192 | tf_op jit(solution)/shard_map/ppermute | solution.py:345
  49.4 0.0 collective-permute-done.7.refs_0_
  49.4 2.1 %collective-permute-start.18 = (bf16[144,256]{1,0:T(8,128)(2,1)S(1)}, bf16[144,256]{1,0:T(8,128)(2,1)S(1)}, u32[]{:S(2)}, u32[]{:S(2)}) collective-permute-start(bf16[144,256]{1,0:T(8,128)(2,1)S(1)} %add.3.own), channel_id=1, source_target_pairs={{0,3},{1,2},{2,1},{3,0},{4,7},{5,6},{6,5},{7,4},{8,11},{9,10},{10,... | collective-permute-start | bytes 221192 | tf_op jit(solution)/shard_map/ppermute | solution.py:345
  51.5 0.0 collective-permute-done.8.refs_1_
  51.5 0.0 collective-permute-done.9.refs_2_
  51.5 1.5 %aux.1 = (bf16[8,128,256]{2,1,0:T(8,128)(2,1)}, f32[8,128]{1,0:T(8,128)S(1)}) custom-call(s32[2,4]{1,0:T(2,128)S(1)} %bitcast.35, bf16[2,128,256]{2,1,0:T(8,128)(2,1)S(1)} %collective-permute-done.7.refs_0_, bf16[2,128,256]{2,1,0:T(8,128)(2,1)S(1)} %collective-permute-done.8.refs_1_, bf16[2,128,256]{2,1,0:T(8,128)(2,1)S(1)} %collective-permute-done.9.refs_2_), custom_call_target="tpu_custom_call" | custom-call | flops 1000000 | bytes 1000000 | tf_op jit(solution)/shard_map/aux/pallas_call | solution.py:500
  53.0 0.0 collective-permute-done.16.refs_0_
  53.0 0.0 collective-permute-done.17.refs_1_
  53.0 1.6 %collective-permute-done.18.refs_2_ = bf16[144,256]{1,0:T(8,128)(2,1)S(1)} collective-permute-done((bf16[144,256]{1,0:T(8,128)(2,1)S(1)}, bf16[144,256]{1,0:T(8,128)(2,1)S(1)}, u32[]{:S(2)}, u32[]{:S(2)}) %collective-permute-start.18) | collective-permute-done | bytes 73760 | tf_op jit(solution)/shard_map/ppermute | solution.py:345
  54.7 0.1 collective-permute-start.19
  54.7 1.6 %collective-permute-done.19.other = bf16[576,256]{1,0:T(8,128)(2,1)S(1)} collective-permute-done((bf16[576,256]{1,0:T(8,128)(2,1)S(1)}, bf16[576,256]{1,0:T(8,128)(2,1)S(1)}, u32[]{:S(2)}, u32[]{:S(2)}) %collective-permute-start.19) | collective-permute-done | bytes 294944 | tf_op jit(solution)/shard_map/ppermute | solution.py:356
  56.3 1.0 %finish.1 = (f32[256,256]{1,0:T(8,128)}, f32[256,256]{1,0:T(8,128)}, f32[256,256]{1,0:T(8,128)}, f32[256,256]{1,0:T(8,128)}, f32[32,256]{1,0:T(8,128)}, /*index=5*/f32[1,1]{1,0:T(1,128)}) custom-call(bf16[576,256]{1,0:T(8,128)(2,1)S(1)} %bitcast.22, bf16[576,256]{1,0:T(8,128)(2,1)S(1)} %collective-permute-done.19.other), custom_call_target="tpu_custom_call" | custom-call | tf_op jit(solution)/shard_map/finish/pallas_call | solution.py:525
  (13 shorter events, 0.2 us)
Async XLA Ops:
  0.6 0.7 %copy-start.11 = (s32[1,1,4,2]{2,3,1,0:T(2,128)S(1)}, s32[1,1,4,2]{2,3,1,0:T(2,128)}, u32[]{:S(2)}) copy-start(s32[1,1,4,2]{2,3,1,0:T(2,128)} %param.18) | copy-start | bytes 100
  1.3 1.0 %copy-start.1 = (bf16[1,1,1024,256]{3,2,1,0:T(8,128)(2,1)S(1)}, bf16[1,1,1024,256]{3,2,1,0:T(8,128)(2,1)}, u32[]{:S(2)}) copy-start(bf16[1,1,1024,256]{3,2,1,0:T(8,128)(2,1)} %param.14) | copy-start | bytes 1572868
  2.4 1.0 %copy-start.2 = (bf16[1,1,1024,256]{3,2,1,0:T(8,128)(2,1)S(1)}, bf16[1,1,1024,256]{3,2,1,0:T(8,128)(2,1)}, u32[]{:S(2)}) copy-start(bf16[1,1,1024,256]{3,2,1,0:T(8,128)(2,1)} %param.13) | copy-start | bytes 1572868
  3.4 11.0 %copy-start.12 = (bf16[1,1,8,4,128,128]{5,4,3,2,1,0:T(8,128)(2,1)S(1)}, bf16[1,1,8,4,128,128]{5,4,3,2,1,0:T(8,128)(2,1)}, u32[]{:S(2)}) copy-start(bf16[1,1,8,4,128,128]{5,4,3,2,1,0:T(8,128)(2,1)} %param.16) | copy-start | bytes 3145732
  4.1 8.0 %collective-permute-start = (bf16[2,128,256]{2,1,0:T(8,128)(2,1)S(1)}, bf16[2,128,256]{2,1,0:T(8,128)(2,1)S(1)}, u32[]{:S(2)}, u32[]{:S(2)}) collective-permute-start(bf16[2,128,256]{2,1,0:T(8,128)(2,1)S(1)} %get-tuple-element.47), channel_id=1, source_target_pairs={{0,1},{1,0},{2,3},{3,2},{4,5},{5,4},{6,7},{7,6},{8,9},{9,8},{10,11... | collective-permute-start | bytes 393224 | tf_op jit(solution)/shard_map/ppermute | solution.py:345
  7.1 9.7 %collective-permute-start.1 = (bf16[2,128,256]{2,1,0:T(8,128)(2,1)S(1)}, bf16[2,128,256]{2,1,0:T(8,128)(2,1)S(1)}, u32[]{:S(2)}, u32[]{:S(2)}) collective-permute-start(bf16[2,128,256]{2,1,0:T(8,128)(2,1)S(1)} %get-tuple-element.48), channel_id=1, source_target_pairs={{0,2},{1,3},{2,0},{3,1},{4,6},{5,7},{6,4},{7,5},{8,10},{9,11},{10,... | collective-permute-start | bytes 393224 | tf_op jit(solution)/shard_map/ppermute | solution.py:345
  8.6 8.2 %collective-permute-start.2 = (bf16[2,128,256]{2,1,0:T(8,128)(2,1)S(1)}, bf16[2,128,256]{2,1,0:T(8,128)(2,1)S(1)}, u32[]{:S(2)}, u32[]{:S(2)}) collective-permute-start(bf16[2,128,256]{2,1,0:T(8,128)(2,1)S(1)} %get-tuple-element.49), channel_id=1, source_target_pairs={{0,3},{1,2},{2,1},{3,0},{4,7},{5,6},{6,5},{7,4},{8,11},{9,10},{10,... | collective-permute-start | bytes 393224 | tf_op jit(solution)/shard_map/ppermute | solution.py:345
  8.6 11.5 %collective-permute-start.3 = (bf16[2,128,256]{2,1,0:T(8,128)(2,1)S(1)}, bf16[2,128,256]{2,1,0:T(8,128)(2,1)S(1)}, u32[]{:S(2)}, u32[]{:S(2)}) collective-permute-start(bf16[2,128,256]{2,1,0:T(8,128)(2,1)S(1)} %get-tuple-element.57), channel_id=1, source_target_pairs={{0,1},{1,0},{2,3},{3,2},{4,5},{5,4},{6,7},{7,6},{8,9},{9,8},{10,11... | collective-permute-start | bytes 393224 | tf_op jit(solution)/shard_map/ppermute | solution.py:345
  10.5 9.9 %collective-permute-start.4 = (bf16[2,128,256]{2,1,0:T(8,128)(2,1)S(1)}, bf16[2,128,256]{2,1,0:T(8,128)(2,1)S(1)}, u32[]{:S(2)}, u32[]{:S(2)}) collective-permute-start(bf16[2,128,256]{2,1,0:T(8,128)(2,1)S(1)} %get-tuple-element.58), channel_id=1, source_target_pairs={{0,2},{1,3},{2,0},{3,1},{4,6},{5,7},{6,4},{7,5},{8,10},{9,11},{10,... | collective-permute-start | bytes 393224 | tf_op jit(solution)/shard_map/ppermute | solution.py:345
  12.1 8.4 %collective-permute-start.5 = (bf16[2,128,256]{2,1,0:T(8,128)(2,1)S(1)}, bf16[2,128,256]{2,1,0:T(8,128)(2,1)S(1)}, u32[]{:S(2)}, u32[]{:S(2)}) collective-permute-start(bf16[2,128,256]{2,1,0:T(8,128)(2,1)S(1)} %get-tuple-element.59), channel_id=1, source_target_pairs={{0,3},{1,2},{2,1},{3,0},{4,7},{5,6},{6,5},{7,4},{8,11},{9,10},{10,... | collective-permute-start | bytes 393224 | tf_op jit(solution)/shard_map/ppermute | solution.py:345
  14.4 2.4 %copy-start.3 = (bf16[256,256]{1,0:T(8,128)(2,1)S(1)}, bf16[256,256]{1,0:T(8,128)(2,1)}, u32[]{:S(2)}) copy-start(bf16[256,256]{1,0:T(8,128)(2,1)} %wn_in.1) | copy-start | bytes 393220
  14.4 2.4 %copy-start.4 = (bf16[256,256]{1,0:T(8,128)(2,1)S(1)}, bf16[256,256]{1,0:T(8,128)(2,1)}, u32[]{:S(2)}) copy-start(bf16[256,256]{1,0:T(8,128)(2,1)} %ws_in.1) | copy-start | bytes 393220
  16.8 0.7 %copy-start.8 = (s32[1,1,8,4]{2,3,1,0:T(4,128)S(1)}, s32[1,1,8,4]{2,3,1,0:T(4,128)}, u32[]{:S(2)}) copy-start(s32[1,1,8,4]{2,3,1,0:T(4,128)} %param.17) | copy-start | bytes 388
  17.5 3.0 %copy-start = (bf16[1,1,1024,256]{3,2,1,0:T(8,128)(2,1)S(1)}, bf16[1,1,1024,256]{3,2,1,0:T(8,128)(2,1)}, u32[]{:S(2)}) copy-start(bf16[1,1,1024,256]{3,2,1,0:T(8,128)(2,1)} %param.15) | copy-start | bytes 1572868
  17.5 3.0 %copy-start.5 = (bf16[256,256]{1,0:T(8,128)(2,1)S(1)}, bf16[256,256]{1,0:T(8,128)(2,1)}, u32[]{:S(2)}) copy-start(bf16[256,256]{1,0:T(8,128)(2,1)} %refs_1_.1) | copy-start | bytes 393220
  17.5 3.0 %copy-start.6 = (bf16[256,256]{1,0:T(8,128)(2,1)S(1)}, bf16[256,256]{1,0:T(8,128)(2,1)}, u32[]{:S(2)}) copy-start(bf16[256,256]{1,0:T(8,128)(2,1)} %refs_2_.1) | copy-start | bytes 393220
  17.5 3.0 %copy-start.9 = (s32[1,1,1024]{2,1,0:T(1,128)S(1)}, s32[1,1,1024]{2,1,0:T(1,128)}, u32[]{:S(2)}) copy-start(s32[1,1,1024]{2,1,0:T(1,128)} %param.19) | copy-start | bytes 12292
  17.5 3.0 %copy-start.10 = (s32[1,1,1024]{2,1,0:T(1,128)S(1)}, s32[1,1,1024]{2,1,0:T(1,128)}, u32[]{:S(2)}) copy-start(s32[1,1,1024]{2,1,0:T(1,128)} %param.20) | copy-start | bytes 12292
  20.1 0.7 %copy-start.7 = (bf16[256,32]{0,1:T(8,128)(2,1)S(1)}, bf16[256,32]{0,1:T(8,128)(2,1)}, u32[]{:S(2)}) copy-start(bf16[256,32]{0,1:T(8,128)(2,1)} %param.25) | copy-start | bytes 49156
  26.7 1.6 %collective-permute-start.6 = (bf16[576,256]{1,0:T(8,128)(2,1)S(1)}, bf16[576,256]{1,0:T(8,128)(2,1)S(1)}, u32[]{:S(2)}, u32[]{:S(2)}) collective-permute-start(bf16[576,256]{1,0:T(8,128)(2,1)S(1)} %get-tuple-element.63), channel_id=1, source_target_pairs={{0,4},{4,0},{8,12},{12,8},{16,20},{20,16},{24,28},{28,24},{1,5},{5... | collective-permute-start | bytes 884744 | tf_op jit(solution)/shard_map/ppermute | solution.py:356
  28.4 4.4 %collective-permute-start.10 = (bf16[144,256]{1,0:T(8,128)(2,1)S(1)}, bf16[144,256]{1,0:T(8,128)(2,1)S(1)}, u32[]{:S(2)}, u32[]{:S(2)}) collective-permute-start(bf16[144,256]{1,0:T(8,128)(2,1)S(1)} %get-tuple-element.69), channel_id=1, source_target_pairs={{0,1},{1,0},{2,3},{3,2},{4,5},{5,4},{6,7},{7,6},{8,9},{9,8},{10,11... | collective-permute-start | bytes 221192 | tf_op jit(solution)/shard_map/ppermute | solution.py:345
  29.4 4.4 %collective-permute-start.11 = (bf16[144,256]{1,0:T(8,128)(2,1)S(1)}, bf16[144,256]{1,0:T(8,128)(2,1)S(1)}, u32[]{:S(2)}, u32[]{:S(2)}) collective-permute-start(bf16[144,256]{1,0:T(8,128)(2,1)S(1)} %get-tuple-element.70), channel_id=1, source_target_pairs={{0,2},{1,3},{2,0},{3,1},{4,6},{5,7},{6,4},{7,5},{8,10},{9,11},{10,... | collective-permute-start | bytes 221192 | tf_op jit(solution)/shard_map/ppermute | solution.py:345
  31.0 5.3 %collective-permute-start.12 = (bf16[144,256]{1,0:T(8,128)(2,1)S(1)}, bf16[144,256]{1,0:T(8,128)(2,1)S(1)}, u32[]{:S(2)}, u32[]{:S(2)}) collective-permute-start(bf16[144,256]{1,0:T(8,128)(2,1)S(1)} %get-tuple-element.71), channel_id=1, source_target_pairs={{0,3},{1,2},{2,1},{3,0},{4,7},{5,6},{6,5},{7,4},{8,11},{9,10},{10,... | collective-permute-start | bytes 221192 | tf_op jit(solution)/shard_map/ppermute | solution.py:345
  36.3 6.9 %collective-permute-start.13 = (bf16[144,256]{1,0:T(8,128)(2,1)S(1)}, bf16[144,256]{1,0:T(8,128)(2,1)S(1)}, u32[]{:S(2)}, u32[]{:S(2)}) collective-permute-start(bf16[144,256]{1,0:T(8,128)(2,1)S(1)} %add.2.refs_0_), channel_id=1, source_target_pairs={{0,8},{4,12},{8,0},{12,4},{16,24},{20,28},{24,16},{28,20},{1,9},{5... | collective-permute-start | bytes 221192 | tf_op jit(solution)/shard_map/ppermute | solution.py:353
  37.2 12.1 %collective-permute-start.7 = (bf16[2,128,256]{2,1,0:T(8,128)(2,1)S(1)}, bf16[2,128,256]{2,1,0:T(8,128)(2,1)S(1)}, u32[]{:S(2)}, u32[]{:S(2)}) collective-permute-start(bf16[2,128,256]{2,1,0:T(8,128)(2,1)S(1)} %get-tuple-element.65), channel_id=1, source_target_pairs={{0,1},{1,0},{2,3},{3,2},{4,5},{5,4},{6,7},{7,6},{8,9},{9,8},{10,11... | collective-permute-start | bytes 393224 | tf_op jit(solution)/shard_map/ppermute | solution.py:345
  39.2 6.8 %collective-permute-start.14 = (bf16[144,256]{1,0:T(8,128)(2,1)S(1)}, bf16[144,256]{1,0:T(8,128)(2,1)S(1)}, u32[]{:S(2)}, u32[]{:S(2)}) collective-permute-start(bf16[144,256]{1,0:T(8,128)(2,1)S(1)} %add.2.refs_0_), channel_id=1, source_target_pairs={{0,16},{4,20},{8,24},{12,28},{16,0},{20,4},{24,8},{28,12},{1,17},{... | collective-permute-start | bytes 221192 | tf_op jit(solution)/shard_map/ppermute | solution.py:353
  41.8 6.2 %collective-permute-start.15 = (bf16[144,256]{1,0:T(8,128)(2,1)S(1)}, bf16[144,256]{1,0:T(8,128)(2,1)S(1)}, u32[]{:S(2)}, u32[]{:S(2)}) collective-permute-start(bf16[144,256]{1,0:T(8,128)(2,1)S(1)} %add.2.refs_0_), channel_id=1, source_target_pairs={{0,24},{4,28},{8,16},{12,20},{16,8},{20,12},{24,0},{28,4},{1,25},{... | collective-permute-start | bytes 221192 | tf_op jit(solution)/shard_map/ppermute | solution.py:353
  42.8 8.7 %collective-permute-start.8 = (bf16[2,128,256]{2,1,0:T(8,128)(2,1)S(1)}, bf16[2,128,256]{2,1,0:T(8,128)(2,1)S(1)}, u32[]{:S(2)}, u32[]{:S(2)}) collective-permute-start(bf16[2,128,256]{2,1,0:T(8,128)(2,1)S(1)} %get-tuple-element.66), channel_id=1, source_target_pairs={{0,2},{1,3},{2,0},{3,1},{4,6},{5,7},{6,4},{7,5},{8,10},{9,11},{10,... | collective-permute-start | bytes 393224 | tf_op jit(solution)/shard_map/ppermute | solution.py:345
  43.3 8.2 %collective-permute-start.9 = (bf16[2,128,256]{2,1,0:T(8,128)(2,1)S(1)}, bf16[2,128,256]{2,1,0:T(8,128)(2,1)S(1)}, u32[]{:S(2)}, u32[]{:S(2)}) collective-permute-start(bf16[2,128,256]{2,1,0:T(8,128)(2,1)S(1)} %get-tuple-element.67), channel_id=1, source_target_pairs={{0,3},{1,2},{2,1},{3,0},{4,7},{5,6},{6,5},{7,4},{8,11},{9,10},{10,... | collective-permute-start | bytes 393224 | tf_op jit(solution)/shard_map/ppermute | solution.py:345
  48.0 5.1 %collective-permute-start.16 = (bf16[144,256]{1,0:T(8,128)(2,1)S(1)}, bf16[144,256]{1,0:T(8,128)(2,1)S(1)}, u32[]{:S(2)}, u32[]{:S(2)}) collective-permute-start(bf16[144,256]{1,0:T(8,128)(2,1)S(1)} %add.3.own), channel_id=1, source_target_pairs={{0,1},{1,0},{2,3},{3,2},{4,5},{5,4},{6,7},{7,6},{8,9},{9,8},{10,11... | collective-permute-start | bytes 221192 | tf_op jit(solution)/shard_map/ppermute | solution.py:345
  48.2 4.8 %collective-permute-start.17 = (bf16[144,256]{1,0:T(8,128)(2,1)S(1)}, bf16[144,256]{1,0:T(8,128)(2,1)S(1)}, u32[]{:S(2)}, u32[]{:S(2)}) collective-permute-start(bf16[144,256]{1,0:T(8,128)(2,1)S(1)} %add.3.own), channel_id=1, source_target_pairs={{0,2},{1,3},{2,0},{3,1},{4,6},{5,7},{6,4},{7,5},{8,10},{9,11},{10,... | collective-permute-start | bytes 221192 | tf_op jit(solution)/shard_map/ppermute | solution.py:345
  49.4 5.3 %collective-permute-start.18 = (bf16[144,256]{1,0:T(8,128)(2,1)S(1)}, bf16[144,256]{1,0:T(8,128)(2,1)S(1)}, u32[]{:S(2)}, u32[]{:S(2)}) collective-permute-start(bf16[144,256]{1,0:T(8,128)(2,1)S(1)} %add.3.own), channel_id=1, source_target_pairs={{0,3},{1,2},{2,1},{3,0},{4,7},{5,6},{6,5},{7,4},{8,11},{9,10},{10,... | collective-permute-start | bytes 221192 | tf_op jit(solution)/shard_map/ppermute | solution.py:345
  54.7 1.6 %collective-permute-start.19 = (bf16[576,256]{1,0:T(8,128)(2,1)S(1)}, bf16[576,256]{1,0:T(8,128)(2,1)S(1)}, u32[]{:S(2)}, u32[]{:S(2)}) collective-permute-start(bf16[576,256]{1,0:T(8,128)(2,1)S(1)} %bitcast.21), channel_id=1, source_target_pairs={{0,4},{4,0},{8,12},{12,8},{16,20},{20,16},{24,28},{28,24},{1,5},{5... | collective-permute-start | bytes 884744 | tf_op jit(solution)/shard_map/ppermute | solution.py:356

commit v3 on v2

--- a/solution.py
+++ b/solution.py
@@ -13,7 +13,7 @@
 SMEM = pl.BlockSpec(memory_space=pltpu.SMEM)
 HBM = pl.BlockSpec(memory_space=pltpu.HBM)
 CORES = 2
-PACK_LIMIT = 40 << 20
+PACK_LIMIT = 53 << 20
 PREP_LIMIT = 4 << 20
 AUX_FLOPS = 10**6
 
@@ -54,19 +54,13 @@
                 outs[which * (peers - 1) + step - 1][s] = values[block]
 
 
-def prepare_kernel(dims, feat_in, tiles_in, token, tiles, tiles_t, feat, feat_t, sems):
-    blocks, picks, rows = dims
-    whole = pltpu.make_async_copy(feat_in, feat, sems.at[0])
-    copies = [
-        pltpu.make_async_copy(tiles_in.at[b], tiles.at[b], sems.at[1 + b]) for b in range(blocks)
-    ]
-    for copy in [whole] + copies:
-        copy.start()
-    whole.wait()
+def prepare_kernel(dims, feat, tiles, wn, ws, token, tiles_t, feat_t, w_t):
+    blocks, picks, rows, width = dims
+    w_t[:, :width] = wn[...].T
+    w_t[:, width:] = ws[...].T
     for b in range(blocks):
         feat_t[:, b * rows : (b + 1) * rows] = feat[b].T
     for b in range(blocks):
-        copies[b].wait()
         for k in range(picks):
             tiles_t[b, k * rows : (k + 1) * rows] = tiles[b, k].T
 
@@ -81,20 +75,14 @@
     return value, gate + value * (1.0 - gate)
 
 
-def first_kernel(dims, sources_in, wn_in, ws_in, feat, tiles, *refs):
+def first_kernel(dims, sources_in, wn, ws, feat, tiles, *refs):
     peers, slots, blocks, picks, rows, width = dims
     inc = peers - 1
     feat_in, refs = refs[:inc], refs[inc:]
-    (hidden_out, own2, slope1, agg_t, hidden_t), refs = refs[:5], refs[5:]
-    table, sources, wn, ws, sems, out_sem = refs
-    g = lax.axis_index("grp")
-    listed = pltpu.make_async_copy(sources_in, sources, sems.at[0])
-    weights = [
-        pltpu.make_async_copy(wn_in, wn, sems.at[1]),
-        pltpu.make_async_copy(ws_in, ws, sems.at[2]),
-    ]
-    for copy in [listed] + weights:
-        copy.start()
+    own2, slope1, agg_t, hidden_t, table, sources, sem = refs
+    g = lax.axis_index("grp")
+    listed = pltpu.make_async_copy(sources_in, sources, sem)
+    listed.start()
     table[pl.ds(0, blocks)] = feat[...]
     for step in range(1, peers):
         _, origin = partner(g, step, peers)
@@ -106,8 +94,6 @@
         agg = dot(row, gathered(table, sources, b, picks)).astype(BF16)
         aggs.append(agg)
         agg_t[:, b * rows : (b + 1) * rows] = agg.T
-    for copy in weights:
-        copy.wait()
     both_w = jnp.concatenate([wn[...], ws[...]], axis=0)
     pair = 2
     span = pair * rows
@@ -122,91 +108,82 @@
         hidden = value.astype(BF16)
         own2[pl.ds(i * pair, pair)] = hidden.reshape(pair, rows, width)
         hidden_t[:, at] = hidden.T
-    out = pltpu.make_async_copy(own2, hidden_out, out_sem)
-    out.start()
-    out.wait()
-
-
-def second_kernel(dims, *refs):
+
+
+def second_kernel(dims, sources_in, *refs):
     peers, slots, blocks, picks, rows, width, bins_count, pay_rows = dims
     inc = peers - 1
-    hbm_in, refs = refs[:7], refs[7:]
+    (wn, ws, w_t, head, bins, flags, aux), refs = refs[:7], refs[7:]
     (own2, slope1, tiles, tiles_t, agg1_t, feat_t, hidden_t), refs = refs[:7], refs[7:]
     past_in, refs = refs[:inc], refs[inc:]
-    (grad_hidden_out, keep, send, back), refs = refs[:4], refs[4:]
-    loaded, refs = refs[:7], refs[7:]
-    table, agg_t, gtab, grad_hidden, pay, sems, out_sem = refs
-    sources, wn, ws, hw, bins, flags, aux = loaded
+    (grad_hidden, keep, send, back), refs = refs[:4], refs[4:]
+    sources, table, agg_t, gtab, pay, sem = refs
     g = lax.axis_index("grp")
     core = lax.axis_index("clus") % CORES
     device = lax.axis_index("clus") * peers + g
     nodes = blocks * rows
     scale = 1.0 / (nodes * peers)
-    loads = [
-        pltpu.make_async_copy(src, dst, sems.at[i])
-        for i, (src, dst) in enumerate(zip(hbm_in, loaded))
-    ]
-    for load in loads:
-        load.start()
+    listed = pltpu.make_async_copy(sources_in, sources, sem)
+    listed.start()
     table[pl.ds(0, blocks)] = own2[...]
     for step in range(1, peers):
         _, origin = partner(g, step, peers)
         table[pl.ds(blocks + origin * slots, slots)] = past_in[step - 1][...]
-    back[...] = jnp.zeros(back.shape, F32)
-    loads[0].wait()
+    remote = pl.ds(blocks, peers * slots)
+    gtab[remote] = jnp.zeros((peers * slots, rows, width), F32)
+    listed.wait()
     aggs = []
     for b in range(blocks):
         row = jnp.concatenate([tiles[b, k] for k in range(picks)], axis=1)
         agg = dot(row, gathered(table, sources, b, picks)).astype(BF16)
         aggs.append(agg)
         agg_t[:, b * rows : (b + 1) * rows] = agg.T
-    for load in loads[1:]:
-        load.wait()
     pair = 2
     span = pair * rows
-    head = hw[...]
     step_col = lax.broadcasted_iota(jnp.int32, (bins_count, span), 0)
     both_w = jnp.concatenate([wn[...], ws[...]], axis=0)
     loss = jnp.zeros((bins_count, span), F32)
     ghw = jnp.zeros((bins_count, width), F32)
-    grad_pres, grad_aggs = [], []
-    for i in range(blocks // pair):
-        at = pl.ds(i * pair, pair)
+    chunks = range(blocks // pair)
+    at = [pl.ds(i * pair, pair) for i in chunks]
+    gates = []
+    for i in chunks:
         both = jnp.concatenate(
             [
                 jnp.concatenate(aggs[i * pair : (i + 1) * pair], axis=0),
-                table[at].reshape(span, width),
+                table[at[i]].reshape(span, width),
             ],
             axis=1,
         )
-        value, slope = gate_of(dot(both, both_w))
-        hidden = value.astype(BF16)
-        logits = dot_by_transpose(head, hidden)
+        gates.append(gate_of(dot(both, both_w)))
+    hidden = [value.astype(BF16) for value, _ in gates]
+    logits = [dot_by_transpose(head[...], hidden[i]) for i in chunks]
+    glogs = []
+    for i in chunks:
         counted = step_col <= bins[i]
         event = jnp.where(step_col == bins[i], flags[i].astype(F32), 0.0)
-        tail = jnp.exp(-jnp.abs(logits))
-        soft = jnp.maximum(logits, 0.0) + jnp.log1p(tail)
-        loss = loss + jnp.where(counted, soft, 0.0) - event * logits
-        chance = jnp.where(logits >= 0.0, 1.0, tail) / (1.0 + tail)
-        glog = (jnp.where(counted, chance, 0.0) - event).astype(BF16)
-        ghw = ghw + dot(glog, hidden)
-        grad_pre = (transpose_dot(glog, head) * slope).astype(BF16)
-        grad_pres.append(grad_pre)
-        grad_aggs.append(dot_by_transpose(grad_pre, wn[...]).astype(BF16))
-        own = dot_by_transpose(grad_pre, ws[...]) + aux[at].reshape(span, width).astype(F32)
-        gtab[at] = own.reshape(pair, rows, width)
-    remote = pl.ds(blocks, peers * slots)
-    gtab[remote] = jnp.zeros((peers * slots, rows, width), F32)
+        tail = jnp.exp(-jnp.abs(logits[i]))
+        soft = jnp.maximum(logits[i], 0.0) + jnp.log1p(tail)
+        loss = loss + jnp.where(counted, soft, 0.0) - event * logits[i]
+        chance = jnp.where(logits[i] >= 0.0, 1.0, tail) / (1.0 + tail)
+        glogs.append((jnp.where(counted, chance, 0.0) - event).astype(BF16))
+    grad_pres = [(transpose_dot(glogs[i], head[...]) * gates[i][1]).astype(BF16) for i in chunks]
+    grad_aggs = []
+    for i in chunks:
+        onward = dot(grad_pres[i], w_t[...])
+        grad_aggs.append(onward[:, :width].astype(BF16))
+        own = onward[:, width:] + aux[at[i]].reshape(span, width).astype(F32)
+        gtab[at[i]] = own.reshape(pair, rows, width)
+    for i in chunks:
+        ghw = ghw + dot(glogs[i], hidden[i])
     for b in range(blocks):
         part = grad_aggs[b // pair][(b % pair) * rows : (b % pair + 1) * rows]
         spread = dot(tiles_t[b], part)
         for k in range(picks):
             gtab[sources[k, b]] += spread[k * rows : (k + 1) * rows]
-    back[...] = gtab[remote]
+    back[...] = gtab[remote].astype(BF16)
     total = gtab[pl.ds(0, blocks)]
     grad_hidden[...] = total.astype(BF16)
-    out = pltpu.make_async_copy(grad_hidden, grad_hidden_out, out_sem)
-    out.start()
     grad_first = (total.reshape(nodes, width) * slope1[...]).astype(BF16)
     grad_second = jnp.concatenate(grad_pres, axis=0)
     terms = (
@@ -231,7 +208,6 @@
     half = pay_rows // CORES
     keep[...] = pay[pl.ds(pl.multiple_of(core * half, 16), half)]
     send[...] = pay[pl.ds(pl.multiple_of((1 - core) * half, 16), half)]
-    out.wait()
 
 
 def split_kernel(peers, kept, came, own, *outs):
@@ -244,6 +220,18 @@
     for step in range(1, peers):
         peer, _ = partner(g, step, peers)
         outs[step - 1][...] = chunk(peer)
+
+
+def store_kernel(hidden, grad_hidden, after, hidden_out, grad_hidden_out, token, sems):
+    copies = [
+        pltpu.make_async_copy(hidden, hidden_out, sems.at[0]),
+        pltpu.make_async_copy(grad_hidden, grad_hidden_out, sems.at[1]),
+    ]
+    for copy in copies:
+        copy.start()
+    token[...] = jnp.zeros_like(token)
+    for copy in copies:
+        copy.wait()
 
 
 def add_kernel(*refs):
@@ -281,7 +269,7 @@
     g = lax.axis_index("grp")
     for step in range(1, peers):
         _, origin = partner(g, step, peers)
-        outs[step - 1][...] = back[pl.ds(origin * slots, slots)].astype(BF16)
+        outs[step - 1][...] = back[pl.ds(origin * slots, slots)]
 
 
 def aux_kernel(peers, slots, blocks, send, *refs):
@@ -378,47 +366,35 @@
     )(routing, feat, past)
     feat_in = [over_grp(packed[i], i + 1) for i in range(inc)]
     past_in = [over_grp(packed[inc + i], i + 1) for i in range(inc)]
-    tiles, tiles_t, feat, feat_t = pl.pallas_call(
-        functools.partial(prepare_kernel, (blocks, picks, rows)),
+    tiles_t, feat_t, w_t = pl.pallas_call(
+        functools.partial(prepare_kernel, (blocks, picks, rows, width)),
         out_shape=[
-            shape(tiles.shape),
             shape((blocks, picks * rows, rows)),
-            shape(block_shape),
             shape(turned),
+            shape((width, 2 * width)),
         ],
-        in_specs=[HBM] * 2 + [VMEM],
-        out_specs=[VMEM] * 4,
-        scratch_shapes=[pltpu.SemaphoreType.DMA((1 + blocks,))],
+        in_specs=[VMEM] * 5,
+        out_specs=[VMEM] * 3,
         compiler_params=pltpu.CompilerParams(vmem_limit_bytes=PREP_LIMIT),
         cost_estimate=pl.CostEstimate(flops=10**9, bytes_accessed=10**7, transcendentals=0),
         name="prepare",
-    )(feat, tiles, packed[2 * inc])
+    )(feat, tiles, neigh_second, self_second, packed[2 * inc])
 
     pair_shape = (blocks // 2, 1, 2 * rows)
-    first = pl.pallas_call(
+    own2, slope1, agg_t, hidden_t = pl.pallas_call(
         functools.partial(first_kernel, (peers, slots, blocks, picks, rows, width)),
-        out_shape=[
-            shape(block_shape),
-            shape(block_shape),
-            shape((nodes, width), F32),
-            shape(turned),
-            shape(turned),
-        ],
-        in_specs=[HBM] * 3 + [VMEM] * (2 + inc),
-        out_specs=[HBM] + [VMEM] * 4,
+        out_shape=[shape(block_shape), shape((nodes, width), F32), shape(turned), shape(turned)],
+        in_specs=[HBM] + [VMEM] * (4 + inc),
+        out_specs=[VMEM] * 4,
         scratch_shapes=[
             pltpu.VMEM((table, rows, width), BF16),
             pltpu.SMEM((picks, blocks), jnp.int32),
-            pltpu.VMEM(square, BF16),
-            pltpu.VMEM(square, BF16),
-            pltpu.SemaphoreType.DMA((3,)),
             pltpu.SemaphoreType.DMA,
         ],
         compiler_params=params,
         name="first_layer",
     )(sources, neigh_first, self_first, feat, tiles, *feat_in)
-    hidden_first = first[0]
-    grad_hidden, kept, sent, gtab_back = pl.pallas_call(
+    grad_hidden, kept, sent, back = pl.pallas_call(
         functools.partial(
             second_kernel, (peers, slots, blocks, picks, rows, width, bins_count, pay_rows)
         ),
@@ -426,24 +402,16 @@
             shape(block_shape),
             shape((half, width)),
             shape((half, width)),
-            shape((peers * slots, rows, width), F32),
+            shape((peers * slots, rows, width)),
         ],
-        in_specs=[HBM] * 7 + [VMEM] * (7 + inc),
-        out_specs=[HBM] + [VMEM] * 3,
+        in_specs=[HBM] + [VMEM] * (14 + inc),
+        out_specs=[VMEM] * 4,
         scratch_shapes=[
             pltpu.SMEM((picks, blocks), jnp.int32),
-            pltpu.VMEM(square, BF16),
-            pltpu.VMEM(square, BF16),
-            pltpu.VMEM((bins_count, width), BF16),
-            pltpu.VMEM(pair_shape, jnp.int32),
-            pltpu.VMEM(pair_shape, jnp.int32),
-            pltpu.VMEM(block_shape, BF16),
             pltpu.VMEM((table, rows, width), BF16),
             pltpu.VMEM(turned, BF16),
             pltpu.VMEM((table, rows, width), F32),
-            pltpu.VMEM(block_shape, BF16),
             pltpu.VMEM((pay_rows, width), BF16),
-            pltpu.SemaphoreType.DMA((7,)),
             pltpu.SemaphoreType.DMA,
         ],
         compiler_params=params,
@@ -452,17 +420,18 @@
         sources,
         neigh_second,
         self_second,
+        w_t,
         hazard_weight.T,
         event_bins.reshape(pair_shape),
         event_flags.reshape(pair_shape),
         aux_history.reshape(block_shape),
-        first[1],
-        first[2],
+        own2,
+        slope1,
         tiles,
         tiles_t,
-        first[3],
+        agg_t,
         feat_t,
-        first[4],
+        hidden_t,
         *past_in,
     )
 
@@ -487,7 +456,16 @@
             name="add",
         )(*values)
 
-    mine = add(parts[0], *from_grp)
+    hidden_first, grad_hidden, stored = pl.pallas_call(
+        store_kernel,
+        out_shape=[shape(block_shape), shape(block_shape), shape((8, 128), F32)],
+        in_specs=[VMEM] * 3,
+        out_specs=[HBM, HBM, VMEM],
+        scratch_shapes=[pltpu.SemaphoreType.DMA((2,))],
+        compiler_params=small,
+        name="store",
+    )(own2, grad_hidden, parts[0])
+    mine = add(parts[0], *from_grp, stored)
     back = pl.pallas_call(
         functools.partial(back_kernel, peers, slots, blocks),
         out_shape=[shape(slot_shape)] * inc,
@@ -495,7 +473,7 @@
         out_specs=[VMEM] * inc,
         compiler_params=small,
         name="back",
-    )(gtab_back, parts[0])
+    )(back, parts[0])
     came_back = [over_grp(back[i], i + 1) for i in range(inc)]
     new_aux, token = pl.pallas_call(
         functools.partial(aux_kernel, peers, slots, blocks),

time: 57.7 us -> 52.7 us (0.913)
  Pallas kernels: 14.2 us -> 10.9 us
  waiting for transfers between devices: 12.5 us -> 9.83 us
  local copies, waits for them, and re-layouts: 3.79 us -> 4.82 us
    pallas_call x1, Pallas kernels: 5.85 us -> 3.77 us  [shards(): pl.pallas_call(functools.partial(second_kernel, (peers, slots, blocks, pi...]
    ppermute x3, waiting for transfers between devices: 3.53 us -> 2.1 us  [over_z(): return lax.ppermute(value, 'clus', pairs)]
    ppermute x15, waiting for transfers between devices: 5.84 us -> 4.59 us  [over_grp(): return lax.ppermute(value, 'grp', grp_pairs(step))]
    unnamed x26 -> x28, local copies, waits for them, and re-layouts: 3.79 us -> 4.82 us
    pallas_call x1, Pallas kernels: 2.58 us -> 1.65 us  [shards(): pl.pallas_call(functools.partial(first_kernel, (peers, slots, blocks, pic...]
    pallas_call x1 -> x2, Pallas kernels: 2.38 us -> 1.53 us  [the longest x1 0.98 us: shards(): pl.pallas_call(store_kernel, out_shape=[shape(block_shape), shape(block_s...]
    pallas_call x1, Pallas kernels: 0.64 us -> 1.25 us  [shards(): pl.pallas_call(functools.partial(pack_kernel, peers, slots, blocks), out_...]
  transfers between devices with their start and end apart: 20 -> 20, of which waited for: 9 -> 10; matrix products, arithmetic and copies ran while one was open for 0% -> 0% of each run, Pallas kernels for 11% -> 9%
where the time goes in v3:
time: 52.7 us; the launch traced here: 52.4 us
  starting transfers between devices  26 us (49%)
  Pallas kernels  10.9 us (21%)
  waiting for transfers between devices  9.83 us (19%)
  local copies, waits for them, and re-layouts  4.82 us (9%)
  between operations  0.83 us (2%)
    ppermute x15, starting transfers between devices, over_grp(): return lax.ppermute(value, 'grp', grp_pairs(step))  21.4 us
    unnamed x28, local copies, waits for them, and re-layouts  4.82 us
    ppermute x15, waiting for transfers between devices, over_grp(): return lax.ppermute(value, 'grp', grp_pairs(step))  4.59 us
    ppermute x3, starting transfers between devices, over_z(): return lax.ppermute(value, 'clus', pairs)  4.46 us
    pallas_call x1, Pallas kernels, shards(): pl.pallas_call(functools.partial(second_kernel, (peers, slots, blocks, pi...  3.77 us
    ppermute x2, waiting for transfers between devices, over_core(): return lax.ppermute(value, 'clus', [(i, i ^ 1) for i in range(clus_count)])  3.14 us
    ppermute x3, waiting for transfers between devices, over_z(): return lax.ppermute(value, 'clus', pairs)  2.1 us
    pallas_call x1, Pallas kernels, shards(): pl.pallas_call(functools.partial(first_kernel, (peers, slots, blocks, pic...  1.65 us
  transfers between devices with their start and end apart: 20, of which 10 were waited for; matrix products, arithmetic and copies ran while one was open for 0% of the time, Pallas kernels for 9%

profile of v3, /device:TPU:0, one launch (start us, length us, event | category | flops | bytes accessed | tf_op | source)
XLA Modules:
  0.0 52.4 jit_solution(7406867962649232707)
XLA Ops:
  0.6 0.0 copy-start
  0.7 0.0 copy-start.13
  0.7 0.8 %copy-done.13 = s32[1,1,4,2]{2,3,1,0:T(2,128)S(1)} copy-done((s32[1,1,4,2]{2,3,1,0:T(2,128)S(1)}, s32[1,1,4,2]{2,3,1,0:T(2,128)}, u32[]{:S(2)}) %copy-start.13) | copy-done | bytes 56
  1.4 1.3 %pack.1 = (bf16[2,128,256]{2,1,0:T(8,128)(2,1)S(1)}, bf16[2,128,256]{2,1,0:T(8,128)(2,1)S(1)}, bf16[2,128,256]{2,1,0:T(8,128)(2,1)S(1)}, bf16[2,128,256]{2,1,0:T...) custom-call(s32[2,4]{1,0:T(2,128)S(1)} %bitcast.37, ...), custom_call_target="tpu_custom_call" | custom-call | tf_op jit(solution)/shard_map/pack/pallas_call | solution.py:353
  2.7 3.0 %collective-permute-start = (bf16[2,128,256]{2,1,0:T(8,128)(2,1)S(1)}, bf16[2,128,256]{2,1,0:T(8,128)(2,1)S(1)}, u32[]{:S(2)}, u32[]{:S(2)}) collective-permute-start(bf16[2,128,256]{2,1,0:T(8,128)(2,1)S(1)} %get-tuple-element.45), channel_id=1, source_target_pairs={{0,1},{1,0},{2,3},{3,2},{4,5},{5,4},{6,7},{7,6},{8,9},{9,8},{10,11... | collective-permute-start | bytes 393224 | tf_op jit(solution)/shard_map/ppermute | solution.py:333
  5.7 1.5 %collective-permute-start.1 = (bf16[2,128,256]{2,1,0:T(8,128)(2,1)S(1)}, bf16[2,128,256]{2,1,0:T(8,128)(2,1)S(1)}, u32[]{:S(2)}, u32[]{:S(2)}) collective-permute-start(bf16[2,128,256]{2,1,0:T(8,128)(2,1)S(1)} %get-tuple-element.46), channel_id=1, source_target_pairs={{0,2},{1,3},{2,0},{3,1},{4,6},{5,7},{6,4},{7,5},{8,10},{9,11},{10,... | collective-permute-start | bytes 393224 | tf_op jit(solution)/shard_map/ppermute | solution.py:333
  7.2 0.0 collective-permute-start.2
  7.2 1.9 %collective-permute-start.3 = (bf16[2,128,256]{2,1,0:T(8,128)(2,1)S(1)}, bf16[2,128,256]{2,1,0:T(8,128)(2,1)S(1)}, u32[]{:S(2)}, u32[]{:S(2)}) collective-permute-start(bf16[2,128,256]{2,1,0:T(8,128)(2,1)S(1)} %get-tuple-element.56), channel_id=1, source_target_pairs={{0,1},{1,0},{2,3},{3,2},{4,5},{5,4},{6,7},{7,6},{8,9},{9,8},{10,11... | collective-permute-start | bytes 393224 | tf_op jit(solution)/shard_map/ppermute | solution.py:333
  9.2 1.5 %collective-permute-start.4 = (bf16[2,128,256]{2,1,0:T(8,128)(2,1)S(1)}, bf16[2,128,256]{2,1,0:T(8,128)(2,1)S(1)}, u32[]{:S(2)}, u32[]{:S(2)}) collective-permute-start(bf16[2,128,256]{2,1,0:T(8,128)(2,1)S(1)} %get-tuple-element.57), channel_id=1, source_target_pairs={{0,2},{1,3},{2,0},{3,1},{4,6},{5,7},{6,4},{7,5},{8,10},{9,11},{10,... | collective-permute-start | bytes 393224 | tf_op jit(solution)/shard_map/ppermute | solution.py:333
  10.7 0.0 collective-permute-done.refs_0_
  10.7 2.3 %collective-permute-start.5 = (bf16[2,128,256]{2,1,0:T(8,128)(2,1)S(1)}, bf16[2,128,256]{2,1,0:T(8,128)(2,1)S(1)}, u32[]{:S(2)}, u32[]{:S(2)}) collective-permute-start(bf16[2,128,256]{2,1,0:T(8,128)(2,1)S(1)} %get-tuple-element.58), channel_id=1, source_target_pairs={{0,3},{1,2},{2,1},{3,0},{4,7},{5,6},{6,5},{7,4},{8,11},{9,10},{10,... | collective-permute-start | bytes 393224 | tf_op jit(solution)/shard_map/ppermute | solution.py:333
  13.0 0.0 copy-done
  13.0 1.0 %copy-done.1 = bf16[1,1,1024,256]{3,2,1,0:T(8,128)(2,1)S(1)} copy-done((bf16[1,1,1024,256]{3,2,1,0:T(8,128)(2,1)S(1)}, bf16[1,1,1024,256]{3,2,1,0:T(8,128)(2,1)}, u32[]{:S(2)}) %copy-start.1) | copy-done | bytes 524312
  14.1 0.9 %copy-done.6 = bf16[256,256]{1,0:T(8,128)(2,1)S(1)} copy-done((bf16[256,256]{1,0:T(8,128)(2,1)S(1)}, bf16[256,256]{1,0:T(8,128)(2,1)}, u32[]{:S(2)}) %copy-start.6) | copy-done | bytes 131096
  15.0 0.9 %copy-done.7 = bf16[256,256]{1,0:T(8,128)(2,1)S(1)} copy-done((bf16[256,256]{1,0:T(8,128)(2,1)S(1)}, bf16[256,256]{1,0:T(8,128)(2,1)}, u32[]{:S(2)}) %copy-start.7) | copy-done | bytes 131096
  15.9 0.5 %prepare.1 = (bf16[8,512,128]{2,1,0:T(8,128)(2,1)S(1)}, bf16[256,1024]{1,0:T(8,128)(2,1)S(1)}, bf16[256,512]{1,0:T(8,128)(2,1)S(1)}) custom-call(bf16[8,128,256]{2,1,0:T(8,128)(2,1)S(1)} %bitcast.25, bf16[8,4,128,128]{3,2,1,0:T(8,128)(2,1)S(1)} %bitcast.21, bf16[256,256]{1,0:T(8,128)(2,1)S(1)} %copy-done.6, bf16[256,256]{1,0:T(8,128)(2,1)S(1)} %copy-done.7, ...), custom_call_target="tpu_custom_call" | custom-call | flops 1000000000 | bytes 10000000 | tf_op jit(solution)/shard_map/prepare/pallas_call | solution.py:369
  16.4 0.0 collective-permute-done.1.refs_1_
  16.4 0.0 collective-permute-done.2.refs_2_
  16.5 0.5 copy-done.2
  16.9 0.0 copy-done.4
  16.9 0.0 copy-done.5
  17.0 0.0 copy-done.10
  17.0 1.7 %first_layer.1 = (bf16[8,128,256]{2,1,0:T(8,128)(2,1)S(1)}, f32[1024,256]{1,0:T(8,128)S(1)}, bf16[256,1024]{1,0:T(8,128)(2,1)S(1)}, bf16[256,1024]{1,0:T(8,128)(2,1)S(1)}) custom-call(s32[4,8]{1,0:T(4,128)S(1)} %bitcast.33, bf16[256,256]{1,0:T(8,128)(2,1)S(1)} %copy-done.4, bf16[256,256]{1,0:T(8,128)(2,1)S(1)} %copy-done.5, ...), custom_call_target="tpu_custom_call" | custom-call | tf_op jit(solution)/shard_map/first_layer/pallas_call | solution.py:384
  18.7 0.0 copy-start.9
  18.7 0.0 collective-permute-done.3.refs_14_
  18.7 0.4 collective-permute-done.4.refs_15_
  19.1 0.0 collective-permute-done.5.refs_16_
  19.1 0.0 copy-done.8
  19.1 0.0 copy-done.12
  19.1 0.3 copy-done.9
  19.4 0.4 copy-done.11
  19.8 3.8 %second_layer.1 = (bf16[8,128,256]{2,1,0:T(8,128)(2,1)S(1)}, bf16[576,256]{1,0:T(8,128)(2,1)S(1)}, bf16[576,256]{1,0:T(8,128)(2,1)S(1)}, bf16[8,128,256]{2,1,0:T(8,128)(2,1)S(1)}) custom-call(s32[4,8]{1,0:T(4,128)S(1)} %bitcast.34, bf16[256,256]{1,0:T(8,128)(2,1)S(1)} %copy-done.6, bf16[256,256]{1,0:T(8,128)(2,1)S(1)} %copy-done.8, ...), custom_call_target="tpu_custom_call" | custom-call | tf_op jit(solution)/shard_map/second_layer/pallas_call | solution.py:397
  23.5 0.1 collective-permute-start.6
  23.6 1.6 %collective-permute-done.6 = bf16[576,256]{1,0:T(8,128)(2,1)S(1)} collective-permute-done((bf16[576,256]{1,0:T(8,128)(2,1)S(1)}, bf16[576,256]{1,0:T(8,128)(2,1)S(1)}, u32[]{:S(2)}, u32[]{:S(2)}) %collective-permute-start.6) | collective-permute-done | bytes 294944 | tf_op jit(solution)/shard_map/ppermute | solution.py:344
  25.2 0.1 split.1
  25.3 1.3 %collective-permute-start.10 = (bf16[144,256]{1,0:T(8,128)(2,1)S(1)}, bf16[144,256]{1,0:T(8,128)(2,1)S(1)}, u32[]{:S(2)}, u32[]{:S(2)}) collective-permute-start(bf16[144,256]{1,0:T(8,128)(2,1)S(1)} %get-tuple-element.70), channel_id=1, source_target_pairs={{0,1},{1,0},{2,3},{3,2},{4,5},{5,4},{6,7},{7,6},{8,9},{9,8},{10,11... | collective-permute-start | bytes 221192 | tf_op jit(solution)/shard_map/ppermute | solution.py:333
  26.6 0.8 %collective-permute-start.11 = (bf16[144,256]{1,0:T(8,128)(2,1)S(1)}, bf16[144,256]{1,0:T(8,128)(2,1)S(1)}, u32[]{:S(2)}, u32[]{:S(2)}) collective-permute-start(bf16[144,256]{1,0:T(8,128)(2,1)S(1)} %get-tuple-element.71), channel_id=1, source_target_pairs={{0,2},{1,3},{2,0},{3,1},{4,6},{5,7},{6,4},{7,5},{8,10},{9,11},{10,... | collective-permute-start | bytes 221192 | tf_op jit(solution)/shard_map/ppermute | solution.py:333
  27.4 1.4 %collective-permute-start.12 = (bf16[144,256]{1,0:T(8,128)(2,1)S(1)}, bf16[144,256]{1,0:T(8,128)(2,1)S(1)}, u32[]{:S(2)}, u32[]{:S(2)}) collective-permute-start(bf16[144,256]{1,0:T(8,128)(2,1)S(1)} %get-tuple-element.72), channel_id=1, source_target_pairs={{0,3},{1,2},{2,1},{3,0},{4,7},{5,6},{6,5},{7,4},{8,11},{9,10},{10,... | collective-permute-start | bytes 221192 | tf_op jit(solution)/shard_map/ppermute | solution.py:333
  28.8 1.0 %store.1 = (bf16[8,128,256]{2,1,0:T(8,128)(2,1)}, bf16[8,128,256]{2,1,0:T(8,128)(2,1)}, f32[8,128]{1,0:T(8,128)S(1)}) custom-call(bf16[8,128,256]{2,1,0:T(8,128)(2,1)S(1)} %get-tuple-element.48.refs_7_.hidden, bf16[8,128,256]{2,1,0:T(8,128)(2,1)S(1)} %get-tuple-element.59.grad_hidden, bf16[144,256]{1,0:T(8,128)(2,1)S(1)} %get-tuple-element.62.after.refs_0_), custom_call_target="tpu_custom_call" | custom-call | tf_op jit(solution)/shard_map/store/pallas_call | solution.py:459
  29.8 0.0 collective-permute-done.10.refs_1_
  29.8 1.9 %collective-permute-done.11.refs_2_ = bf16[144,256]{1,0:T(8,128)(2,1)S(1)} collective-permute-done((bf16[144,256]{1,0:T(8,128)(2,1)S(1)}, bf16[144,256]{1,0:T(8,128)(2,1)S(1)}, u32[]{:S(2)}, u32[]{:S(2)}) %collective-permute-start.11) | collective-permute-done | bytes 73760 | tf_op jit(solution)/shard_map/ppermute | solution.py:333
  31.7 0.9 %collective-permute-done.12.refs_3_ = bf16[144,256]{1,0:T(8,128)(2,1)S(1)} collective-permute-done((bf16[144,256]{1,0:T(8,128)(2,1)S(1)}, bf16[144,256]{1,0:T(8,128)(2,1)S(1)}, u32[]{:S(2)}, u32[]{:S(2)}) %collective-permute-start.12) | collective-permute-done | bytes 73760 | tf_op jit(solution)/shard_map/ppermute | solution.py:333
  32.7 3.7 %collective-permute-start.15 = (bf16[144,256]{1,0:T(8,128)(2,1)S(1)}, bf16[144,256]{1,0:T(8,128)(2,1)S(1)}, u32[]{:S(2)}, u32[]{:S(2)}) collective-permute-start(bf16[144,256]{1,0:T(8,128)(2,1)S(1)} %add.2.refs_0_), channel_id=1, source_target_pairs={{0,24},{4,28},{8,16},{12,20},{16,8},{20,12},{24,0},{28,4},{1,25},{... | collective-permute-start | bytes 221192 | tf_op jit(solution)/shard_map/ppermute | solution.py:341
  36.4 1.6 %collective-permute-start.7 = (bf16[2,128,256]{2,1,0:T(8,128)(2,1)S(1)}, bf16[2,128,256]{2,1,0:T(8,128)(2,1)S(1)}, u32[]{:S(2)}, u32[]{:S(2)}) collective-permute-start(bf16[2,128,256]{2,1,0:T(8,128)(2,1)S(1)} %get-tuple-element.66), channel_id=1, source_target_pairs={{0,1},{1,0},{2,3},{3,2},{4,5},{5,4},{6,7},{7,6},{8,9},{9,8},{10,11... | collective-permute-start | bytes 393224 | tf_op jit(solution)/shard_map/ppermute | solution.py:333
  37.9 0.0 collective-permute-start.14
  37.9 0.8 %collective-permute-start.13 = (bf16[144,256]{1,0:T(8,128)(2,1)S(1)}, bf16[144,256]{1,0:T(8,128)(2,1)S(1)}, u32[]{:S(2)}, u32[]{:S(2)}) collective-permute-start(bf16[144,256]{1,0:T(8,128)(2,1)S(1)} %add.2.refs_0_), channel_id=1, source_target_pairs={{0,8},{4,12},{8,0},{12,4},{16,24},{20,28},{24,16},{28,20},{1,9},{5... | collective-permute-start | bytes 221192 | tf_op jit(solution)/shard_map/ppermute | solution.py:341
  38.7 0.7 %collective-permute-start.8 = (bf16[2,128,256]{2,1,0:T(8,128)(2,1)S(1)}, bf16[2,128,256]{2,1,0:T(8,128)(2,1)S(1)}, u32[]{:S(2)}, u32[]{:S(2)}) collective-permute-start(bf16[2,128,256]{2,1,0:T(8,128)(2,1)S(1)} %get-tuple-element.67), channel_id=1, source_target_pairs={{0,2},{1,3},{2,0},{3,1},{4,6},{5,7},{6,4},{7,5},{8,10},{9,11},{10,... | collective-permute-start | bytes 393224 | tf_op jit(solution)/shard_map/ppermute | solution.py:333
  39.4 0.1 collective-permute-done.15.refs_3_
  39.6 1.7 %collective-permute-start.9 = (bf16[2,128,256]{2,1,0:T(8,128)(2,1)S(1)}, bf16[2,128,256]{2,1,0:T(8,128)(2,1)S(1)}, u32[]{:S(2)}, u32[]{:S(2)}) collective-permute-start(bf16[2,128,256]{2,1,0:T(8,128)(2,1)S(1)} %get-tuple-element.68), channel_id=1, source_target_pairs={{0,3},{1,2},{2,1},{3,0},{4,7},{5,6},{6,5},{7,4},{8,11},{9,10},{10,... | collective-permute-start | bytes 393224 | tf_op jit(solution)/shard_map/ppermute | solution.py:333
  41.2 2.0 %collective-permute-done.14.refs_2_ = bf16[144,256]{1,0:T(8,128)(2,1)S(1)} collective-permute-done((bf16[144,256]{1,0:T(8,128)(2,1)S(1)}, bf16[144,256]{1,0:T(8,128)(2,1)S(1)}, u32[]{:S(2)}, u32[]{:S(2)}) %collective-permute-start.14) | collective-permute-done | bytes 73760 | tf_op jit(solution)/shard_map/ppermute | solution.py:341
  43.2 0.0 collective-permute-done.13.refs_1_
  43.2 1.2 %collective-permute-start.18 = (bf16[144,256]{1,0:T(8,128)(2,1)S(1)}, bf16[144,256]{1,0:T(8,128)(2,1)S(1)}, u32[]{:S(2)}, u32[]{:S(2)}) collective-permute-start(bf16[144,256]{1,0:T(8,128)(2,1)S(1)} %add.3.own), channel_id=1, source_target_pairs={{0,3},{1,2},{2,1},{3,0},{4,7},{5,6},{6,5},{7,4},{8,11},{9,10},{10,... | collective-permute-start | bytes 221192 | tf_op jit(solution)/shard_map/ppermute | solution.py:333
  44.5 0.8 %collective-permute-start.17 = (bf16[144,256]{1,0:T(8,128)(2,1)S(1)}, bf16[144,256]{1,0:T(8,128)(2,1)S(1)}, u32[]{:S(2)}, u32[]{:S(2)}) collective-permute-start(bf16[144,256]{1,0:T(8,128)(2,1)S(1)} %add.3.own), channel_id=1, source_target_pairs={{0,2},{1,3},{2,0},{3,1},{4,6},{5,7},{6,4},{7,5},{8,10},{9,11},{10,... | collective-permute-start | bytes 221192 | tf_op jit(solution)/shard_map/ppermute | solution.py:333
  45.3 0.0 collective-permute-done.7.refs_0_
  45.3 1.5 %collective-permute-start.16 = (bf16[144,256]{1,0:T(8,128)(2,1)S(1)}, bf16[144,256]{1,0:T(8,128)(2,1)S(1)}, u32[]{:S(2)}, u32[]{:S(2)}) collective-permute-start(bf16[144,256]{1,0:T(8,128)(2,1)S(1)} %add.3.own), channel_id=1, source_target_pairs={{0,1},{1,0},{2,3},{3,2},{4,5},{5,4},{6,7},{7,6},{8,9},{9,8},{10,11... | collective-permute-start | bytes 221192 | tf_op jit(solution)/shard_map/ppermute | solution.py:333
  46.8 0.0 collective-permute-done.8.refs_1_
  46.8 0.0 collective-permute-done.9.refs_2_
  46.8 1.5 %aux.1 = (bf16[8,128,256]{2,1,0:T(8,128)(2,1)}, f32[8,128]{1,0:T(8,128)S(1)}) custom-call(s32[2,4]{1,0:T(2,128)S(1)} %bitcast.38, bf16[2,128,256]{2,1,0:T(8,128)(2,1)S(1)} %collective-permute-done.7.refs_0_, bf16[2,128,256]{2,1,0:T(8,128)(2,1)S(1)} %collective-permute-done.8.refs_1_, bf16[2,128,256]{2,1,0:T(8,128)(2,1)S(1)} %collective-permute-done.9.refs_2_), custom_call_target="tpu_custom_call" | custom-call | flops 1000000 | bytes 1000000 | tf_op jit(solution)/shard_map/aux/pallas_call | solution.py:478
  48.3 0.3 collective-permute-done.18.refs_2_
  48.6 0.7 %collective-permute-done.17.refs_1_ = bf16[144,256]{1,0:T(8,128)(2,1)S(1)} collective-permute-done((bf16[144,256]{1,0:T(8,128)(2,1)S(1)}, bf16[144,256]{1,0:T(8,128)(2,1)S(1)}, u32[]{:S(2)}, u32[]{:S(2)}) %collective-permute-start.17) | collective-permute-done | bytes 73760 | tf_op jit(solution)/shard_map/ppermute | solution.py:333
  49.3 0.3 collective-permute-done.16.refs_0_
  49.7 0.1 collective-permute-start.19
  49.8 1.6 %collective-permute-done.19.other = bf16[576,256]{1,0:T(8,128)(2,1)S(1)} collective-permute-done((bf16[576,256]{1,0:T(8,128)(2,1)S(1)}, bf16[576,256]{1,0:T(8,128)(2,1)S(1)}, u32[]{:S(2)}, u32[]{:S(2)}) %collective-permute-start.19) | collective-permute-done | bytes 294944 | tf_op jit(solution)/shard_map/ppermute | solution.py:344
  51.3 1.0 %finish.1 = (f32[256,256]{1,0:T(8,128)}, f32[256,256]{1,0:T(8,128)}, f32[256,256]{1,0:T(8,128)}, f32[256,256]{1,0:T(8,128)}, f32[32,256]{1,0:T(8,128)}, /*index=5*/f32[1,1]{1,0:T(1,128)}) custom-call(bf16[576,256]{1,0:T(8,128)(2,1)S(1)} %bitcast.28, bf16[576,256]{1,0:T(8,128)(2,1)S(1)} %collective-permute-done.19.other), custom_call_target="tpu_custom_call" | custom-call | tf_op jit(solution)/shard_map/finish/pallas_call | solution.py:503
  (16 shorter events, 0.2 us)
Async XLA Ops:
  0.6 12.4 %copy-start = (bf16[1,1,8,4,128,128]{5,4,3,2,1,0:T(8,128)(2,1)S(1)}, bf16[1,1,8,4,128,128]{5,4,3,2,1,0:T(8,128)(2,1)}, u32[]{:S(2)}) copy-start(bf16[1,1,8,4,128,128]{5,4,3,2,1,0:T(8,128)(2,1)} %param.16) | copy-start | bytes 3145732
  0.7 0.8 %copy-start.13 = (s32[1,1,4,2]{2,3,1,0:T(2,128)S(1)}, s32[1,1,4,2]{2,3,1,0:T(2,128)}, u32[]{:S(2)}) copy-start(s32[1,1,4,2]{2,3,1,0:T(2,128)} %param.18) | copy-start | bytes 100
  2.7 8.0 %collective-permute-start = (bf16[2,128,256]{2,1,0:T(8,128)(2,1)S(1)}, bf16[2,128,256]{2,1,0:T(8,128)(2,1)S(1)}, u32[]{:S(2)}, u32[]{:S(2)}) collective-permute-start(bf16[2,128,256]{2,1,0:T(8,128)(2,1)S(1)} %get-tuple-element.45), channel_id=1, source_target_pairs={{0,1},{1,0},{2,3},{3,2},{4,5},{5,4},{6,7},{7,6},{8,9},{9,8},{10,11... | collective-permute-start | bytes 393224 | tf_op jit(solution)/shard_map/ppermute | solution.py:333
  5.7 10.8 %collective-permute-start.1 = (bf16[2,128,256]{2,1,0:T(8,128)(2,1)S(1)}, bf16[2,128,256]{2,1,0:T(8,128)(2,1)S(1)}, u32[]{:S(2)}, u32[]{:S(2)}) collective-permute-start(bf16[2,128,256]{2,1,0:T(8,128)(2,1)S(1)} %get-tuple-element.46), channel_id=1, source_target_pairs={{0,2},{1,3},{2,0},{3,1},{4,6},{5,7},{6,4},{7,5},{8,10},{9,11},{10,... | collective-permute-start | bytes 393224 | tf_op jit(solution)/shard_map/ppermute | solution.py:333
  7.2 9.2 %collective-permute-start.2 = (bf16[2,128,256]{2,1,0:T(8,128)(2,1)S(1)}, bf16[2,128,256]{2,1,0:T(8,128)(2,1)S(1)}, u32[]{:S(2)}, u32[]{:S(2)}) collective-permute-start(bf16[2,128,256]{2,1,0:T(8,128)(2,1)S(1)} %get-tuple-element.47), channel_id=1, source_target_pairs={{0,3},{1,2},{2,1},{3,0},{4,7},{5,6},{6,5},{7,4},{8,11},{9,10},{10,... | collective-permute-start | bytes 393224 | tf_op jit(solution)/shard_map/ppermute | solution.py:333
  7.2 11.4 %collective-permute-start.3 = (bf16[2,128,256]{2,1,0:T(8,128)(2,1)S(1)}, bf16[2,128,256]{2,1,0:T(8,128)(2,1)S(1)}, u32[]{:S(2)}, u32[]{:S(2)}) collective-permute-start(bf16[2,128,256]{2,1,0:T(8,128)(2,1)S(1)} %get-tuple-element.56), channel_id=1, source_target_pairs={{0,1},{1,0},{2,3},{3,2},{4,5},{5,4},{6,7},{7,6},{8,9},{9,8},{10,11... | collective-permute-start | bytes 393224 | tf_op jit(solution)/shard_map/ppermute | solution.py:333
  9.2 9.9 %collective-permute-start.4 = (bf16[2,128,256]{2,1,0:T(8,128)(2,1)S(1)}, bf16[2,128,256]{2,1,0:T(8,128)(2,1)S(1)}, u32[]{:S(2)}, u32[]{:S(2)}) collective-permute-start(bf16[2,128,256]{2,1,0:T(8,128)(2,1)S(1)} %get-tuple-element.57), channel_id=1, source_target_pairs={{0,2},{1,3},{2,0},{3,1},{4,6},{5,7},{6,4},{7,5},{8,10},{9,11},{10,... | collective-permute-start | bytes 393224 | tf_op jit(solution)/shard_map/ppermute | solution.py:333
  10.7 8.4 %collective-permute-start.5 = (bf16[2,128,256]{2,1,0:T(8,128)(2,1)S(1)}, bf16[2,128,256]{2,1,0:T(8,128)(2,1)S(1)}, u32[]{:S(2)}, u32[]{:S(2)}) collective-permute-start(bf16[2,128,256]{2,1,0:T(8,128)(2,1)S(1)} %get-tuple-element.58), channel_id=1, source_target_pairs={{0,3},{1,2},{2,1},{3,0},{4,7},{5,6},{6,5},{7,4},{8,11},{9,10},{10,... | collective-permute-start | bytes 393224 | tf_op jit(solution)/shard_map/ppermute | solution.py:333
  13.0 1.0 %copy-start.1 = (bf16[1,1,1024,256]{3,2,1,0:T(8,128)(2,1)S(1)}, bf16[1,1,1024,256]{3,2,1,0:T(8,128)(2,1)}, u32[]{:S(2)}) copy-start(bf16[1,1,1024,256]{3,2,1,0:T(8,128)(2,1)} %param.13) | copy-start | bytes 1572868
  14.1 0.9 %copy-start.6 = (bf16[256,256]{1,0:T(8,128)(2,1)S(1)}, bf16[256,256]{1,0:T(8,128)(2,1)}, u32[]{:S(2)}) copy-start(bf16[256,256]{1,0:T(8,128)(2,1)} %refs_0_.1) | copy-start | bytes 393220
  15.0 0.9 %copy-start.7 = (bf16[256,256]{1,0:T(8,128)(2,1)S(1)}, bf16[256,256]{1,0:T(8,128)(2,1)}, u32[]{:S(2)}) copy-start(bf16[256,256]{1,0:T(8,128)(2,1)} %refs_1_.1) | copy-start | bytes 393220
  15.9 1.0 %copy-start.2 = (bf16[1,1,1024,256]{3,2,1,0:T(8,128)(2,1)S(1)}, bf16[1,1,1024,256]{3,2,1,0:T(8,128)(2,1)}, u32[]{:S(2)}) copy-start(bf16[1,1,1024,256]{3,2,1,0:T(8,128)(2,1)} %param.13) | copy-start | bytes 1572868
  15.9 1.1 %copy-start.4 = (bf16[256,256]{1,0:T(8,128)(2,1)S(1)}, bf16[256,256]{1,0:T(8,128)(2,1)}, u32[]{:S(2)}) copy-start(bf16[256,256]{1,0:T(8,128)(2,1)} %wn.2) | copy-start | bytes 393220
  15.9 1.1 %copy-start.5 = (bf16[256,256]{1,0:T(8,128)(2,1)S(1)}, bf16[256,256]{1,0:T(8,128)(2,1)}, u32[]{:S(2)}) copy-start(bf16[256,256]{1,0:T(8,128)(2,1)} %ws.2) | copy-start | bytes 393220
  15.9 1.1 %copy-start.10 = (s32[1,1,8,4]{2,3,1,0:T(4,128)S(1)}, s32[1,1,8,4]{2,3,1,0:T(4,128)}, u32[]{:S(2)}) copy-start(s32[1,1,8,4]{2,3,1,0:T(4,128)} %param.17) | copy-start | bytes 388
  17.0 2.1 %copy-start.3 = (bf16[1,1,1024,256]{3,2,1,0:T(8,128)(2,1)S(1)}, bf16[1,1,1024,256]{3,2,1,0:T(8,128)(2,1)}, u32[]{:S(2)}) copy-start(bf16[1,1,1024,256]{3,2,1,0:T(8,128)(2,1)} %param.15) | copy-start | bytes 1572868
  17.0 2.1 %copy-start.8 = (bf16[256,256]{1,0:T(8,128)(2,1)S(1)}, bf16[256,256]{1,0:T(8,128)(2,1)}, u32[]{:S(2)}) copy-start(bf16[256,256]{1,0:T(8,128)(2,1)} %refs_1_.1) | copy-start | bytes 393220
  17.0 2.1 %copy-start.12 = (s32[1,1,1024]{2,1,0:T(1,128)S(1)}, s32[1,1,1024]{2,1,0:T(1,128)}, u32[]{:S(2)}) copy-start(s32[1,1,1024]{2,1,0:T(1,128)} %param.20) | copy-start | bytes 12292
  18.7 0.7 %copy-start.9 = (bf16[256,32]{0,1:T(8,128)(2,1)S(1)}, bf16[256,32]{0,1:T(8,128)(2,1)}, u32[]{:S(2)}) copy-start(bf16[256,32]{0,1:T(8,128)(2,1)} %param.25) | copy-start | bytes 49156
  19.1 0.7 %copy-start.11 = (s32[1,1,1024]{2,1,0:T(1,128)S(1)}, s32[1,1,1024]{2,1,0:T(1,128)}, u32[]{:S(2)}) copy-start(s32[1,1,1024]{2,1,0:T(1,128)} %param.19) | copy-start | bytes 12292
  23.5 1.6 %collective-permute-start.6 = (bf16[576,256]{1,0:T(8,128)(2,1)S(1)}, bf16[576,256]{1,0:T(8,128)(2,1)S(1)}, u32[]{:S(2)}, u32[]{:S(2)}) collective-permute-start(bf16[576,256]{1,0:T(8,128)(2,1)S(1)} %get-tuple-element.61), channel_id=1, source_target_pairs={{0,4},{4,0},{8,12},{12,8},{16,20},{20,16},{24,28},{28,24},{1,5},{5... | collective-permute-start | bytes 884744 | tf_op jit(solution)/shard_map/ppermute | solution.py:344
  25.3 4.5 %collective-permute-start.10 = (bf16[144,256]{1,0:T(8,128)(2,1)S(1)}, bf16[144,256]{1,0:T(8,128)(2,1)S(1)}, u32[]{:S(2)}, u32[]{:S(2)}) collective-permute-start(bf16[144,256]{1,0:T(8,128)(2,1)S(1)} %get-tuple-element.70), channel_id=1, source_target_pairs={{0,1},{1,0},{2,3},{3,2},{4,5},{5,4},{6,7},{7,6},{8,9},{9,8},{10,11... | collective-permute-start | bytes 221192 | tf_op jit(solution)/shard_map/ppermute | solution.py:333
  26.6 5.1 %collective-permute-start.11 = (bf16[144,256]{1,0:T(8,128)(2,1)S(1)}, bf16[144,256]{1,0:T(8,128)(2,1)S(1)}, u32[]{:S(2)}, u32[]{:S(2)}) collective-permute-start(bf16[144,256]{1,0:T(8,128)(2,1)S(1)} %get-tuple-element.71), channel_id=1, source_target_pairs={{0,2},{1,3},{2,0},{3,1},{4,6},{5,7},{6,4},{7,5},{8,10},{9,11},{10,... | collective-permute-start | bytes 221192 | tf_op jit(solution)/shard_map/ppermute | solution.py:333
  27.4 5.3 %collective-permute-start.12 = (bf16[144,256]{1,0:T(8,128)(2,1)S(1)}, bf16[144,256]{1,0:T(8,128)(2,1)S(1)}, u32[]{:S(2)}, u32[]{:S(2)}) collective-permute-start(bf16[144,256]{1,0:T(8,128)(2,1)S(1)} %get-tuple-element.72), channel_id=1, source_target_pairs={{0,3},{1,2},{2,1},{3,0},{4,7},{5,6},{6,5},{7,4},{8,11},{9,10},{10,... | collective-permute-start | bytes 221192 | tf_op jit(solution)/shard_map/ppermute | solution.py:333
  32.7 6.9 %collective-permute-start.15 = (bf16[144,256]{1,0:T(8,128)(2,1)S(1)}, bf16[144,256]{1,0:T(8,128)(2,1)S(1)}, u32[]{:S(2)}, u32[]{:S(2)}) collective-permute-start(bf16[144,256]{1,0:T(8,128)(2,1)S(1)} %add.2.refs_0_), channel_id=1, source_target_pairs={{0,24},{4,28},{8,16},{12,20},{16,8},{20,12},{24,0},{28,4},{1,25},{... | collective-permute-start | bytes 221192 | tf_op jit(solution)/shard_map/ppermute | solution.py:341
  36.4 8.9 %collective-permute-start.7 = (bf16[2,128,256]{2,1,0:T(8,128)(2,1)S(1)}, bf16[2,128,256]{2,1,0:T(8,128)(2,1)S(1)}, u32[]{:S(2)}, u32[]{:S(2)}) collective-permute-start(bf16[2,128,256]{2,1,0:T(8,128)(2,1)S(1)} %get-tuple-element.66), channel_id=1, source_target_pairs={{0,1},{1,0},{2,3},{3,2},{4,5},{5,4},{6,7},{7,6},{8,9},{9,8},{10,11... | collective-permute-start | bytes 393224 | tf_op jit(solution)/shard_map/ppermute | solution.py:333
  37.9 5.3 %collective-permute-start.14 = (bf16[144,256]{1,0:T(8,128)(2,1)S(1)}, bf16[144,256]{1,0:T(8,128)(2,1)S(1)}, u32[]{:S(2)}, u32[]{:S(2)}) collective-permute-start(bf16[144,256]{1,0:T(8,128)(2,1)S(1)} %add.2.refs_0_), channel_id=1, source_target_pairs={{0,16},{4,20},{8,24},{12,28},{16,0},{20,4},{24,8},{28,12},{1,17},{... | collective-permute-start | bytes 221192 | tf_op jit(solution)/shard_map/ppermute | solution.py:341
  37.9 5.3 %collective-permute-start.13 = (bf16[144,256]{1,0:T(8,128)(2,1)S(1)}, bf16[144,256]{1,0:T(8,128)(2,1)S(1)}, u32[]{:S(2)}, u32[]{:S(2)}) collective-permute-start(bf16[144,256]{1,0:T(8,128)(2,1)S(1)} %add.2.refs_0_), channel_id=1, source_target_pairs={{0,8},{4,12},{8,0},{12,4},{16,24},{20,28},{24,16},{28,20},{1,9},{5... | collective-permute-start | bytes 221192 | tf_op jit(solution)/shard_map/ppermute | solution.py:341
  38.7 8.1 %collective-permute-start.8 = (bf16[2,128,256]{2,1,0:T(8,128)(2,1)S(1)}, bf16[2,128,256]{2,1,0:T(8,128)(2,1)S(1)}, u32[]{:S(2)}, u32[]{:S(2)}) collective-permute-start(bf16[2,128,256]{2,1,0:T(8,128)(2,1)S(1)} %get-tuple-element.67), channel_id=1, source_target_pairs={{0,2},{1,3},{2,0},{3,1},{4,6},{5,7},{6,4},{7,5},{8,10},{9,11},{10,... | collective-permute-start | bytes 393224 | tf_op jit(solution)/shard_map/ppermute | solution.py:333
  39.6 7.2 %collective-permute-start.9 = (bf16[2,128,256]{2,1,0:T(8,128)(2,1)S(1)}, bf16[2,128,256]{2,1,0:T(8,128)(2,1)S(1)}, u32[]{:S(2)}, u32[]{:S(2)}) collective-permute-start(bf16[2,128,256]{2,1,0:T(8,128)(2,1)S(1)} %get-tuple-element.68), channel_id=1, source_target_pairs={{0,3},{1,2},{2,1},{3,0},{4,7},{5,6},{6,5},{7,4},{8,11},{9,10},{10,... | collective-permute-start | bytes 393224 | tf_op jit(solution)/shard_map/ppermute | solution.py:333
  43.2 5.4 %collective-permute-start.18 = (bf16[144,256]{1,0:T(8,128)(2,1)S(1)}, bf16[144,256]{1,0:T(8,128)(2,1)S(1)}, u32[]{:S(2)}, u32[]{:S(2)}) collective-permute-start(bf16[144,256]{1,0:T(8,128)(2,1)S(1)} %add.3.own), channel_id=1, source_target_pairs={{0,3},{1,2},{2,1},{3,0},{4,7},{5,6},{6,5},{7,4},{8,11},{9,10},{10,... | collective-permute-start | bytes 221192 | tf_op jit(solution)/shard_map/ppermute | solution.py:333
  44.5 4.9 %collective-permute-start.17 = (bf16[144,256]{1,0:T(8,128)(2,1)S(1)}, bf16[144,256]{1,0:T(8,128)(2,1)S(1)}, u32[]{:S(2)}, u32[]{:S(2)}) collective-permute-start(bf16[144,256]{1,0:T(8,128)(2,1)S(1)} %add.3.own), channel_id=1, source_target_pairs={{0,2},{1,3},{2,0},{3,1},{4,6},{5,7},{6,4},{7,5},{8,10},{9,11},{10,... | collective-permute-start | bytes 221192 | tf_op jit(solution)/shard_map/ppermute | solution.py:333
  45.3 4.4 %collective-permute-start.16 = (bf16[144,256]{1,0:T(8,128)(2,1)S(1)}, bf16[144,256]{1,0:T(8,128)(2,1)S(1)}, u32[]{:S(2)}, u32[]{:S(2)}) collective-permute-start(bf16[144,256]{1,0:T(8,128)(2,1)S(1)} %add.3.own), channel_id=1, source_target_pairs={{0,1},{1,0},{2,3},{3,2},{4,5},{5,4},{6,7},{7,6},{8,9},{9,8},{10,11... | collective-permute-start | bytes 221192 | tf_op jit(solution)/shard_map/ppermute | solution.py:333
  49.7 1.6 %collective-permute-start.19 = (bf16[576,256]{1,0:T(8,128)(2,1)S(1)}, bf16[576,256]{1,0:T(8,128)(2,1)S(1)}, u32[]{:S(2)}, u32[]{:S(2)}) collective-permute-start(bf16[576,256]{1,0:T(8,128)(2,1)S(1)} %bitcast.27), channel_id=1, source_target_pairs={{0,4},{4,0},{8,12},{12,8},{16,20},{20,16},{24,28},{28,24},{1,5},{5... | collective-permute-start | bytes 884744 | tf_op jit(solution)/shard_map/ppermute | solution.py:344

commit v4 on v3

--- a/solution.py
+++ b/solution.py
@@ -54,10 +54,9 @@
                 outs[which * (peers - 1) + step - 1][s] = values[block]
 
 
-def prepare_kernel(dims, feat, tiles, wn, ws, token, tiles_t, feat_t, w_t):
-    blocks, picks, rows, width = dims
-    w_t[:, :width] = wn[...].T
-    w_t[:, width:] = ws[...].T
+def prepare_kernel(dims, feat, tiles, token, tiles_t, feat_t, feat_kept):
+    blocks, picks, rows = dims
+    feat_kept[...] = feat[...]
     for b in range(blocks):
         feat_t[:, b * rows : (b + 1) * rows] = feat[b].T
     for b in range(blocks):
@@ -75,11 +74,12 @@
     return value, gate + value * (1.0 - gate)
 
 
-def first_kernel(dims, sources_in, wn, ws, feat, tiles, *refs):
+def first_kernel(dims, sources_in, wn, ws, wn_next, ws_next, head, bins, flags, feat, tiles, *refs):
     peers, slots, blocks, picks, rows, width = dims
     inc = peers - 1
     feat_in, refs = refs[:inc], refs[inc:]
-    own2, slope1, agg_t, hidden_t, table, sources, sem = refs
+    own2, slope1, agg_t, hidden_t, w, w_t, head_kept, bins_kept, flags_kept = refs[:9]
+    table, sources, sem = refs[9:]
     g = lax.axis_index("grp")
     listed = pltpu.make_async_copy(sources_in, sources, sem)
     listed.start()
@@ -87,6 +87,13 @@
     for step in range(1, peers):
         _, origin = partner(g, step, peers)
         table[pl.ds(blocks + origin * slots, slots)] = feat_in[step - 1][...]
+    head_kept[...] = head[...]
+    bins_kept[...] = bins[...]
+    flags_kept[...] = flags[...]
+    w[:width] = wn_next[...]
+    w[width:] = ws_next[...]
+    w_t[:, :width] = wn_next[...].T
+    w_t[:, width:] = ws_next[...].T
     listed.wait()
     aggs = []
     for b in range(blocks):
@@ -113,7 +120,7 @@
 def second_kernel(dims, sources_in, *refs):
     peers, slots, blocks, picks, rows, width, bins_count, pay_rows = dims
     inc = peers - 1
-    (wn, ws, w_t, head, bins, flags, aux), refs = refs[:7], refs[7:]
+    (w, w_t, head, bins, flags, aux), refs = refs[:6], refs[6:]
     (own2, slope1, tiles, tiles_t, agg1_t, feat_t, hidden_t), refs = refs[:7], refs[7:]
     past_in, refs = refs[:inc], refs[inc:]
     (grad_hidden, keep, send, back), refs = refs[:4], refs[4:]
@@ -141,7 +148,6 @@
     pair = 2
     span = pair * rows
     step_col = lax.broadcasted_iota(jnp.int32, (bins_count, span), 0)
-    both_w = jnp.concatenate([wn[...], ws[...]], axis=0)
     loss = jnp.zeros((bins_count, span), F32)
     ghw = jnp.zeros((bins_count, width), F32)
     chunks = range(blocks // pair)
@@ -155,7 +161,7 @@
             ],
             axis=1,
         )
-        gates.append(gate_of(dot(both, both_w)))
+        gates.append(gate_of(dot(both, w[...])))
     hidden = [value.astype(BF16) for value, _ in gates]
     logits = [dot_by_transpose(head[...], hidden[i]) for i in chunks]
     glogs = []
@@ -366,26 +372,36 @@
     )(routing, feat, past)
     feat_in = [over_grp(packed[i], i + 1) for i in range(inc)]
     past_in = [over_grp(packed[inc + i], i + 1) for i in range(inc)]
-    tiles_t, feat_t, w_t = pl.pallas_call(
-        functools.partial(prepare_kernel, (blocks, picks, rows, width)),
+    tiles_t, feat_t, feat = pl.pallas_call(
+        functools.partial(prepare_kernel, (blocks, picks, rows)),
         out_shape=[
             shape((blocks, picks * rows, rows)),
             shape(turned),
-            shape((width, 2 * width)),
-        ],
-        in_specs=[VMEM] * 5,
+            shape(block_shape),
+        ],
+        in_specs=[VMEM] * 3,
         out_specs=[VMEM] * 3,
         compiler_params=pltpu.CompilerParams(vmem_limit_bytes=PREP_LIMIT),
         cost_estimate=pl.CostEstimate(flops=10**9, bytes_accessed=10**7, transcendentals=0),
         name="prepare",
-    )(feat, tiles, neigh_second, self_second, packed[2 * inc])
+    )(feat, tiles, packed[2 * inc])
 
     pair_shape = (blocks // 2, 1, 2 * rows)
-    own2, slope1, agg_t, hidden_t = pl.pallas_call(
+    own2, slope1, agg_t, hidden_t, w, w_t, head, bins, flags = pl.pallas_call(
         functools.partial(first_kernel, (peers, slots, blocks, picks, rows, width)),
-        out_shape=[shape(block_shape), shape((nodes, width), F32), shape(turned), shape(turned)],
-        in_specs=[HBM] + [VMEM] * (4 + inc),
-        out_specs=[VMEM] * 4,
+        out_shape=[
+            shape(block_shape),
+            shape((nodes, width), F32),
+            shape(turned),
+            shape(turned),
+            shape((2 * width, width)),
+            shape((width, 2 * width)),
+            shape((bins_count, width)),
+            shape(pair_shape, jnp.int32),
+            shape(pair_shape, jnp.int32),
+        ],
+        in_specs=[HBM] + [VMEM] * (9 + inc),
+        out_specs=[VMEM] * 9,
         scratch_shapes=[
             pltpu.VMEM((table, rows, width), BF16),
             pltpu.SMEM((picks, blocks), jnp.int32),
@@ -393,7 +409,19 @@
         ],
         compiler_params=params,
         name="first_layer",
-    )(sources, neigh_first, self_first, feat, tiles, *feat_in)
+    )(
+        sources,
+        neigh_first,
+        self_first,
+        neigh_second,
+        self_second,
+        hazard_weight.T,
+        event_bins.reshape(pair_shape),
+        event_flags.reshape(pair_shape),
+        feat,
+        tiles,
+        *feat_in,
+    )
     grad_hidden, kept, sent, back = pl.pallas_call(
         functools.partial(
             second_kernel, (peers, slots, blocks, picks, rows, width, bins_count, pay_rows)
@@ -404,7 +432,7 @@
             shape((half, width)),
             shape((peers * slots, rows, width)),
         ],
-        in_specs=[HBM] + [VMEM] * (14 + inc),
+        in_specs=[HBM] + [VMEM] * (13 + inc),
         out_specs=[VMEM] * 4,
         scratch_shapes=[
             pltpu.SMEM((picks, blocks), jnp.int32),
@@ -418,12 +446,11 @@
         name="second_layer",
     )(
         sources,
-        neigh_second,
-        self_second,
+        w,
         w_t,
-        hazard_weight.T,
-        event_bins.reshape(pair_shape),
-        event_flags.reshape(pair_shape),
+        head,
+        bins,
+        flags,
         aux_history.reshape(block_shape),
         own2,
         slope1,

time: 52.7 us -> 51.9 us (0.985)
  local copies, waits for them, and re-layouts: 4.82 us -> 2.58 us
  waiting for transfers between devices: 9.83 us -> 11.5 us
    unnamed x28 -> x24, local copies, waits for them, and re-layouts: 4.82 us -> 2.58 us
    ppermute x15, waiting for transfers between devices: 4.59 us -> 6.23 us  [over_grp(): return lax.ppermute(value, 'grp', grp_pairs(step))]
  transfers between devices with their start and end apart: 20 -> 20, of which waited for: 10 -> 11; matrix products, arithmetic and copies ran while one was open for 0% -> 0% of each run, Pallas kernels for 9% -> 9%
where the time goes in v4:
time: 51.9 us; the launch traced here: 51.7 us
  starting transfers between devices  26 us (50%)
  waiting for transfers between devices  11.5 us (22%)
  Pallas kernels  10.9 us (21%)
  local copies, waits for them, and re-layouts  2.58 us (5%)
  between operations  0.8 us (2%)
    ppermute x15, starting transfers between devices, over_grp(): return lax.ppermute(value, 'grp', grp_pairs(step))  21.4 us
    ppermute x15, waiting for transfers between devices, over_grp(): return lax.ppermute(value, 'grp', grp_pairs(step))  6.23 us
    ppermute x3, starting transfers between devices, over_z(): return lax.ppermute(value, 'clus', pairs)  4.45 us
    pallas_call x1, Pallas kernels, shards(): pl.pallas_call(functools.partial(second_kernel, (peers, slots, blocks, pi...  3.75 us
    ppermute x2, waiting for transfers between devices, over_core(): return lax.ppermute(value, 'clus', [(i, i ^ 1) for i in range(clus_count)])  3.14 us
    unnamed x24, local copies, waits for them, and re-layouts  2.58 us
    ppermute x3, waiting for transfers between devices, over_z(): return lax.ppermute(value, 'clus', pairs)  2.11 us
    pallas_call x1, Pallas kernels, shards(): pl.pallas_call(functools.partial(first_kernel, (peers, slots, blocks, pic...  1.67 us
  transfers between devices with their start and end apart: 20, of which 11 were waited for; matrix products, arithmetic and copies ran while one was open for 0% of the time, Pallas kernels for 9%

profile of v4, /device:TPU:0, one launch (start us, length us, event | category | flops | bytes accessed | tf_op | source)
XLA Modules:
  0.0 51.7 jit_solution(11348736506913146914)
XLA Ops:
  0.6 0.0 copy-start
  0.7 0.0 copy-start.11
  0.7 0.8 %copy-done.11 = s32[1,1,4,2]{2,3,1,0:T(2,128)S(1)} copy-done((s32[1,1,4,2]{2,3,1,0:T(2,128)S(1)}, s32[1,1,4,2]{2,3,1,0:T(2,128)}, u32[]{:S(2)}) %copy-start.11) | copy-done | bytes 56
  1.4 1.3 %pack.1 = (bf16[2,128,256]{2,1,0:T(8,128)(2,1)S(1)}, bf16[2,128,256]{2,1,0:T(8,128)(2,1)S(1)}, bf16[2,128,256]{2,1,0:T(8,128)(2,1)S(1)}, bf16[2,128,256]{2,1,0:T...) custom-call(s32[2,4]{1,0:T(2,128)S(1)} %bitcast.36, ...), custom_call_target="tpu_custom_call" | custom-call | tf_op jit(solution)/shard_map/pack/pallas_call | solution.py:359
  2.7 3.0 %collective-permute-start = (bf16[2,128,256]{2,1,0:T(8,128)(2,1)S(1)}, bf16[2,128,256]{2,1,0:T(8,128)(2,1)S(1)}, u32[]{:S(2)}, u32[]{:S(2)}) collective-permute-start(bf16[2,128,256]{2,1,0:T(8,128)(2,1)S(1)} %get-tuple-element.52), channel_id=1, source_target_pairs={{0,1},{1,0},{2,3},{3,2},{4,5},{5,4},{6,7},{7,6},{8,9},{9,8},{10,11... | collective-permute-start | bytes 393224 | tf_op jit(solution)/shard_map/ppermute | solution.py:339
  5.7 1.5 %collective-permute-start.1 = (bf16[2,128,256]{2,1,0:T(8,128)(2,1)S(1)}, bf16[2,128,256]{2,1,0:T(8,128)(2,1)S(1)}, u32[]{:S(2)}, u32[]{:S(2)}) collective-permute-start(bf16[2,128,256]{2,1,0:T(8,128)(2,1)S(1)} %get-tuple-element.53), channel_id=1, source_target_pairs={{0,2},{1,3},{2,0},{3,1},{4,6},{5,7},{6,4},{7,5},{8,10},{9,11},{10,... | collective-permute-start | bytes 393224 | tf_op jit(solution)/shard_map/ppermute | solution.py:339
  7.2 0.0 collective-permute-start.2
  7.2 1.9 %collective-permute-start.3 = (bf16[2,128,256]{2,1,0:T(8,128)(2,1)S(1)}, bf16[2,128,256]{2,1,0:T(8,128)(2,1)S(1)}, u32[]{:S(2)}, u32[]{:S(2)}) collective-permute-start(bf16[2,128,256]{2,1,0:T(8,128)(2,1)S(1)} %get-tuple-element.66), channel_id=1, source_target_pairs={{0,1},{1,0},{2,3},{3,2},{4,5},{5,4},{6,7},{7,6},{8,9},{9,8},{10,11... | collective-permute-start | bytes 393224 | tf_op jit(solution)/shard_map/ppermute | solution.py:339
  9.2 1.5 %collective-permute-start.4 = (bf16[2,128,256]{2,1,0:T(8,128)(2,1)S(1)}, bf16[2,128,256]{2,1,0:T(8,128)(2,1)S(1)}, u32[]{:S(2)}, u32[]{:S(2)}) collective-permute-start(bf16[2,128,256]{2,1,0:T(8,128)(2,1)S(1)} %get-tuple-element.67), channel_id=1, source_target_pairs={{0,2},{1,3},{2,0},{3,1},{4,6},{5,7},{6,4},{7,5},{8,10},{9,11},{10,... | collective-permute-start | bytes 393224 | tf_op jit(solution)/shard_map/ppermute | solution.py:339
  10.7 0.0 collective-permute-done.refs_0_
  10.7 2.3 %collective-permute-start.5 = (bf16[2,128,256]{2,1,0:T(8,128)(2,1)S(1)}, bf16[2,128,256]{2,1,0:T(8,128)(2,1)S(1)}, u32[]{:S(2)}, u32[]{:S(2)}) collective-permute-start(bf16[2,128,256]{2,1,0:T(8,128)(2,1)S(1)} %get-tuple-element.68), channel_id=1, source_target_pairs={{0,3},{1,2},{2,1},{3,0},{4,7},{5,6},{6,5},{7,4},{8,11},{9,10},{10,... | collective-permute-start | bytes 393224 | tf_op jit(solution)/shard_map/ppermute | solution.py:339
  13.0 0.0 copy-done
  13.0 1.0 %copy-done.2 = bf16[1,1,1024,256]{3,2,1,0:T(8,128)(2,1)S(1)} copy-done((bf16[1,1,1024,256]{3,2,1,0:T(8,128)(2,1)S(1)}, bf16[1,1,1024,256]{3,2,1,0:T(8,128)(2,1)}, u32[]{:S(2)}) %copy-start.2) | copy-done | bytes 524312
  14.1 0.0 copy-start.7
  14.1 0.0 copy-start.10
  14.1 0.5 prepare.1
  14.6 0.3 collective-permute-done.1.refs_1_
  14.9 0.0 collective-permute-done.2.refs_2_
  14.9 0.1 copy-done.3
  15.0 0.1 copy-done.4
  15.0 0.1 copy-done.5
  15.1 0.1 copy-done.6
  15.2 0.0 copy-done.7
  15.2 0.0 copy-done.10
  15.2 0.5 copy-done.9
  15.7 0.0 copy-done.8
  15.7 1.7 %first_layer.1 = (bf16[8,128,256]{2,1,0:T(8,128)(2,1)S(1)}, f32[1024,256]{1,0:T(8,128)S(1)}, bf16[256,1024]{1,0:T(8,128)(2,1)S(1)}, bf16[256,1024]{1,0:T(8,128)(...) custom-call(s32[4,8]{1,0:T(4,128)S(1)} %bitcast.32, ...), custom_call_target="tpu_custom_call" | custom-call | tf_op jit(solution)/shard_map/first_layer/pallas_call | solution.py:390
  17.4 0.0 collective-permute-done.3.refs_13_
  17.4 1.7 %collective-permute-done.4.refs_14_ = bf16[2,128,256]{2,1,0:T(8,128)(2,1)S(1)} collective-permute-done((bf16[2,128,256]{2,1,0:T(8,128)(2,1)S(1)}, bf16[2,128,256]{2,1,0:T(8,128)(2,1)S(1)}, u32[]{:S(2)}, u32[]{:S(2)}) %collective-permute-start.4) | collective-permute-done | bytes 131104 | tf_op jit(solution)/shard_map/ppermute | solution.py:339
  19.1 0.0 collective-permute-done.5.refs_15_
  19.1 0.0 copy-done.1
  19.1 3.8 %second_layer.1 = (bf16[8,128,256]{2,1,0:T(8,128)(2,1)S(1)}, bf16[576,256]{1,0:T(8,128)(2,1)S(1)}, bf16[576,256]{1,0:T(8,128)(2,1)S(1)}, bf16[8,128,256]{2,1,0:T(8,128)(2,1)S(1)}) custom-call(s32[4,8]{1,0:T(4,128)S(1)} %bitcast.33, bf16[512,256]{1,0:T(8,128)(2,1)S(1)} %get-tuple-element.56.refs_0_, bf16[256,512]{1,0:T(8,128)(2,1)S(1)} %get-tuple-element.57.refs_1_, ...), custom_call_target="tpu_custom_call" | custom-call | tf_op jit(solution)/shard_map/second_layer/pallas_call | solution.py:425
  22.8 0.1 collective-permute-start.6
  22.9 1.6 %collective-permute-done.6 = bf16[576,256]{1,0:T(8,128)(2,1)S(1)} collective-permute-done((bf16[576,256]{1,0:T(8,128)(2,1)S(1)}, bf16[576,256]{1,0:T(8,128)(2,1)S(1)}, u32[]{:S(2)}, u32[]{:S(2)}) %collective-permute-start.6) | collective-permute-done | bytes 294944 | tf_op jit(solution)/shard_map/ppermute | solution.py:350
  24.5 0.1 split.1
  24.6 1.3 %collective-permute-start.10 = (bf16[144,256]{1,0:T(8,128)(2,1)S(1)}, bf16[144,256]{1,0:T(8,128)(2,1)S(1)}, u32[]{:S(2)}, u32[]{:S(2)}) collective-permute-start(bf16[144,256]{1,0:T(8,128)(2,1)S(1)} %get-tuple-element.80), channel_id=1, source_target_pairs={{0,1},{1,0},{2,3},{3,2},{4,5},{5,4},{6,7},{7,6},{8,9},{9,8},{10,11... | collective-permute-start | bytes 221192 | tf_op jit(solution)/shard_map/ppermute | solution.py:339
  25.9 0.8 %collective-permute-start.11 = (bf16[144,256]{1,0:T(8,128)(2,1)S(1)}, bf16[144,256]{1,0:T(8,128)(2,1)S(1)}, u32[]{:S(2)}, u32[]{:S(2)}) collective-permute-start(bf16[144,256]{1,0:T(8,128)(2,1)S(1)} %get-tuple-element.81), channel_id=1, source_target_pairs={{0,2},{1,3},{2,0},{3,1},{4,6},{5,7},{6,4},{7,5},{8,10},{9,11},{10,... | collective-permute-start | bytes 221192 | tf_op jit(solution)/shard_map/ppermute | solution.py:339
  26.7 1.4 %collective-permute-start.12 = (bf16[144,256]{1,0:T(8,128)(2,1)S(1)}, bf16[144,256]{1,0:T(8,128)(2,1)S(1)}, u32[]{:S(2)}, u32[]{:S(2)}) collective-permute-start(bf16[144,256]{1,0:T(8,128)(2,1)S(1)} %get-tuple-element.82), channel_id=1, source_target_pairs={{0,3},{1,2},{2,1},{3,0},{4,7},{5,6},{6,5},{7,4},{8,11},{9,10},{10,... | collective-permute-start | bytes 221192 | tf_op jit(solution)/shard_map/ppermute | solution.py:339
  28.1 1.0 %store.1 = (bf16[8,128,256]{2,1,0:T(8,128)(2,1)}, bf16[8,128,256]{2,1,0:T(8,128)(2,1)}, f32[8,128]{1,0:T(8,128)S(1)}) custom-call(bf16[8,128,256]{2,1,0:T(8,128)(2,1)S(1)} %get-tuple-element.55.refs_6_.hidden, bf16[8,128,256]{2,1,0:T(8,128)(2,1)S(1)} %get-tuple-element.69.grad_hidden, bf16[144,256]{1,0:T(8,128)(2,1)S(1)} %get-tuple-element.72.after.refs_0_), custom_call_target="tpu_custom_call" | custom-call | tf_op jit(solution)/shard_map/store/pallas_call | solution.py:486
  29.1 0.0 collective-permute-done.10.refs_1_
  29.1 1.9 %collective-permute-done.11.refs_2_ = bf16[144,256]{1,0:T(8,128)(2,1)S(1)} collective-permute-done((bf16[144,256]{1,0:T(8,128)(2,1)S(1)}, bf16[144,256]{1,0:T(8,128)(2,1)S(1)}, u32[]{:S(2)}, u32[]{:S(2)}) %collective-permute-start.11) | collective-permute-done | bytes 73760 | tf_op jit(solution)/shard_map/ppermute | solution.py:339
  31.0 0.9 %collective-permute-done.12.refs_3_ = bf16[144,256]{1,0:T(8,128)(2,1)S(1)} collective-permute-done((bf16[144,256]{1,0:T(8,128)(2,1)S(1)}, bf16[144,256]{1,0:T(8,128)(2,1)S(1)}, u32[]{:S(2)}, u32[]{:S(2)}) %collective-permute-start.12) | collective-permute-done | bytes 73760 | tf_op jit(solution)/shard_map/ppermute | solution.py:339
  32.0 3.7 %collective-permute-start.15 = (bf16[144,256]{1,0:T(8,128)(2,1)S(1)}, bf16[144,256]{1,0:T(8,128)(2,1)S(1)}, u32[]{:S(2)}, u32[]{:S(2)}) collective-permute-start(bf16[144,256]{1,0:T(8,128)(2,1)S(1)} %add.2.refs_0_), channel_id=1, source_target_pairs={{0,24},{4,28},{8,16},{12,20},{16,8},{20,12},{24,0},{28,4},{1,25},{... | collective-permute-start | bytes 221192 | tf_op jit(solution)/shard_map/ppermute | solution.py:347
  35.7 1.6 %collective-permute-start.7 = (bf16[2,128,256]{2,1,0:T(8,128)(2,1)S(1)}, bf16[2,128,256]{2,1,0:T(8,128)(2,1)S(1)}, u32[]{:S(2)}, u32[]{:S(2)}) collective-permute-start(bf16[2,128,256]{2,1,0:T(8,128)(2,1)S(1)} %get-tuple-element.76), channel_id=1, source_target_pairs={{0,1},{1,0},{2,3},{3,2},{4,5},{5,4},{6,7},{7,6},{8,9},{9,8},{10,11... | collective-permute-start | bytes 393224 | tf_op jit(solution)/shard_map/ppermute | solution.py:339
  37.2 0.0 collective-permute-start.14
  37.2 0.8 %collective-permute-start.13 = (bf16[144,256]{1,0:T(8,128)(2,1)S(1)}, bf16[144,256]{1,0:T(8,128)(2,1)S(1)}, u32[]{:S(2)}, u32[]{:S(2)}) collective-permute-start(bf16[144,256]{1,0:T(8,128)(2,1)S(1)} %add.2.refs_0_), channel_id=1, source_target_pairs={{0,8},{4,12},{8,0},{12,4},{16,24},{20,28},{24,16},{28,20},{1,9},{5... | collective-permute-start | bytes 221192 | tf_op jit(solution)/shard_map/ppermute | solution.py:347
  38.0 0.7 %collective-permute-start.8 = (bf16[2,128,256]{2,1,0:T(8,128)(2,1)S(1)}, bf16[2,128,256]{2,1,0:T(8,128)(2,1)S(1)}, u32[]{:S(2)}, u32[]{:S(2)}) collective-permute-start(bf16[2,128,256]{2,1,0:T(8,128)(2,1)S(1)} %get-tuple-element.77), channel_id=1, source_target_pairs={{0,2},{1,3},{2,0},{3,1},{4,6},{5,7},{6,4},{7,5},{8,10},{9,11},{10,... | collective-permute-start | bytes 393224 | tf_op jit(solution)/shard_map/ppermute | solution.py:339
  38.7 0.2 collective-permute-done.15.refs_3_
  38.9 1.7 %collective-permute-start.9 = (bf16[2,128,256]{2,1,0:T(8,128)(2,1)S(1)}, bf16[2,128,256]{2,1,0:T(8,128)(2,1)S(1)}, u32[]{:S(2)}, u32[]{:S(2)}) collective-permute-start(bf16[2,128,256]{2,1,0:T(8,128)(2,1)S(1)} %get-tuple-element.78), channel_id=1, source_target_pairs={{0,3},{1,2},{2,1},{3,0},{4,7},{5,6},{6,5},{7,4},{8,11},{9,10},{10,... | collective-permute-start | bytes 393224 | tf_op jit(solution)/shard_map/ppermute | solution.py:339
  40.5 2.0 %collective-permute-done.14.refs_2_ = bf16[144,256]{1,0:T(8,128)(2,1)S(1)} collective-permute-done((bf16[144,256]{1,0:T(8,128)(2,1)S(1)}, bf16[144,256]{1,0:T(8,128)(2,1)S(1)}, u32[]{:S(2)}, u32[]{:S(2)}) %collective-permute-start.14) | collective-permute-done | bytes 73760 | tf_op jit(solution)/shard_map/ppermute | solution.py:347
  42.5 0.0 collective-permute-done.13.refs_1_
  42.5 1.2 %collective-permute-start.18 = (bf16[144,256]{1,0:T(8,128)(2,1)S(1)}, bf16[144,256]{1,0:T(8,128)(2,1)S(1)}, u32[]{:S(2)}, u32[]{:S(2)}) collective-permute-start(bf16[144,256]{1,0:T(8,128)(2,1)S(1)} %add.3.own), channel_id=1, source_target_pairs={{0,3},{1,2},{2,1},{3,0},{4,7},{5,6},{6,5},{7,4},{8,11},{9,10},{10,... | collective-permute-start | bytes 221192 | tf_op jit(solution)/shard_map/ppermute | solution.py:339
  43.8 0.8 %collective-permute-start.17 = (bf16[144,256]{1,0:T(8,128)(2,1)S(1)}, bf16[144,256]{1,0:T(8,128)(2,1)S(1)}, u32[]{:S(2)}, u32[]{:S(2)}) collective-permute-start(bf16[144,256]{1,0:T(8,128)(2,1)S(1)} %add.3.own), channel_id=1, source_target_pairs={{0,2},{1,3},{2,0},{3,1},{4,6},{5,7},{6,4},{7,5},{8,10},{9,11},{10,... | collective-permute-start | bytes 221192 | tf_op jit(solution)/shard_map/ppermute | solution.py:339
  44.6 0.0 collective-permute-done.7.refs_0_
  44.6 1.5 %collective-permute-start.16 = (bf16[144,256]{1,0:T(8,128)(2,1)S(1)}, bf16[144,256]{1,0:T(8,128)(2,1)S(1)}, u32[]{:S(2)}, u32[]{:S(2)}) collective-permute-start(bf16[144,256]{1,0:T(8,128)(2,1)S(1)} %add.3.own), channel_id=1, source_target_pairs={{0,1},{1,0},{2,3},{3,2},{4,5},{5,4},{6,7},{7,6},{8,9},{9,8},{10,11... | collective-permute-start | bytes 221192 | tf_op jit(solution)/shard_map/ppermute | solution.py:339
  46.1 0.0 collective-permute-done.8.refs_1_
  46.1 0.0 collective-permute-done.9.refs_2_
  46.1 1.5 %aux.1 = (bf16[8,128,256]{2,1,0:T(8,128)(2,1)}, f32[8,128]{1,0:T(8,128)S(1)}) custom-call(s32[2,4]{1,0:T(2,128)S(1)} %bitcast.37, bf16[2,128,256]{2,1,0:T(8,128)(2,1)S(1)} %collective-permute-done.7.refs_0_, bf16[2,128,256]{2,1,0:T(8,128)(2,1)S(1)} %collective-permute-done.8.refs_1_, bf16[2,128,256]{2,1,0:T(8,128)(2,1)S(1)} %collective-permute-done.9.refs_2_), custom_call_target="tpu_custom_call" | custom-call | flops 1000000 | bytes 1000000 | tf_op jit(solution)/shard_map/aux/pallas_call | solution.py:505
  47.6 0.3 collective-permute-done.18.refs_2_
  47.9 0.7 %collective-permute-done.17.refs_1_ = bf16[144,256]{1,0:T(8,128)(2,1)S(1)} collective-permute-done((bf16[144,256]{1,0:T(8,128)(2,1)S(1)}, bf16[144,256]{1,0:T(8,128)(2,1)S(1)}, u32[]{:S(2)}, u32[]{:S(2)}) %collective-permute-start.17) | collective-permute-done | bytes 73760 | tf_op jit(solution)/shard_map/ppermute | solution.py:339
  48.7 0.3 collective-permute-done.16.refs_0_
  49.0 0.1 collective-permute-start.19
  49.1 1.6 %collective-permute-done.19.other = bf16[576,256]{1,0:T(8,128)(2,1)S(1)} collective-permute-done((bf16[576,256]{1,0:T(8,128)(2,1)S(1)}, bf16[576,256]{1,0:T(8,128)(2,1)S(1)}, u32[]{:S(2)}, u32[]{:S(2)}) %collective-permute-start.19) | collective-permute-done | bytes 294944 | tf_op jit(solution)/shard_map/ppermute | solution.py:350
  50.6 1.0 %finish.1 = (f32[256,256]{1,0:T(8,128)}, f32[256,256]{1,0:T(8,128)}, f32[256,256]{1,0:T(8,128)}, f32[256,256]{1,0:T(8,128)}, f32[32,256]{1,0:T(8,128)}, /*index=5*/f32[1,1]{1,0:T(1,128)}) custom-call(bf16[576,256]{1,0:T(8,128)(2,1)S(1)} %bitcast.25, bf16[576,256]{1,0:T(8,128)(2,1)S(1)} %collective-permute-done.19.other), custom_call_target="tpu_custom_call" | custom-call | tf_op jit(solution)/shard_map/finish/pallas_call | solution.py:530
  (12 shorter events, 0.2 us)
Async XLA Ops:
  0.6 12.4 %copy-start = (bf16[1,1,8,4,128,128]{5,4,3,2,1,0:T(8,128)(2,1)S(1)}, bf16[1,1,8,4,128,128]{5,4,3,2,1,0:T(8,128)(2,1)}, u32[]{:S(2)}) copy-start(bf16[1,1,8,4,128,128]{5,4,3,2,1,0:T(8,128)(2,1)} %param.16) | copy-start | bytes 3145732
  0.7 0.8 %copy-start.11 = (s32[1,1,4,2]{2,3,1,0:T(2,128)S(1)}, s32[1,1,4,2]{2,3,1,0:T(2,128)}, u32[]{:S(2)}) copy-start(s32[1,1,4,2]{2,3,1,0:T(2,128)} %param.18) | copy-start | bytes 100
  2.7 8.0 %collective-permute-start = (bf16[2,128,256]{2,1,0:T(8,128)(2,1)S(1)}, bf16[2,128,256]{2,1,0:T(8,128)(2,1)S(1)}, u32[]{:S(2)}, u32[]{:S(2)}) collective-permute-start(bf16[2,128,256]{2,1,0:T(8,128)(2,1)S(1)} %get-tuple-element.52), channel_id=1, source_target_pairs={{0,1},{1,0},{2,3},{3,2},{4,5},{5,4},{6,7},{7,6},{8,9},{9,8},{10,11... | collective-permute-start | bytes 393224 | tf_op jit(solution)/shard_map/ppermute | solution.py:339
  5.7 9.2 %collective-permute-start.1 = (bf16[2,128,256]{2,1,0:T(8,128)(2,1)S(1)}, bf16[2,128,256]{2,1,0:T(8,128)(2,1)S(1)}, u32[]{:S(2)}, u32[]{:S(2)}) collective-permute-start(bf16[2,128,256]{2,1,0:T(8,128)(2,1)S(1)} %get-tuple-element.53), channel_id=1, source_target_pairs={{0,2},{1,3},{2,0},{3,1},{4,6},{5,7},{6,4},{7,5},{8,10},{9,11},{10,... | collective-permute-start | bytes 393224 | tf_op jit(solution)/shard_map/ppermute | solution.py:339
  7.2 7.7 %collective-permute-start.2 = (bf16[2,128,256]{2,1,0:T(8,128)(2,1)S(1)}, bf16[2,128,256]{2,1,0:T(8,128)(2,1)S(1)}, u32[]{:S(2)}, u32[]{:S(2)}) collective-permute-start(bf16[2,128,256]{2,1,0:T(8,128)(2,1)S(1)} %get-tuple-element.54), channel_id=1, source_target_pairs={{0,3},{1,2},{2,1},{3,0},{4,7},{5,6},{6,5},{7,4},{8,11},{9,10},{10,... | collective-permute-start | bytes 393224 | tf_op jit(solution)/shard_map/ppermute | solution.py:339
  7.2 10.1 %collective-permute-start.3 = (bf16[2,128,256]{2,1,0:T(8,128)(2,1)S(1)}, bf16[2,128,256]{2,1,0:T(8,128)(2,1)S(1)}, u32[]{:S(2)}, u32[]{:S(2)}) collective-permute-start(bf16[2,128,256]{2,1,0:T(8,128)(2,1)S(1)} %get-tuple-element.66), channel_id=1, source_target_pairs={{0,1},{1,0},{2,3},{3,2},{4,5},{5,4},{6,7},{7,6},{8,9},{9,8},{10,11... | collective-permute-start | bytes 393224 | tf_op jit(solution)/shard_map/ppermute | solution.py:339
  9.2 9.9 %collective-permute-start.4 = (bf16[2,128,256]{2,1,0:T(8,128)(2,1)S(1)}, bf16[2,128,256]{2,1,0:T(8,128)(2,1)S(1)}, u32[]{:S(2)}, u32[]{:S(2)}) collective-permute-start(bf16[2,128,256]{2,1,0:T(8,128)(2,1)S(1)} %get-tuple-element.67), channel_id=1, source_target_pairs={{0,2},{1,3},{2,0},{3,1},{4,6},{5,7},{6,4},{7,5},{8,10},{9,11},{10,... | collective-permute-start | bytes 393224 | tf_op jit(solution)/shard_map/ppermute | solution.py:339
  10.7 8.4 %collective-permute-start.5 = (bf16[2,128,256]{2,1,0:T(8,128)(2,1)S(1)}, bf16[2,128,256]{2,1,0:T(8,128)(2,1)S(1)}, u32[]{:S(2)}, u32[]{:S(2)}) collective-permute-start(bf16[2,128,256]{2,1,0:T(8,128)(2,1)S(1)} %get-tuple-element.68), channel_id=1, source_target_pairs={{0,3},{1,2},{2,1},{3,0},{4,7},{5,6},{6,5},{7,4},{8,11},{9,10},{10,... | collective-permute-start | bytes 393224 | tf_op jit(solution)/shard_map/ppermute | solution.py:339
  13.0 1.0 %copy-start.2 = (bf16[1,1,1024,256]{3,2,1,0:T(8,128)(2,1)S(1)}, bf16[1,1,1024,256]{3,2,1,0:T(8,128)(2,1)}, u32[]{:S(2)}) copy-start(bf16[1,1,1024,256]{3,2,1,0:T(8,128)(2,1)} %param.13) | copy-start | bytes 1572868
  14.1 0.9 %copy-start.3 = (bf16[256,256]{1,0:T(8,128)(2,1)S(1)}, bf16[256,256]{1,0:T(8,128)(2,1)}, u32[]{:S(2)}) copy-start(bf16[256,256]{1,0:T(8,128)(2,1)} %wn.1) | copy-start | bytes 393220
  14.1 1.0 %copy-start.4 = (bf16[256,256]{1,0:T(8,128)(2,1)S(1)}, bf16[256,256]{1,0:T(8,128)(2,1)}, u32[]{:S(2)}) copy-start(bf16[256,256]{1,0:T(8,128)(2,1)} %ws.1) | copy-start | bytes 393220
  14.1 1.0 %copy-start.5 = (bf16[256,256]{1,0:T(8,128)(2,1)S(1)}, bf16[256,256]{1,0:T(8,128)(2,1)}, u32[]{:S(2)}) copy-start(bf16[256,256]{1,0:T(8,128)(2,1)} %wn_next.1) | copy-start | bytes 393220
  14.1 1.1 %copy-start.6 = (bf16[256,256]{1,0:T(8,128)(2,1)S(1)}, bf16[256,256]{1,0:T(8,128)(2,1)}, u32[]{:S(2)}) copy-start(bf16[256,256]{1,0:T(8,128)(2,1)} %ws_next.1) | copy-start | bytes 393220
  14.1 1.1 %copy-start.7 = (bf16[256,32]{0,1:T(8,128)(2,1)S(1)}, bf16[256,32]{0,1:T(8,128)(2,1)}, u32[]{:S(2)}) copy-start(bf16[256,32]{0,1:T(8,128)(2,1)} %param.25) | copy-start | bytes 49156
  14.1 1.1 %copy-start.10 = (s32[1,1,1024]{2,1,0:T(1,128)S(1)}, s32[1,1,1024]{2,1,0:T(1,128)}, u32[]{:S(2)}) copy-start(s32[1,1,1024]{2,1,0:T(1,128)} %param.20) | copy-start | bytes 12292
  14.9 0.7 %copy-start.9 = (s32[1,1,1024]{2,1,0:T(1,128)S(1)}, s32[1,1,1024]{2,1,0:T(1,128)}, u32[]{:S(2)}) copy-start(s32[1,1,1024]{2,1,0:T(1,128)} %param.19) | copy-start | bytes 12292
  14.9 0.8 %copy-start.8 = (s32[1,1,8,4]{2,3,1,0:T(4,128)S(1)}, s32[1,1,8,4]{2,3,1,0:T(4,128)}, u32[]{:S(2)}) copy-start(s32[1,1,8,4]{2,3,1,0:T(4,128)} %param.17) | copy-start | bytes 388
  15.7 3.4 %copy-start.1 = (bf16[1,1,1024,256]{3,2,1,0:T(8,128)(2,1)S(1)}, bf16[1,1,1024,256]{3,2,1,0:T(8,128)(2,1)}, u32[]{:S(2)}) copy-start(bf16[1,1,1024,256]{3,2,1,0:T(8,128)(2,1)} %param.15) | copy-start | bytes 1572868
  22.8 1.6 %collective-permute-start.6 = (bf16[576,256]{1,0:T(8,128)(2,1)S(1)}, bf16[576,256]{1,0:T(8,128)(2,1)S(1)}, u32[]{:S(2)}, u32[]{:S(2)}) collective-permute-start(bf16[576,256]{1,0:T(8,128)(2,1)S(1)} %get-tuple-element.71), channel_id=1, source_target_pairs={{0,4},{4,0},{8,12},{12,8},{16,20},{20,16},{24,28},{28,24},{1,5},{5... | collective-permute-start | bytes 884744 | tf_op jit(solution)/shard_map/ppermute | solution.py:350
  24.6 4.5 %collective-permute-start.10 = (bf16[144,256]{1,0:T(8,128)(2,1)S(1)}, bf16[144,256]{1,0:T(8,128)(2,1)S(1)}, u32[]{:S(2)}, u32[]{:S(2)}) collective-permute-start(bf16[144,256]{1,0:T(8,128)(2,1)S(1)} %get-tuple-element.80), channel_id=1, source_target_pairs={{0,1},{1,0},{2,3},{3,2},{4,5},{5,4},{6,7},{7,6},{8,9},{9,8},{10,11... | collective-permute-start | bytes 221192 | tf_op jit(solution)/shard_map/ppermute | solution.py:339
  25.9 5.1 %collective-permute-start.11 = (bf16[144,256]{1,0:T(8,128)(2,1)S(1)}, bf16[144,256]{1,0:T(8,128)(2,1)S(1)}, u32[]{:S(2)}, u32[]{:S(2)}) collective-permute-start(bf16[144,256]{1,0:T(8,128)(2,1)S(1)} %get-tuple-element.81), channel_id=1, source_target_pairs={{0,2},{1,3},{2,0},{3,1},{4,6},{5,7},{6,4},{7,5},{8,10},{9,11},{10,... | collective-permute-start | bytes 221192 | tf_op jit(solution)/shard_map/ppermute | solution.py:339
  26.7 5.3 %collective-permute-start.12 = (bf16[144,256]{1,0:T(8,128)(2,1)S(1)}, bf16[144,256]{1,0:T(8,128)(2,1)S(1)}, u32[]{:S(2)}, u32[]{:S(2)}) collective-permute-start(bf16[144,256]{1,0:T(8,128)(2,1)S(1)} %get-tuple-element.82), channel_id=1, source_target_pairs={{0,3},{1,2},{2,1},{3,0},{4,7},{5,6},{6,5},{7,4},{8,11},{9,10},{10,... | collective-permute-start | bytes 221192 | tf_op jit(solution)/shard_map/ppermute | solution.py:339
  32.0 6.9 %collective-permute-start.15 = (bf16[144,256]{1,0:T(8,128)(2,1)S(1)}, bf16[144,256]{1,0:T(8,128)(2,1)S(1)}, u32[]{:S(2)}, u32[]{:S(2)}) collective-permute-start(bf16[144,256]{1,0:T(8,128)(2,1)S(1)} %add.2.refs_0_), channel_id=1, source_target_pairs={{0,24},{4,28},{8,16},{12,20},{16,8},{20,12},{24,0},{28,4},{1,25},{... | collective-permute-start | bytes 221192 | tf_op jit(solution)/shard_map/ppermute | solution.py:347
  35.7 8.9 %collective-permute-start.7 = (bf16[2,128,256]{2,1,0:T(8,128)(2,1)S(1)}, bf16[2,128,256]{2,1,0:T(8,128)(2,1)S(1)}, u32[]{:S(2)}, u32[]{:S(2)}) collective-permute-start(bf16[2,128,256]{2,1,0:T(8,128)(2,1)S(1)} %get-tuple-element.76), channel_id=1, source_target_pairs={{0,1},{1,0},{2,3},{3,2},{4,5},{5,4},{6,7},{7,6},{8,9},{9,8},{10,11... | collective-permute-start | bytes 393224 | tf_op jit(solution)/shard_map/ppermute | solution.py:339
  37.2 5.3 %collective-permute-start.14 = (bf16[144,256]{1,0:T(8,128)(2,1)S(1)}, bf16[144,256]{1,0:T(8,128)(2,1)S(1)}, u32[]{:S(2)}, u32[]{:S(2)}) collective-permute-start(bf16[144,256]{1,0:T(8,128)(2,1)S(1)} %add.2.refs_0_), channel_id=1, source_target_pairs={{0,16},{4,20},{8,24},{12,28},{16,0},{20,4},{24,8},{28,12},{1,17},{... | collective-permute-start | bytes 221192 | tf_op jit(solution)/shard_map/ppermute | solution.py:347
  37.2 5.3 %collective-permute-start.13 = (bf16[144,256]{1,0:T(8,128)(2,1)S(1)}, bf16[144,256]{1,0:T(8,128)(2,1)S(1)}, u32[]{:S(2)}, u32[]{:S(2)}) collective-permute-start(bf16[144,256]{1,0:T(8,128)(2,1)S(1)} %add.2.refs_0_), channel_id=1, source_target_pairs={{0,8},{4,12},{8,0},{12,4},{16,24},{20,28},{24,16},{28,20},{1,9},{5... | collective-permute-start | bytes 221192 | tf_op jit(solution)/shard_map/ppermute | solution.py:347
  38.0 8.1 %collective-permute-start.8 = (bf16[2,128,256]{2,1,0:T(8,128)(2,1)S(1)}, bf16[2,128,256]{2,1,0:T(8,128)(2,1)S(1)}, u32[]{:S(2)}, u32[]{:S(2)}) collective-permute-start(bf16[2,128,256]{2,1,0:T(8,128)(2,1)S(1)} %get-tuple-element.77), channel_id=1, source_target_pairs={{0,2},{1,3},{2,0},{3,1},{4,6},{5,7},{6,4},{7,5},{8,10},{9,11},{10,... | collective-permute-start | bytes 393224 | tf_op jit(solution)/shard_map/ppermute | solution.py:339
  38.9 7.2 %collective-permute-start.9 = (bf16[2,128,256]{2,1,0:T(8,128)(2,1)S(1)}, bf16[2,128,256]{2,1,0:T(8,128)(2,1)S(1)}, u32[]{:S(2)}, u32[]{:S(2)}) collective-permute-start(bf16[2,128,256]{2,1,0:T(8,128)(2,1)S(1)} %get-tuple-element.78), channel_id=1, source_target_pairs={{0,3},{1,2},{2,1},{3,0},{4,7},{5,6},{6,5},{7,4},{8,11},{9,10},{10,... | collective-permute-start | bytes 393224 | tf_op jit(solution)/shard_map/ppermute | solution.py:339
  42.5 5.4 %collective-permute-start.18 = (bf16[144,256]{1,0:T(8,128)(2,1)S(1)}, bf16[144,256]{1,0:T(8,128)(2,1)S(1)}, u32[]{:S(2)}, u32[]{:S(2)}) collective-permute-start(bf16[144,256]{1,0:T(8,128)(2,1)S(1)} %add.3.own), channel_id=1, source_target_pairs={{0,3},{1,2},{2,1},{3,0},{4,7},{5,6},{6,5},{7,4},{8,11},{9,10},{10,... | collective-permute-start | bytes 221192 | tf_op jit(solution)/shard_map/ppermute | solution.py:339
  43.8 4.9 %collective-permute-start.17 = (bf16[144,256]{1,0:T(8,128)(2,1)S(1)}, bf16[144,256]{1,0:T(8,128)(2,1)S(1)}, u32[]{:S(2)}, u32[]{:S(2)}) collective-permute-start(bf16[144,256]{1,0:T(8,128)(2,1)S(1)} %add.3.own), channel_id=1, source_target_pairs={{0,2},{1,3},{2,0},{3,1},{4,6},{5,7},{6,4},{7,5},{8,10},{9,11},{10,... | collective-permute-start | bytes 221192 | tf_op jit(solution)/shard_map/ppermute | solution.py:339
  44.6 4.4 %collective-permute-start.16 = (bf16[144,256]{1,0:T(8,128)(2,1)S(1)}, bf16[144,256]{1,0:T(8,128)(2,1)S(1)}, u32[]{:S(2)}, u32[]{:S(2)}) collective-permute-start(bf16[144,256]{1,0:T(8,128)(2,1)S(1)} %add.3.own), channel_id=1, source_target_pairs={{0,1},{1,0},{2,3},{3,2},{4,5},{5,4},{6,7},{7,6},{8,9},{9,8},{10,11... | collective-permute-start | bytes 221192 | tf_op jit(solution)/shard_map/ppermute | solution.py:339
  49.0 1.6 %collective-permute-start.19 = (bf16[576,256]{1,0:T(8,128)(2,1)S(1)}, bf16[576,256]{1,0:T(8,128)(2,1)S(1)}, u32[]{:S(2)}, u32[]{:S(2)}) collective-permute-start(bf16[576,256]{1,0:T(8,128)(2,1)S(1)} %bitcast.24), channel_id=1, source_target_pairs={{0,4},{4,0},{8,12},{12,8},{16,20},{20,16},{24,28},{28,24},{1,5},{5... | collective-permute-start | bytes 884744 | tf_op jit(solution)/shard_map/ppermute | solution.py:350

commit v5 on v4

--- a/solution.py
+++ b/solution.py
@@ -78,8 +78,8 @@
     peers, slots, blocks, picks, rows, width = dims
     inc = peers - 1
     feat_in, refs = refs[:inc], refs[inc:]
-    own2, slope1, agg_t, hidden_t, w, w_t, head_kept, bins_kept, flags_kept = refs[:9]
-    table, sources, sem = refs[9:]
+    own2, slope1, agg_t, hidden_t, self2, w, w_t, head_kept, bins_kept, flags_kept = refs[:10]
+    table, sources, sem = refs[10:]
     g = lax.axis_index("grp")
     listed = pltpu.make_async_copy(sources_in, sources, sem)
     listed.start()
@@ -90,8 +90,7 @@
     head_kept[...] = head[...]
     bins_kept[...] = bins[...]
     flags_kept[...] = flags[...]
-    w[:width] = wn_next[...]
-    w[width:] = ws_next[...]
+    w[...] = wn_next[...]
     w_t[:, :width] = wn_next[...].T
     w_t[:, width:] = ws_next[...].T
     listed.wait()
@@ -115,12 +114,13 @@
         hidden = value.astype(BF16)
         own2[pl.ds(i * pair, pair)] = hidden.reshape(pair, rows, width)
         hidden_t[:, at] = hidden.T
+        self2[at] = dot(hidden, ws_next[...])
 
 
 def second_kernel(dims, sources_in, *refs):
     peers, slots, blocks, picks, rows, width, bins_count, pay_rows = dims
     inc = peers - 1
-    (w, w_t, head, bins, flags, aux), refs = refs[:6], refs[6:]
+    (w, w_t, head, bins, flags, aux, self2), refs = refs[:7], refs[7:]
     (own2, slope1, tiles, tiles_t, agg1_t, feat_t, hidden_t), refs = refs[:7], refs[7:]
     past_in, refs = refs[:inc], refs[inc:]
     (grad_hidden, keep, send, back), refs = refs[:4], refs[4:]
@@ -154,14 +154,8 @@
     at = [pl.ds(i * pair, pair) for i in chunks]
     gates = []
     for i in chunks:
-        both = jnp.concatenate(
-            [
-                jnp.concatenate(aggs[i * pair : (i + 1) * pair], axis=0),
-                table[at[i]].reshape(span, width),
-            ],
-            axis=1,
-        )
-        gates.append(gate_of(dot(both, w[...])))
+        agg = jnp.concatenate(aggs[i * pair : (i + 1) * pair], axis=0)
+        gates.append(gate_of(dot(agg, w[...]) + self2[pl.ds(i * span, span)]))
     hidden = [value.astype(BF16) for value, _ in gates]
     logits = [dot_by_transpose(head[...], hidden[i]) for i in chunks]
     glogs = []
@@ -387,21 +381,22 @@
     )(feat, tiles, packed[2 * inc])
 
     pair_shape = (blocks // 2, 1, 2 * rows)
-    own2, slope1, agg_t, hidden_t, w, w_t, head, bins, flags = pl.pallas_call(
+    own2, slope1, agg_t, hidden_t, self2, w, w_t, head, bins, flags = pl.pallas_call(
         functools.partial(first_kernel, (peers, slots, blocks, picks, rows, width)),
         out_shape=[
             shape(block_shape),
             shape((nodes, width), F32),
             shape(turned),
             shape(turned),
-            shape((2 * width, width)),
+            shape((nodes, width), F32),
+            shape(square),
             shape((width, 2 * width)),
             shape((bins_count, width)),
             shape(pair_shape, jnp.int32),
             shape(pair_shape, jnp.int32),
         ],
         in_specs=[HBM] + [VMEM] * (9 + inc),
-        out_specs=[VMEM] * 9,
+        out_specs=[VMEM] * 10,
         scratch_shapes=[
             pltpu.VMEM((table, rows, width), BF16),
             pltpu.SMEM((picks, blocks), jnp.int32),
@@ -432,7 +427,7 @@
             shape((half, width)),
             shape((peers * slots, rows, width)),
         ],
-        in_specs=[HBM] + [VMEM] * (13 + inc),
+        in_specs=[HBM] + [VMEM] * (14 + inc),
         out_specs=[VMEM] * 4,
         scratch_shapes=[
             pltpu.SMEM((picks, blocks), jnp.int32),
@@ -452,6 +447,7 @@
         bins,
         flags,
         aux_history.reshape(block_shape),
+        self2,
         own2,
         slope1,
         tiles,

time: 51.9 us -> 51.9 us (level)
  waiting for transfers between devices: 11.5 us -> 10.9 us
    ppermute x15, waiting for transfers between devices: 6.23 us -> 5.68 us  [over_grp(): return lax.ppermute(value, 'grp', grp_pairs(step))]
    pallas_call x1, Pallas kernels: 1.67 us -> 2.21 us  [shards(): pl.pallas_call(functools.partial(first_kernel, (peers, slots, blocks, pic...]
  transfers between devices with their start and end apart: 20 -> 20, of which waited for: 11 -> 11; matrix products, arithmetic and copies ran while one was open for 0% -> 0% of each run, Pallas kernels for 9% -> 10%
where the time goes in v5:
time: 51.9 us; the launch traced here: 51.6 us
  starting transfers between devices  26 us (50%)
  Pallas kernels  11.4 us (22%)
  waiting for transfers between devices  10.9 us (21%)
  local copies, waits for them, and re-layouts  2.58 us (5%)
  between operations  0.8 us (2%)
    ppermute x15, starting transfers between devices, over_grp(): return lax.ppermute(value, 'grp', grp_pairs(step))  21.2 us
    ppermute x15, waiting for transfers between devices, over_grp(): return lax.ppermute(value, 'grp', grp_pairs(step))  5.68 us
    ppermute x3, starting transfers between devices, over_z(): return lax.ppermute(value, 'clus', pairs)  4.71 us
    pallas_call x1, Pallas kernels, shards(): pl.pallas_call(functools.partial(second_kernel, (peers, slots, blocks, pi...  3.69 us
    ppermute x2, waiting for transfers between devices, over_core(): return lax.ppermute(value, 'clus', [(i, i ^ 1) for i in range(clus_count)])  3.14 us
    unnamed x24, local copies, waits for them, and re-layouts  2.58 us
    pallas_call x1, Pallas kernels, shards(): pl.pallas_call(functools.partial(first_kernel, (peers, slots, blocks, pic...  2.21 us
    ppermute x3, waiting for transfers between devices, over_z(): return lax.ppermute(value, 'clus', pairs)  2.06 us
  transfers between devices with their start and end apart: 20, of which 11 were waited for; matrix products, arithmetic and copies ran while one was open for 0% of the time, Pallas kernels for 10%

profile of v5, /device:TPU:0, one launch (start us, length us, event | category | flops | bytes accessed | tf_op | source)
XLA Modules:
  0.0 51.6 jit_solution(2544982827820608389)
XLA Ops:
  0.6 0.0 copy-start
  0.7 0.0 copy-start.11
  0.7 0.8 %copy-done.11 = s32[1,1,4,2]{2,3,1,0:T(2,128)S(1)} copy-done((s32[1,1,4,2]{2,3,1,0:T(2,128)S(1)}, s32[1,1,4,2]{2,3,1,0:T(2,128)}, u32[]{:S(2)}) %copy-start.11) | copy-done | bytes 56
  1.4 1.3 %pack.1 = (bf16[2,128,256]{2,1,0:T(8,128)(2,1)S(1)}, bf16[2,128,256]{2,1,0:T(8,128)(2,1)S(1)}, bf16[2,128,256]{2,1,0:T(8,128)(2,1)S(1)}, bf16[2,128,256]{2,1,0:T...) custom-call(s32[2,4]{1,0:T(2,128)S(1)} %bitcast.36, ...), custom_call_target="tpu_custom_call" | custom-call | tf_op jit(solution)/shard_map/pack/pallas_call | solution.py:353
  2.7 3.0 %collective-permute-start = (bf16[2,128,256]{2,1,0:T(8,128)(2,1)S(1)}, bf16[2,128,256]{2,1,0:T(8,128)(2,1)S(1)}, u32[]{:S(2)}, u32[]{:S(2)}) collective-permute-start(bf16[2,128,256]{2,1,0:T(8,128)(2,1)S(1)} %get-tuple-element.53), channel_id=1, source_target_pairs={{0,1},{1,0},{2,3},{3,2},{4,5},{5,4},{6,7},{7,6},{8,9},{9,8},{10,11... | collective-permute-start | bytes 393224 | tf_op jit(solution)/shard_map/ppermute | solution.py:333
  5.7 1.5 %collective-permute-start.1 = (bf16[2,128,256]{2,1,0:T(8,128)(2,1)S(1)}, bf16[2,128,256]{2,1,0:T(8,128)(2,1)S(1)}, u32[]{:S(2)}, u32[]{:S(2)}) collective-permute-start(bf16[2,128,256]{2,1,0:T(8,128)(2,1)S(1)} %get-tuple-element.54), channel_id=1, source_target_pairs={{0,2},{1,3},{2,0},{3,1},{4,6},{5,7},{6,4},{7,5},{8,10},{9,11},{10,... | collective-permute-start | bytes 393224 | tf_op jit(solution)/shard_map/ppermute | solution.py:333
  7.2 0.0 collective-permute-start.2
  7.2 1.9 %collective-permute-start.3 = (bf16[2,128,256]{2,1,0:T(8,128)(2,1)S(1)}, bf16[2,128,256]{2,1,0:T(8,128)(2,1)S(1)}, u32[]{:S(2)}, u32[]{:S(2)}) collective-permute-start(bf16[2,128,256]{2,1,0:T(8,128)(2,1)S(1)} %get-tuple-element.68), channel_id=1, source_target_pairs={{0,1},{1,0},{2,3},{3,2},{4,5},{5,4},{6,7},{7,6},{8,9},{9,8},{10,11... | collective-permute-start | bytes 393224 | tf_op jit(solution)/shard_map/ppermute | solution.py:333
  9.2 1.5 %collective-permute-start.4 = (bf16[2,128,256]{2,1,0:T(8,128)(2,1)S(1)}, bf16[2,128,256]{2,1,0:T(8,128)(2,1)S(1)}, u32[]{:S(2)}, u32[]{:S(2)}) collective-permute-start(bf16[2,128,256]{2,1,0:T(8,128)(2,1)S(1)} %get-tuple-element.69), channel_id=1, source_target_pairs={{0,2},{1,3},{2,0},{3,1},{4,6},{5,7},{6,4},{7,5},{8,10},{9,11},{10,... | collective-permute-start | bytes 393224 | tf_op jit(solution)/shard_map/ppermute | solution.py:333
  10.7 0.0 collective-permute-done.refs_0_
  10.7 2.3 %collective-permute-start.5 = (bf16[2,128,256]{2,1,0:T(8,128)(2,1)S(1)}, bf16[2,128,256]{2,1,0:T(8,128)(2,1)S(1)}, u32[]{:S(2)}, u32[]{:S(2)}) collective-permute-start(bf16[2,128,256]{2,1,0:T(8,128)(2,1)S(1)} %get-tuple-element.70), channel_id=1, source_target_pairs={{0,3},{1,2},{2,1},{3,0},{4,7},{5,6},{6,5},{7,4},{8,11},{9,10},{10,... | collective-permute-start | bytes 393224 | tf_op jit(solution)/shard_map/ppermute | solution.py:333
  13.0 0.0 copy-done
  13.0 1.0 %copy-done.2 = bf16[1,1,1024,256]{3,2,1,0:T(8,128)(2,1)S(1)} copy-done((bf16[1,1,1024,256]{3,2,1,0:T(8,128)(2,1)S(1)}, bf16[1,1,1024,256]{3,2,1,0:T(8,128)(2,1)}, u32[]{:S(2)}) %copy-start.2) | copy-done | bytes 524312
  14.1 0.0 copy-start.7
  14.1 0.0 copy-start.10
  14.1 0.5 prepare.1
  14.6 0.3 collective-permute-done.1.refs_1_
  14.9 0.0 collective-permute-done.2.refs_2_
  14.9 0.1 copy-done.3
  15.0 0.1 copy-done.4
  15.0 0.1 copy-done.5
  15.1 0.1 copy-done.6
  15.2 0.0 copy-done.7
  15.2 0.0 copy-done.10
  15.2 0.5 copy-done.9
  15.7 0.0 copy-done.8
  15.7 2.2 %first_layer.1 = (bf16[8,128,256]{2,1,0:T(8,128)(2,1)S(1)}, f32[1024,256]{1,0:T(8,128)S(1)}, bf16[256,1024]{1,0:T(8,128)(2,1)S(1)}, bf16[256,1024]{1,0:T(8,128)(...) custom-call(s32[4,8]{1,0:T(4,128)S(1)} %bitcast.32, ...), custom_call_target="tpu_custom_call" | custom-call | tf_op jit(solution)/shard_map/first_layer/pallas_call | solution.py:384
  17.9 0.0 collective-permute-done.3.refs_14_
  17.9 1.2 %collective-permute-done.4.refs_15_ = bf16[2,128,256]{2,1,0:T(8,128)(2,1)S(1)} collective-permute-done((bf16[2,128,256]{2,1,0:T(8,128)(2,1)S(1)}, bf16[2,128,256]{2,1,0:T(8,128)(2,1)S(1)}, u32[]{:S(2)}, u32[]{:S(2)}) %collective-permute-start.4) | collective-permute-done | bytes 131104 | tf_op jit(solution)/shard_map/ppermute | solution.py:333
  19.1 0.0 collective-permute-done.5.refs_16_
  19.1 0.0 copy-done.1
  19.1 3.7 %second_layer.1 = (bf16[8,128,256]{2,1,0:T(8,128)(2,1)S(1)}, bf16[576,256]{1,0:T(8,128)(2,1)S(1)}, bf16[576,256]{1,0:T(8,128)(2,1)S(1)}, bf16[8,128,256]{2,1,0:T(8,128)(2,1)S(1)}) custom-call(s32[4,8]{1,0:T(4,128)S(1)} %bitcast.33, bf16[256,256]{1,0:T(8,128)(2,1)S(1)} %get-tuple-element.57.refs_0_, bf16[256,512]{1,0:T(8,128)(2,1)S(1)} %get-tuple-element.58.refs_1_, ...), custom_call_target="tpu_custom_call" | custom-call | tf_op jit(solution)/shard_map/second_layer/pallas_call | solution.py:420
  22.8 0.1 collective-permute-start.6
  22.9 1.6 %collective-permute-done.6 = bf16[576,256]{1,0:T(8,128)(2,1)S(1)} collective-permute-done((bf16[576,256]{1,0:T(8,128)(2,1)S(1)}, bf16[576,256]{1,0:T(8,128)(2,1)S(1)}, u32[]{:S(2)}, u32[]{:S(2)}) %collective-permute-start.6) | collective-permute-done | bytes 294944 | tf_op jit(solution)/shard_map/ppermute | solution.py:344
  24.4 0.1 split.1
  24.5 1.3 %collective-permute-start.10 = (bf16[144,256]{1,0:T(8,128)(2,1)S(1)}, bf16[144,256]{1,0:T(8,128)(2,1)S(1)}, u32[]{:S(2)}, u32[]{:S(2)}) collective-permute-start(bf16[144,256]{1,0:T(8,128)(2,1)S(1)} %get-tuple-element.82), channel_id=1, source_target_pairs={{0,1},{1,0},{2,3},{3,2},{4,5},{5,4},{6,7},{7,6},{8,9},{9,8},{10,11... | collective-permute-start | bytes 221192 | tf_op jit(solution)/shard_map/ppermute | solution.py:333
  25.8 0.8 %collective-permute-start.11 = (bf16[144,256]{1,0:T(8,128)(2,1)S(1)}, bf16[144,256]{1,0:T(8,128)(2,1)S(1)}, u32[]{:S(2)}, u32[]{:S(2)}) collective-permute-start(bf16[144,256]{1,0:T(8,128)(2,1)S(1)} %get-tuple-element.83), channel_id=1, source_target_pairs={{0,2},{1,3},{2,0},{3,1},{4,6},{5,7},{6,4},{7,5},{8,10},{9,11},{10,... | collective-permute-start | bytes 221192 | tf_op jit(solution)/shard_map/ppermute | solution.py:333
  26.6 1.4 %collective-permute-start.12 = (bf16[144,256]{1,0:T(8,128)(2,1)S(1)}, bf16[144,256]{1,0:T(8,128)(2,1)S(1)}, u32[]{:S(2)}, u32[]{:S(2)}) collective-permute-start(bf16[144,256]{1,0:T(8,128)(2,1)S(1)} %get-tuple-element.84), channel_id=1, source_target_pairs={{0,3},{1,2},{2,1},{3,0},{4,7},{5,6},{6,5},{7,4},{8,11},{9,10},{10,... | collective-permute-start | bytes 221192 | tf_op jit(solution)/shard_map/ppermute | solution.py:333
  28.1 1.0 %store.1 = (bf16[8,128,256]{2,1,0:T(8,128)(2,1)}, bf16[8,128,256]{2,1,0:T(8,128)(2,1)}, f32[8,128]{1,0:T(8,128)S(1)}) custom-call(bf16[8,128,256]{2,1,0:T(8,128)(2,1)S(1)} %get-tuple-element.56.refs_7_.hidden, bf16[8,128,256]{2,1,0:T(8,128)(2,1)S(1)} %get-tuple-element.71.grad_hidden, bf16[144,256]{1,0:T(8,128)(2,1)S(1)} %get-tuple-element.74.after.refs_0_), custom_call_target="tpu_custom_call" | custom-call | tf_op jit(solution)/shard_map/store/pallas_call | solution.py:482
  29.1 0.0 collective-permute-done.10.refs_1_
  29.1 1.7 %collective-permute-done.11.refs_2_ = bf16[144,256]{1,0:T(8,128)(2,1)S(1)} collective-permute-done((bf16[144,256]{1,0:T(8,128)(2,1)S(1)}, bf16[144,256]{1,0:T(8,128)(2,1)S(1)}, u32[]{:S(2)}, u32[]{:S(2)}) %collective-permute-start.11) | collective-permute-done | bytes 73760 | tf_op jit(solution)/shard_map/ppermute | solution.py:333
  30.7 1.1 %collective-permute-done.12.refs_3_ = bf16[144,256]{1,0:T(8,128)(2,1)S(1)} collective-permute-done((bf16[144,256]{1,0:T(8,128)(2,1)S(1)}, bf16[144,256]{1,0:T(8,128)(2,1)S(1)}, u32[]{:S(2)}, u32[]{:S(2)}) %collective-permute-start.12) | collective-permute-done | bytes 73760 | tf_op jit(solution)/shard_map/ppermute | solution.py:333
  31.9 3.7 %collective-permute-start.15 = (bf16[144,256]{1,0:T(8,128)(2,1)S(1)}, bf16[144,256]{1,0:T(8,128)(2,1)S(1)}, u32[]{:S(2)}, u32[]{:S(2)}) collective-permute-start(bf16[144,256]{1,0:T(8,128)(2,1)S(1)} %add.2.refs_0_), channel_id=1, source_target_pairs={{0,24},{4,28},{8,16},{12,20},{16,8},{20,12},{24,0},{28,4},{1,25},{... | collective-permute-start | bytes 221192 | tf_op jit(solution)/shard_map/ppermute | solution.py:341
  35.6 1.6 %collective-permute-start.7 = (bf16[2,128,256]{2,1,0:T(8,128)(2,1)S(1)}, bf16[2,128,256]{2,1,0:T(8,128)(2,1)S(1)}, u32[]{:S(2)}, u32[]{:S(2)}) collective-permute-start(bf16[2,128,256]{2,1,0:T(8,128)(2,1)S(1)} %get-tuple-element.78), channel_id=1, source_target_pairs={{0,1},{1,0},{2,3},{3,2},{4,5},{5,4},{6,7},{7,6},{8,9},{9,8},{10,11... | collective-permute-start | bytes 393224 | tf_op jit(solution)/shard_map/ppermute | solution.py:333
  37.2 0.0 collective-permute-start.14
  37.2 1.0 %collective-permute-start.13 = (bf16[144,256]{1,0:T(8,128)(2,1)S(1)}, bf16[144,256]{1,0:T(8,128)(2,1)S(1)}, u32[]{:S(2)}, u32[]{:S(2)}) collective-permute-start(bf16[144,256]{1,0:T(8,128)(2,1)S(1)} %add.2.refs_0_), channel_id=1, source_target_pairs={{0,8},{4,12},{8,0},{12,4},{16,24},{20,28},{24,16},{28,20},{1,9},{5... | collective-permute-start | bytes 221192 | tf_op jit(solution)/shard_map/ppermute | solution.py:341
  38.2 0.5 collective-permute-start.8
  38.7 0.1 collective-permute-done.15.refs_3_
  38.8 1.7 %collective-permute-start.9 = (bf16[2,128,256]{2,1,0:T(8,128)(2,1)S(1)}, bf16[2,128,256]{2,1,0:T(8,128)(2,1)S(1)}, u32[]{:S(2)}, u32[]{:S(2)}) collective-permute-start(bf16[2,128,256]{2,1,0:T(8,128)(2,1)S(1)} %get-tuple-element.80), channel_id=1, source_target_pairs={{0,3},{1,2},{2,1},{3,0},{4,7},{5,6},{6,5},{7,4},{8,11},{9,10},{10,... | collective-permute-start | bytes 393224 | tf_op jit(solution)/shard_map/ppermute | solution.py:333
  40.5 1.9 %collective-permute-done.14.refs_2_ = bf16[144,256]{1,0:T(8,128)(2,1)S(1)} collective-permute-done((bf16[144,256]{1,0:T(8,128)(2,1)S(1)}, bf16[144,256]{1,0:T(8,128)(2,1)S(1)}, u32[]{:S(2)}, u32[]{:S(2)}) %collective-permute-start.14) | collective-permute-done | bytes 73760 | tf_op jit(solution)/shard_map/ppermute | solution.py:341
  42.4 0.0 collective-permute-done.13.refs_1_
  42.5 1.2 %collective-permute-start.18 = (bf16[144,256]{1,0:T(8,128)(2,1)S(1)}, bf16[144,256]{1,0:T(8,128)(2,1)S(1)}, u32[]{:S(2)}, u32[]{:S(2)}) collective-permute-start(bf16[144,256]{1,0:T(8,128)(2,1)S(1)} %add.3.own), channel_id=1, source_target_pairs={{0,3},{1,2},{2,1},{3,0},{4,7},{5,6},{6,5},{7,4},{8,11},{9,10},{10,... | collective-permute-start | bytes 221192 | tf_op jit(solution)/shard_map/ppermute | solution.py:333
  43.7 0.8 %collective-permute-start.17 = (bf16[144,256]{1,0:T(8,128)(2,1)S(1)}, bf16[144,256]{1,0:T(8,128)(2,1)S(1)}, u32[]{:S(2)}, u32[]{:S(2)}) collective-permute-start(bf16[144,256]{1,0:T(8,128)(2,1)S(1)} %add.3.own), channel_id=1, source_target_pairs={{0,2},{1,3},{2,0},{3,1},{4,6},{5,7},{6,4},{7,5},{8,10},{9,11},{10,... | collective-permute-start | bytes 221192 | tf_op jit(solution)/shard_map/ppermute | solution.py:333
  44.5 0.0 collective-permute-done.7.refs_0_
  44.5 1.5 %collective-permute-start.16 = (bf16[144,256]{1,0:T(8,128)(2,1)S(1)}, bf16[144,256]{1,0:T(8,128)(2,1)S(1)}, u32[]{:S(2)}, u32[]{:S(2)}) collective-permute-start(bf16[144,256]{1,0:T(8,128)(2,1)S(1)} %add.3.own), channel_id=1, source_target_pairs={{0,1},{1,0},{2,3},{3,2},{4,5},{5,4},{6,7},{7,6},{8,9},{9,8},{10,11... | collective-permute-start | bytes 221192 | tf_op jit(solution)/shard_map/ppermute | solution.py:333
  46.0 0.0 collective-permute-done.8.refs_1_
  46.0 0.0 collective-permute-done.9.refs_2_
  46.0 1.5 %aux.1 = (bf16[8,128,256]{2,1,0:T(8,128)(2,1)}, f32[8,128]{1,0:T(8,128)S(1)}) custom-call(s32[2,4]{1,0:T(2,128)S(1)} %bitcast.37, bf16[2,128,256]{2,1,0:T(8,128)(2,1)S(1)} %collective-permute-done.7.refs_0_, bf16[2,128,256]{2,1,0:T(8,128)(2,1)S(1)} %collective-permute-done.8.refs_1_, bf16[2,128,256]{2,1,0:T(8,128)(2,1)S(1)} %collective-permute-done.9.refs_2_), custom_call_target="tpu_custom_call" | custom-call | flops 1000000 | bytes 1000000 | tf_op jit(solution)/shard_map/aux/pallas_call | solution.py:501
  47.5 0.3 collective-permute-done.18.refs_2_
  47.9 0.7 %collective-permute-done.17.refs_1_ = bf16[144,256]{1,0:T(8,128)(2,1)S(1)} collective-permute-done((bf16[144,256]{1,0:T(8,128)(2,1)S(1)}, bf16[144,256]{1,0:T(8,128)(2,1)S(1)}, u32[]{:S(2)}, u32[]{:S(2)}) %collective-permute-start.17) | collective-permute-done | bytes 73760 | tf_op jit(solution)/shard_map/ppermute | solution.py:333
  48.6 0.3 collective-permute-done.16.refs_0_
  48.9 0.1 collective-permute-start.19
  49.0 1.6 %collective-permute-done.19.other = bf16[576,256]{1,0:T(8,128)(2,1)S(1)} collective-permute-done((bf16[576,256]{1,0:T(8,128)(2,1)S(1)}, bf16[576,256]{1,0:T(8,128)(2,1)S(1)}, u32[]{:S(2)}, u32[]{:S(2)}) %collective-permute-start.19) | collective-permute-done | bytes 294944 | tf_op jit(solution)/shard_map/ppermute | solution.py:344
  50.6 1.0 %finish.1 = (f32[256,256]{1,0:T(8,128)}, f32[256,256]{1,0:T(8,128)}, f32[256,256]{1,0:T(8,128)}, f32[256,256]{1,0:T(8,128)}, f32[32,256]{1,0:T(8,128)}, /*index=5*/f32[1,1]{1,0:T(1,128)}) custom-call(bf16[576,256]{1,0:T(8,128)(2,1)S(1)} %bitcast.25, bf16[576,256]{1,0:T(8,128)(2,1)S(1)} %collective-permute-done.19.other), custom_call_target="tpu_custom_call" | custom-call | tf_op jit(solution)/shard_map/finish/pallas_call | solution.py:526
  (12 shorter events, 0.2 us)
Async XLA Ops:
  0.6 12.4 %copy-start = (bf16[1,1,8,4,128,128]{5,4,3,2,1,0:T(8,128)(2,1)S(1)}, bf16[1,1,8,4,128,128]{5,4,3,2,1,0:T(8,128)(2,1)}, u32[]{:S(2)}) copy-start(bf16[1,1,8,4,128,128]{5,4,3,2,1,0:T(8,128)(2,1)} %param.16) | copy-start | bytes 3145732
  0.7 0.8 %copy-start.11 = (s32[1,1,4,2]{2,3,1,0:T(2,128)S(1)}, s32[1,1,4,2]{2,3,1,0:T(2,128)}, u32[]{:S(2)}) copy-start(s32[1,1,4,2]{2,3,1,0:T(2,128)} %param.18) | copy-start | bytes 100
  2.7 8.0 %collective-permute-start = (bf16[2,128,256]{2,1,0:T(8,128)(2,1)S(1)}, bf16[2,128,256]{2,1,0:T(8,128)(2,1)S(1)}, u32[]{:S(2)}, u32[]{:S(2)}) collective-permute-start(bf16[2,128,256]{2,1,0:T(8,128)(2,1)S(1)} %get-tuple-element.53), channel_id=1, source_target_pairs={{0,1},{1,0},{2,3},{3,2},{4,5},{5,4},{6,7},{7,6},{8,9},{9,8},{10,11... | collective-permute-start | bytes 393224 | tf_op jit(solution)/shard_map/ppermute | solution.py:333
  5.7 9.2 %collective-permute-start.1 = (bf16[2,128,256]{2,1,0:T(8,128)(2,1)S(1)}, bf16[2,128,256]{2,1,0:T(8,128)(2,1)S(1)}, u32[]{:S(2)}, u32[]{:S(2)}) collective-permute-start(bf16[2,128,256]{2,1,0:T(8,128)(2,1)S(1)} %get-tuple-element.54), channel_id=1, source_target_pairs={{0,2},{1,3},{2,0},{3,1},{4,6},{5,7},{6,4},{7,5},{8,10},{9,11},{10,... | collective-permute-start | bytes 393224 | tf_op jit(solution)/shard_map/ppermute | solution.py:333
  7.2 7.7 %collective-permute-start.2 = (bf16[2,128,256]{2,1,0:T(8,128)(2,1)S(1)}, bf16[2,128,256]{2,1,0:T(8,128)(2,1)S(1)}, u32[]{:S(2)}, u32[]{:S(2)}) collective-permute-start(bf16[2,128,256]{2,1,0:T(8,128)(2,1)S(1)} %get-tuple-element.55), channel_id=1, source_target_pairs={{0,3},{1,2},{2,1},{3,0},{4,7},{5,6},{6,5},{7,4},{8,11},{9,10},{10,... | collective-permute-start | bytes 393224 | tf_op jit(solution)/shard_map/ppermute | solution.py:333
  7.2 10.7 %collective-permute-start.3 = (bf16[2,128,256]{2,1,0:T(8,128)(2,1)S(1)}, bf16[2,128,256]{2,1,0:T(8,128)(2,1)S(1)}, u32[]{:S(2)}, u32[]{:S(2)}) collective-permute-start(bf16[2,128,256]{2,1,0:T(8,128)(2,1)S(1)} %get-tuple-element.68), channel_id=1, source_target_pairs={{0,1},{1,0},{2,3},{3,2},{4,5},{5,4},{6,7},{7,6},{8,9},{9,8},{10,11... | collective-permute-start | bytes 393224 | tf_op jit(solution)/shard_map/ppermute | solution.py:333
  9.2 9.9 %collective-permute-start.4 = (bf16[2,128,256]{2,1,0:T(8,128)(2,1)S(1)}, bf16[2,128,256]{2,1,0:T(8,128)(2,1)S(1)}, u32[]{:S(2)}, u32[]{:S(2)}) collective-permute-start(bf16[2,128,256]{2,1,0:T(8,128)(2,1)S(1)} %get-tuple-element.69), channel_id=1, source_target_pairs={{0,2},{1,3},{2,0},{3,1},{4,6},{5,7},{6,4},{7,5},{8,10},{9,11},{10,... | collective-permute-start | bytes 393224 | tf_op jit(solution)/shard_map/ppermute | solution.py:333
  10.7 8.4 %collective-permute-start.5 = (bf16[2,128,256]{2,1,0:T(8,128)(2,1)S(1)}, bf16[2,128,256]{2,1,0:T(8,128)(2,1)S(1)}, u32[]{:S(2)}, u32[]{:S(2)}) collective-permute-start(bf16[2,128,256]{2,1,0:T(8,128)(2,1)S(1)} %get-tuple-element.70), channel_id=1, source_target_pairs={{0,3},{1,2},{2,1},{3,0},{4,7},{5,6},{6,5},{7,4},{8,11},{9,10},{10,... | collective-permute-start | bytes 393224 | tf_op jit(solution)/shard_map/ppermute | solution.py:333
  13.0 1.0 %copy-start.2 = (bf16[1,1,1024,256]{3,2,1,0:T(8,128)(2,1)S(1)}, bf16[1,1,1024,256]{3,2,1,0:T(8,128)(2,1)}, u32[]{:S(2)}) copy-start(bf16[1,1,1024,256]{3,2,1,0:T(8,128)(2,1)} %param.13) | copy-start | bytes 1572868
  14.1 0.9 %copy-start.3 = (bf16[256,256]{1,0:T(8,128)(2,1)S(1)}, bf16[256,256]{1,0:T(8,128)(2,1)}, u32[]{:S(2)}) copy-start(bf16[256,256]{1,0:T(8,128)(2,1)} %wn.1) | copy-start | bytes 393220
  14.1 1.0 %copy-start.4 = (bf16[256,256]{1,0:T(8,128)(2,1)S(1)}, bf16[256,256]{1,0:T(8,128)(2,1)}, u32[]{:S(2)}) copy-start(bf16[256,256]{1,0:T(8,128)(2,1)} %ws.1) | copy-start | bytes 393220
  14.1 1.0 %copy-start.5 = (bf16[256,256]{1,0:T(8,128)(2,1)S(1)}, bf16[256,256]{1,0:T(8,128)(2,1)}, u32[]{:S(2)}) copy-start(bf16[256,256]{1,0:T(8,128)(2,1)} %wn_next.1) | copy-start | bytes 393220
  14.1 1.1 %copy-start.6 = (bf16[256,256]{1,0:T(8,128)(2,1)S(1)}, bf16[256,256]{1,0:T(8,128)(2,1)}, u32[]{:S(2)}) copy-start(bf16[256,256]{1,0:T(8,128)(2,1)} %ws_next.1) | copy-start | bytes 393220
  14.1 1.1 %copy-start.7 = (bf16[256,32]{0,1:T(8,128)(2,1)S(1)}, bf16[256,32]{0,1:T(8,128)(2,1)}, u32[]{:S(2)}) copy-start(bf16[256,32]{0,1:T(8,128)(2,1)} %param.25) | copy-start | bytes 49156
  14.1 1.1 %copy-start.10 = (s32[1,1,1024]{2,1,0:T(1,128)S(1)}, s32[1,1,1024]{2,1,0:T(1,128)}, u32[]{:S(2)}) copy-start(s32[1,1,1024]{2,1,0:T(1,128)} %param.20) | copy-start | bytes 12292
  14.9 0.7 %copy-start.9 = (s32[1,1,1024]{2,1,0:T(1,128)S(1)}, s32[1,1,1024]{2,1,0:T(1,128)}, u32[]{:S(2)}) copy-start(s32[1,1,1024]{2,1,0:T(1,128)} %param.19) | copy-start | bytes 12292
  14.9 0.8 %copy-start.8 = (s32[1,1,8,4]{2,3,1,0:T(4,128)S(1)}, s32[1,1,8,4]{2,3,1,0:T(4,128)}, u32[]{:S(2)}) copy-start(s32[1,1,8,4]{2,3,1,0:T(4,128)} %param.17) | copy-start | bytes 388
  15.7 3.4 %copy-start.1 = (bf16[1,1,1024,256]{3,2,1,0:T(8,128)(2,1)S(1)}, bf16[1,1,1024,256]{3,2,1,0:T(8,128)(2,1)}, u32[]{:S(2)}) copy-start(bf16[1,1,1024,256]{3,2,1,0:T(8,128)(2,1)} %param.15) | copy-start | bytes 1572868
  22.8 1.6 %collective-permute-start.6 = (bf16[576,256]{1,0:T(8,128)(2,1)S(1)}, bf16[576,256]{1,0:T(8,128)(2,1)S(1)}, u32[]{:S(2)}, u32[]{:S(2)}) collective-permute-start(bf16[576,256]{1,0:T(8,128)(2,1)S(1)} %get-tuple-element.73), channel_id=1, source_target_pairs={{0,4},{4,0},{8,12},{12,8},{16,20},{20,16},{24,28},{28,24},{1,5},{5... | collective-permute-start | bytes 884744 | tf_op jit(solution)/shard_map/ppermute | solution.py:344
  24.5 4.5 %collective-permute-start.10 = (bf16[144,256]{1,0:T(8,128)(2,1)S(1)}, bf16[144,256]{1,0:T(8,128)(2,1)S(1)}, u32[]{:S(2)}, u32[]{:S(2)}) collective-permute-start(bf16[144,256]{1,0:T(8,128)(2,1)S(1)} %get-tuple-element.82), channel_id=1, source_target_pairs={{0,1},{1,0},{2,3},{3,2},{4,5},{5,4},{6,7},{7,6},{8,9},{9,8},{10,11... | collective-permute-start | bytes 221192 | tf_op jit(solution)/shard_map/ppermute | solution.py:333
  25.8 4.9 %collective-permute-start.11 = (bf16[144,256]{1,0:T(8,128)(2,1)S(1)}, bf16[144,256]{1,0:T(8,128)(2,1)S(1)}, u32[]{:S(2)}, u32[]{:S(2)}) collective-permute-start(bf16[144,256]{1,0:T(8,128)(2,1)S(1)} %get-tuple-element.83), channel_id=1, source_target_pairs={{0,2},{1,3},{2,0},{3,1},{4,6},{5,7},{6,4},{7,5},{8,10},{9,11},{10,... | collective-permute-start | bytes 221192 | tf_op jit(solution)/shard_map/ppermute | solution.py:333
  26.6 5.3 %collective-permute-start.12 = (bf16[144,256]{1,0:T(8,128)(2,1)S(1)}, bf16[144,256]{1,0:T(8,128)(2,1)S(1)}, u32[]{:S(2)}, u32[]{:S(2)}) collective-permute-start(bf16[144,256]{1,0:T(8,128)(2,1)S(1)} %get-tuple-element.84), channel_id=1, source_target_pairs={{0,3},{1,2},{2,1},{3,0},{4,7},{5,6},{6,5},{7,4},{8,11},{9,10},{10,... | collective-permute-start | bytes 221192 | tf_op jit(solution)/shard_map/ppermute | solution.py:333
  31.9 6.9 %collective-permute-start.15 = (bf16[144,256]{1,0:T(8,128)(2,1)S(1)}, bf16[144,256]{1,0:T(8,128)(2,1)S(1)}, u32[]{:S(2)}, u32[]{:S(2)}) collective-permute-start(bf16[144,256]{1,0:T(8,128)(2,1)S(1)} %add.2.refs_0_), channel_id=1, source_target_pairs={{0,24},{4,28},{8,16},{12,20},{16,8},{20,12},{24,0},{28,4},{1,25},{... | collective-permute-start | bytes 221192 | tf_op jit(solution)/shard_map/ppermute | solution.py:341
  35.6 8.9 %collective-permute-start.7 = (bf16[2,128,256]{2,1,0:T(8,128)(2,1)S(1)}, bf16[2,128,256]{2,1,0:T(8,128)(2,1)S(1)}, u32[]{:S(2)}, u32[]{:S(2)}) collective-permute-start(bf16[2,128,256]{2,1,0:T(8,128)(2,1)S(1)} %get-tuple-element.78), channel_id=1, source_target_pairs={{0,1},{1,0},{2,3},{3,2},{4,5},{5,4},{6,7},{7,6},{8,9},{9,8},{10,11... | collective-permute-start | bytes 393224 | tf_op jit(solution)/shard_map/ppermute | solution.py:333
  37.2 5.3 %collective-permute-start.14 = (bf16[144,256]{1,0:T(8,128)(2,1)S(1)}, bf16[144,256]{1,0:T(8,128)(2,1)S(1)}, u32[]{:S(2)}, u32[]{:S(2)}) collective-permute-start(bf16[144,256]{1,0:T(8,128)(2,1)S(1)} %add.2.refs_0_), channel_id=1, source_target_pairs={{0,16},{4,20},{8,24},{12,28},{16,0},{20,4},{24,8},{28,12},{1,17},{... | collective-permute-start | bytes 221192 | tf_op jit(solution)/shard_map/ppermute | solution.py:341
  37.2 5.3 %collective-permute-start.13 = (bf16[144,256]{1,0:T(8,128)(2,1)S(1)}, bf16[144,256]{1,0:T(8,128)(2,1)S(1)}, u32[]{:S(2)}, u32[]{:S(2)}) collective-permute-start(bf16[144,256]{1,0:T(8,128)(2,1)S(1)} %add.2.refs_0_), channel_id=1, source_target_pairs={{0,8},{4,12},{8,0},{12,4},{16,24},{20,28},{24,16},{28,20},{1,9},{5... | collective-permute-start | bytes 221192 | tf_op jit(solution)/shard_map/ppermute | solution.py:341
  38.2 7.8 %collective-permute-start.8 = (bf16[2,128,256]{2,1,0:T(8,128)(2,1)S(1)}, bf16[2,128,256]{2,1,0:T(8,128)(2,1)S(1)}, u32[]{:S(2)}, u32[]{:S(2)}) collective-permute-start(bf16[2,128,256]{2,1,0:T(8,128)(2,1)S(1)} %get-tuple-element.79), channel_id=1, source_target_pairs={{0,2},{1,3},{2,0},{3,1},{4,6},{5,7},{6,4},{7,5},{8,10},{9,11},{10,... | collective-permute-start | bytes 393224 | tf_op jit(solution)/shard_map/ppermute | solution.py:333
  38.8 7.2 %collective-permute-start.9 = (bf16[2,128,256]{2,1,0:T(8,128)(2,1)S(1)}, bf16[2,128,256]{2,1,0:T(8,128)(2,1)S(1)}, u32[]{:S(2)}, u32[]{:S(2)}) collective-permute-start(bf16[2,128,256]{2,1,0:T(8,128)(2,1)S(1)} %get-tuple-element.80), channel_id=1, source_target_pairs={{0,3},{1,2},{2,1},{3,0},{4,7},{5,6},{6,5},{7,4},{8,11},{9,10},{10,... | collective-permute-start | bytes 393224 | tf_op jit(solution)/shard_map/ppermute | solution.py:333
  42.5 5.4 %collective-permute-start.18 = (bf16[144,256]{1,0:T(8,128)(2,1)S(1)}, bf16[144,256]{1,0:T(8,128)(2,1)S(1)}, u32[]{:S(2)}, u32[]{:S(2)}) collective-permute-start(bf16[144,256]{1,0:T(8,128)(2,1)S(1)} %add.3.own), channel_id=1, source_target_pairs={{0,3},{1,2},{2,1},{3,0},{4,7},{5,6},{6,5},{7,4},{8,11},{9,10},{10,... | collective-permute-start | bytes 221192 | tf_op jit(solution)/shard_map/ppermute | solution.py:333
  43.7 4.9 %collective-permute-start.17 = (bf16[144,256]{1,0:T(8,128)(2,1)S(1)}, bf16[144,256]{1,0:T(8,128)(2,1)S(1)}, u32[]{:S(2)}, u32[]{:S(2)}) collective-permute-start(bf16[144,256]{1,0:T(8,128)(2,1)S(1)} %add.3.own), channel_id=1, source_target_pairs={{0,2},{1,3},{2,0},{3,1},{4,6},{5,7},{6,4},{7,5},{8,10},{9,11},{10,... | collective-permute-start | bytes 221192 | tf_op jit(solution)/shard_map/ppermute | solution.py:333
  44.5 4.4 %collective-permute-start.16 = (bf16[144,256]{1,0:T(8,128)(2,1)S(1)}, bf16[144,256]{1,0:T(8,128)(2,1)S(1)}, u32[]{:S(2)}, u32[]{:S(2)}) collective-permute-start(bf16[144,256]{1,0:T(8,128)(2,1)S(1)} %add.3.own), channel_id=1, source_target_pairs={{0,1},{1,0},{2,3},{3,2},{4,5},{5,4},{6,7},{7,6},{8,9},{9,8},{10,11... | collective-permute-start | bytes 221192 | tf_op jit(solution)/shard_map/ppermute | solution.py:333
  48.9 1.6 %collective-permute-start.19 = (bf16[576,256]{1,0:T(8,128)(2,1)S(1)}, bf16[576,256]{1,0:T(8,128)(2,1)S(1)}, u32[]{:S(2)}, u32[]{:S(2)}) collective-permute-start(bf16[576,256]{1,0:T(8,128)(2,1)S(1)} %bitcast.24), channel_id=1, source_target_pairs={{0,4},{4,0},{8,12},{12,8},{16,20},{20,16},{24,28},{28,24},{1,5},{5... | collective-permute-start | bytes 884744 | tf_op jit(solution)/shard_map/ppermute | solution.py:344

commit v6 on v5

--- a/solution.py
+++ b/solution.py
@@ -13,6 +13,7 @@
 SMEM = pl.BlockSpec(memory_space=pltpu.SMEM)
 HBM = pl.BlockSpec(memory_space=pltpu.HBM)
 CORES = 2
+LANES = 128
 PACK_LIMIT = 53 << 20
 PREP_LIMIT = 4 << 20
 AUX_FLOPS = 10**6
@@ -192,19 +193,25 @@
         (agg_t, grad_second),
         (hidden_t, grad_second),
     )
+    def put(at, values):
+        for i in range(width // LANES):
+            count = values.shape[0]
+            pay[pl.ds(at + i * count, count)] = values[:, i * LANES : (i + 1) * LANES]
+
+    folds = width // LANES
     for n, (left, grads) in enumerate(terms):
-        pay[pl.ds(n * width, width)] = (dot(left[...], grads) * scale).astype(BF16)
+        put(n * width * folds, (dot(left[...], grads) * scale).astype(BF16))
     part = jnp.sum(loss) * scale
     high = part.astype(BF16).astype(F32)
-    tail_rows = pay_rows - 4 * width - bins_count
-    lane = lax.broadcasted_iota(jnp.int32, (tail_rows, width), 0) * width + lax.broadcasted_iota(
-        jnp.int32, (tail_rows, width), 1
+    tail_rows = pay_rows - (4 * width + bins_count) * folds
+    lane = lax.broadcasted_iota(jnp.int32, (tail_rows, LANES), 0) * LANES + lax.broadcasted_iota(
+        jnp.int32, (tail_rows, LANES), 1
     )
     loss_rows = jnp.where(lane == 2 * device, high, 0.0) + jnp.where(
         lane == 2 * device + 1, part - high, 0.0
     )
-    pay[pl.ds(4 * width, bins_count)] = (ghw * scale).astype(BF16)
-    pay[pl.ds(4 * width + bins_count, tail_rows)] = loss_rows.astype(BF16)
+    put(4 * width * folds, (ghw * scale).astype(BF16))
+    pay[pl.ds((4 * width + bins_count) * folds, tail_rows)] = loss_rows.astype(BF16)
     half = pay_rows // CORES
     keep[...] = pay[pl.ds(pl.multiple_of(core * half, 16), half)]
     send[...] = pay[pl.ds(pl.multiple_of((1 - core) * half, 16), half)]
@@ -258,10 +265,17 @@
     core = lax.axis_index("clus") % CORES
     pay[pl.ds(pl.multiple_of(core * half, 16), half)] = mine[...]
     pay[pl.ds(pl.multiple_of((1 - core) * half, 16), half)] = other[...]
+    folds = width // LANES
+
+    def get(at, count):
+        parts = [pay[pl.ds(at + i * count, count)] for i in range(folds)]
+        return jnp.concatenate(parts, axis=1).astype(F32)
+
     for i in range(4):
-        outs[i][...] = pay[pl.ds(i * width, width)].astype(F32)
-    outs[4][...] = pay[pl.ds(4 * width, bins_count)].astype(F32)
-    loss_rows = pay[pl.ds(4 * width + bins_count, pay_rows - 4 * width - bins_count)].astype(F32)
+        outs[i][...] = get(i * width * folds, width)
+    outs[4][...] = get(4 * width * folds, bins_count)
+    used = (4 * width + bins_count) * folds
+    loss_rows = pay[pl.ds(used, pay_rows - used)].astype(F32)
     outs[5][0, 0] = jnp.sum(loss_rows)
 
 
@@ -311,7 +325,7 @@
     devices = clus_count * peers
     chips_z = clus_count // CORES
     inc = peers - 1
-    used = 4 * width + bins_count + -(-2 * devices // width)
+    used = (4 * width + bins_count) * (width // LANES) + -(-2 * devices // LANES)
     pay_rows = -(-used // (16 * CORES * peers)) * 16 * CORES * peers
     half = pay_rows // CORES
     chunk = half // peers
@@ -423,8 +437,8 @@
         ),
         out_shape=[
             shape(block_shape),
-            shape((half, width)),
-            shape((half, width)),
+            shape((half, LANES)),
+            shape((half, LANES)),
             shape((peers * slots, rows, width)),
         ],
         in_specs=[HBM] + [VMEM] * (14 + inc),
@@ -434,7 +448,7 @@
             pltpu.VMEM((table, rows, width), BF16),
             pltpu.VMEM(turned, BF16),
             pltpu.VMEM((table, rows, width), F32),
-            pltpu.VMEM((pay_rows, width), BF16),
+            pltpu.VMEM((pay_rows, LANES), BF16),
             pltpu.SemaphoreType.DMA,
         ],
         compiler_params=params,
@@ -461,18 +475,18 @@
     came = over_core(sent)
     parts = pl.pallas_call(
         functools.partial(split_kernel, peers),
-        out_shape=[shape((chunk, width))] * peers,
+        out_shape=[shape((chunk, LANES))] * peers,
         in_specs=[VMEM, VMEM],
         out_specs=[VMEM] * peers,
         compiler_params=small,
         name="split",
-    )(kept.reshape(peers, chunk, width), came.reshape(peers, chunk, width))
+    )(kept.reshape(peers, chunk, LANES), came.reshape(peers, chunk, LANES))
     from_grp = [over_grp(parts[i], i) for i in range(1, peers)]
 
     def add(*values):
         return pl.pallas_call(
             add_kernel,
-            out_shape=shape((chunk, width)),
+            out_shape=shape((chunk, LANES)),
             in_specs=[VMEM] * len(values),
             out_specs=VMEM,
             compiler_params=small,
@@ -516,19 +530,19 @@
     others = [over_grp(mine, i) for i in range(1, peers)]
     joined = pl.pallas_call(
         functools.partial(join_kernel, peers),
-        out_shape=shape((peers, chunk, width)),
+        out_shape=shape((peers, chunk, LANES)),
         in_specs=[VMEM] * (peers + 1),
         out_specs=VMEM,
         compiler_params=small,
         name="join",
-    )(mine, *others, token).reshape(half, width)
+    )(mine, *others, token).reshape(half, LANES)
     other_half = over_core(joined)
     grads = pl.pallas_call(
         functools.partial(finish_kernel, (width, bins_count, pay_rows)),
         out_shape=[shape(square, F32)] * 4 + [shape((bins_count, width), F32), shape((1, 1), F32)],
         in_specs=[VMEM] * 2,
         out_specs=[VMEM] * 5 + [SMEM],
-        scratch_shapes=[pltpu.VMEM((pay_rows, width), BF16)],
+        scratch_shapes=[pltpu.VMEM((pay_rows, LANES), BF16)],
         compiler_params=small,
         name="finish",
     )(joined, other_half)

time: 51.9 us -> 51.7 us (level)
  no operation moved by 1% of the time
where the time goes in v6:
time: 51.7 us; the launch traced here: 51.5 us
  starting transfers between devices  25.8 us (50%)
  Pallas kernels  11.4 us (22%)
  waiting for transfers between devices  10.9 us (21%)
  local copies, waits for them, and re-layouts  2.58 us (5%)
  between operations  0.8 us (2%)
    ppermute x15, starting transfers between devices, over_grp(): return lax.ppermute(value, 'grp', grp_pairs(step))  21 us
    ppermute x15, waiting for transfers between devices, over_grp(): return lax.ppermute(value, 'grp', grp_pairs(step))  5.6 us
    ppermute x3, starting transfers between devices, over_z(): return lax.ppermute(value, 'clus', pairs)  4.71 us
    pallas_call x1, Pallas kernels, shards(): pl.pallas_call(functools.partial(second_kernel, (peers, slots, blocks, pi...  3.71 us
    ppermute x2, waiting for transfers between devices, over_core(): return lax.ppermute(value, 'clus', [(i, i ^ 1) for i in range(clus_count)])  3.09 us
    unnamed x24, local copies, waits for them, and re-layouts  2.58 us
    pallas_call x1, Pallas kernels, shards(): pl.pallas_call(functools.partial(first_kernel, (peers, slots, blocks, pic...  2.21 us
    ppermute x3, waiting for transfers between devices, over_z(): return lax.ppermute(value, 'clus', pairs)  2.17 us
  transfers between devices with their start and end apart: 20, of which 11 were waited for; matrix products, arithmetic and copies ran while one was open for 0% of the time, Pallas kernels for 10%

profile of v6, /device:TPU:0, one launch (start us, length us, event | category | flops | bytes accessed | tf_op | source)
XLA Modules:
  0.0 51.5 jit_solution(15318073243286581324)
XLA Ops:
  0.6 0.0 copy-start
  0.7 0.0 copy-start.11
  0.7 0.8 %copy-done.11 = s32[1,1,4,2]{2,3,1,0:T(2,128)S(1)} copy-done((s32[1,1,4,2]{2,3,1,0:T(2,128)S(1)}, s32[1,1,4,2]{2,3,1,0:T(2,128)}, u32[]{:S(2)}) %copy-start.11) | copy-done | bytes 56
  1.4 1.3 %pack.1 = (bf16[2,128,256]{2,1,0:T(8,128)(2,1)S(1)}, bf16[2,128,256]{2,1,0:T(8,128)(2,1)S(1)}, bf16[2,128,256]{2,1,0:T(8,128)(2,1)S(1)}, bf16[2,128,256]{2,1,0:T...) custom-call(s32[2,4]{1,0:T(2,128)S(1)} %bitcast.36, ...), custom_call_target="tpu_custom_call" | custom-call | tf_op jit(solution)/shard_map/pack/pallas_call | solution.py:367
  2.7 3.0 %collective-permute-start = (bf16[2,128,256]{2,1,0:T(8,128)(2,1)S(1)}, bf16[2,128,256]{2,1,0:T(8,128)(2,1)S(1)}, u32[]{:S(2)}, u32[]{:S(2)}) collective-permute-start(bf16[2,128,256]{2,1,0:T(8,128)(2,1)S(1)} %get-tuple-element.53), channel_id=1, source_target_pairs={{0,1},{1,0},{2,3},{3,2},{4,5},{5,4},{6,7},{7,6},{8,9},{9,8},{10,11... | collective-permute-start | bytes 393224 | tf_op jit(solution)/shard_map/ppermute | solution.py:347
  5.7 1.5 %collective-permute-start.1 = (bf16[2,128,256]{2,1,0:T(8,128)(2,1)S(1)}, bf16[2,128,256]{2,1,0:T(8,128)(2,1)S(1)}, u32[]{:S(2)}, u32[]{:S(2)}) collective-permute-start(bf16[2,128,256]{2,1,0:T(8,128)(2,1)S(1)} %get-tuple-element.54), channel_id=1, source_target_pairs={{0,2},{1,3},{2,0},{3,1},{4,6},{5,7},{6,4},{7,5},{8,10},{9,11},{10,... | collective-permute-start | bytes 393224 | tf_op jit(solution)/shard_map/ppermute | solution.py:347
  7.2 0.0 collective-permute-start.2
  7.2 1.9 %collective-permute-start.3 = (bf16[2,128,256]{2,1,0:T(8,128)(2,1)S(1)}, bf16[2,128,256]{2,1,0:T(8,128)(2,1)S(1)}, u32[]{:S(2)}, u32[]{:S(2)}) collective-permute-start(bf16[2,128,256]{2,1,0:T(8,128)(2,1)S(1)} %get-tuple-element.68), channel_id=1, source_target_pairs={{0,1},{1,0},{2,3},{3,2},{4,5},{5,4},{6,7},{7,6},{8,9},{9,8},{10,11... | collective-permute-start | bytes 393224 | tf_op jit(solution)/shard_map/ppermute | solution.py:347
  9.2 1.5 %collective-permute-start.4 = (bf16[2,128,256]{2,1,0:T(8,128)(2,1)S(1)}, bf16[2,128,256]{2,1,0:T(8,128)(2,1)S(1)}, u32[]{:S(2)}, u32[]{:S(2)}) collective-permute-start(bf16[2,128,256]{2,1,0:T(8,128)(2,1)S(1)} %get-tuple-element.69), channel_id=1, source_target_pairs={{0,2},{1,3},{2,0},{3,1},{4,6},{5,7},{6,4},{7,5},{8,10},{9,11},{10,... | collective-permute-start | bytes 393224 | tf_op jit(solution)/shard_map/ppermute | solution.py:347
  10.7 0.0 collective-permute-done.refs_0_
  10.7 2.3 %collective-permute-start.5 = (bf16[2,128,256]{2,1,0:T(8,128)(2,1)S(1)}, bf16[2,128,256]{2,1,0:T(8,128)(2,1)S(1)}, u32[]{:S(2)}, u32[]{:S(2)}) collective-permute-start(bf16[2,128,256]{2,1,0:T(8,128)(2,1)S(1)} %get-tuple-element.70), channel_id=1, source_target_pairs={{0,3},{1,2},{2,1},{3,0},{4,7},{5,6},{6,5},{7,4},{8,11},{9,10},{10,... | collective-permute-start | bytes 393224 | tf_op jit(solution)/shard_map/ppermute | solution.py:347
  13.0 0.0 copy-done
  13.0 1.0 %copy-done.2 = bf16[1,1,1024,256]{3,2,1,0:T(8,128)(2,1)S(1)} copy-done((bf16[1,1,1024,256]{3,2,1,0:T(8,128)(2,1)S(1)}, bf16[1,1,1024,256]{3,2,1,0:T(8,128)(2,1)}, u32[]{:S(2)}) %copy-start.2) | copy-done | bytes 524312
  14.1 0.0 copy-start.7
  14.1 0.0 copy-start.10
  14.1 0.5 prepare.1
  14.6 0.3 collective-permute-done.1.refs_1_
  14.9 0.0 collective-permute-done.2.refs_2_
  14.9 0.1 copy-done.3
  15.0 0.1 copy-done.4
  15.0 0.1 copy-done.5
  15.1 0.1 copy-done.6
  15.2 0.0 copy-done.7
  15.2 0.0 copy-done.10
  15.2 0.5 copy-done.9
  15.7 0.0 copy-done.8
  15.7 2.2 %first_layer.1 = (bf16[8,128,256]{2,1,0:T(8,128)(2,1)S(1)}, f32[1024,256]{1,0:T(8,128)S(1)}, bf16[256,1024]{1,0:T(8,128)(2,1)S(1)}, bf16[256,1024]{1,0:T(8,128)(...) custom-call(s32[4,8]{1,0:T(4,128)S(1)} %bitcast.32, ...), custom_call_target="tpu_custom_call" | custom-call | tf_op jit(solution)/shard_map/first_layer/pallas_call | solution.py:398
  17.9 0.0 collective-permute-done.3.refs_14_
  17.9 1.2 %collective-permute-done.4.refs_15_ = bf16[2,128,256]{2,1,0:T(8,128)(2,1)S(1)} collective-permute-done((bf16[2,128,256]{2,1,0:T(8,128)(2,1)S(1)}, bf16[2,128,256]{2,1,0:T(8,128)(2,1)S(1)}, u32[]{:S(2)}, u32[]{:S(2)}) %collective-permute-start.4) | collective-permute-done | bytes 131104 | tf_op jit(solution)/shard_map/ppermute | solution.py:347
  19.1 0.0 collective-permute-done.5.refs_16_
  19.1 0.0 copy-done.1
  19.1 3.7 %second_layer.1 = (bf16[8,128,256]{2,1,0:T(8,128)(2,1)S(1)}, bf16[1088,128]{1,0:T(8,128)(2,1)S(1)}, bf16[1088,128]{1,0:T(8,128)(2,1)S(1)}, bf16[8,128,256]{2,1,0:T(8,128)(2,1)S(1)}) custom-call(s32[4,8]{1,0:T(4,128)S(1)} %bitcast.33, bf16[256,256]{1,0:T(8,128)(2,1)S(1)} %get-tuple-element.57.refs_0_, bf16[256,512]{1,0:T(8,128)(2,1)S(1)} %get-tuple-element.58.refs_1_, ...), custom_call_target="tpu_custom_call" | custom-call | tf_op jit(solution)/shard_map/second_layer/pallas_call | solution.py:434
  22.8 0.1 collective-permute-start.6
  22.9 1.5 %collective-permute-done.6 = bf16[1088,128]{1,0:T(8,128)(2,1)S(1)} collective-permute-done((bf16[1088,128]{1,0:T(8,128)(2,1)S(1)}, bf16[1088,128]{1,0:T(8,128)(2,1)S(1)}, u32[]{:S(2)}, u32[]{:S(2)}) %collective-permute-start.6) | collective-permute-done | bytes 278560 | tf_op jit(solution)/shard_map/ppermute | solution.py:358
  24.4 0.1 split.1
  24.5 1.3 %collective-permute-start.10 = (bf16[272,128]{1,0:T(8,128)(2,1)S(1)}, bf16[272,128]{1,0:T(8,128)(2,1)S(1)}, u32[]{:S(2)}, u32[]{:S(2)}) collective-permute-start(bf16[272,128]{1,0:T(8,128)(2,1)S(1)} %get-tuple-element.82), channel_id=1, source_target_pairs={{0,1},{1,0},{2,3},{3,2},{4,5},{5,4},{6,7},{7,6},{8,9},{9,8},{10,11... | collective-permute-start | bytes 208904 | tf_op jit(solution)/shard_map/ppermute | solution.py:347
  25.8 0.8 %collective-permute-start.11 = (bf16[272,128]{1,0:T(8,128)(2,1)S(1)}, bf16[272,128]{1,0:T(8,128)(2,1)S(1)}, u32[]{:S(2)}, u32[]{:S(2)}) collective-permute-start(bf16[272,128]{1,0:T(8,128)(2,1)S(1)} %get-tuple-element.83), channel_id=1, source_target_pairs={{0,2},{1,3},{2,0},{3,1},{4,6},{5,7},{6,4},{7,5},{8,10},{9,11},{10,... | collective-permute-start | bytes 208904 | tf_op jit(solution)/shard_map/ppermute | solution.py:347
  26.6 1.4 %collective-permute-start.12 = (bf16[272,128]{1,0:T(8,128)(2,1)S(1)}, bf16[272,128]{1,0:T(8,128)(2,1)S(1)}, u32[]{:S(2)}, u32[]{:S(2)}) collective-permute-start(bf16[272,128]{1,0:T(8,128)(2,1)S(1)} %get-tuple-element.84), channel_id=1, source_target_pairs={{0,3},{1,2},{2,1},{3,0},{4,7},{5,6},{6,5},{7,4},{8,11},{9,10},{10,... | collective-permute-start | bytes 208904 | tf_op jit(solution)/shard_map/ppermute | solution.py:347
  28.1 1.0 %store.1 = (bf16[8,128,256]{2,1,0:T(8,128)(2,1)}, bf16[8,128,256]{2,1,0:T(8,128)(2,1)}, f32[8,128]{1,0:T(8,128)S(1)}) custom-call(bf16[8,128,256]{2,1,0:T(8,128)(2,1)S(1)} %get-tuple-element.56.refs_7_.hidden, bf16[8,128,256]{2,1,0:T(8,128)(2,1)S(1)} %get-tuple-element.71.grad_hidden, bf16[272,128]{1,0:T(8,128)(2,1)S(1)} %get-tuple-element.74.after.refs_0_), custom_call_target="tpu_custom_call" | custom-call | tf_op jit(solution)/shard_map/store/pallas_call | solution.py:496
  29.0 0.0 collective-permute-done.10.refs_1_
  29.1 1.6 %collective-permute-done.11.refs_2_ = bf16[272,128]{1,0:T(8,128)(2,1)S(1)} collective-permute-done((bf16[272,128]{1,0:T(8,128)(2,1)S(1)}, bf16[272,128]{1,0:T(8,128)(2,1)S(1)}, u32[]{:S(2)}, u32[]{:S(2)}) %collective-permute-start.11) | collective-permute-done | bytes 69664 | tf_op jit(solution)/shard_map/ppermute | solution.py:347
  30.6 1.2 %collective-permute-done.12.refs_3_ = bf16[272,128]{1,0:T(8,128)(2,1)S(1)} collective-permute-done((bf16[272,128]{1,0:T(8,128)(2,1)S(1)}, bf16[272,128]{1,0:T(8,128)(2,1)S(1)}, u32[]{:S(2)}, u32[]{:S(2)}) %collective-permute-start.12) | collective-permute-done | bytes 69664 | tf_op jit(solution)/shard_map/ppermute | solution.py:347
  31.9 3.7 %collective-permute-start.15 = (bf16[272,128]{1,0:T(8,128)(2,1)S(1)}, bf16[272,128]{1,0:T(8,128)(2,1)S(1)}, u32[]{:S(2)}, u32[]{:S(2)}) collective-permute-start(bf16[272,128]{1,0:T(8,128)(2,1)S(1)} %add.2.refs_0_), channel_id=1, source_target_pairs={{0,24},{4,28},{8,16},{12,20},{16,8},{20,12},{24,0},{28,4},{1,25},{... | collective-permute-start | bytes 208904 | tf_op jit(solution)/shard_map/ppermute | solution.py:355
  35.6 1.6 %collective-permute-start.7 = (bf16[2,128,256]{2,1,0:T(8,128)(2,1)S(1)}, bf16[2,128,256]{2,1,0:T(8,128)(2,1)S(1)}, u32[]{:S(2)}, u32[]{:S(2)}) collective-permute-start(bf16[2,128,256]{2,1,0:T(8,128)(2,1)S(1)} %get-tuple-element.78), channel_id=1, source_target_pairs={{0,1},{1,0},{2,3},{3,2},{4,5},{5,4},{6,7},{7,6},{8,9},{9,8},{10,11... | collective-permute-start | bytes 393224 | tf_op jit(solution)/shard_map/ppermute | solution.py:347
  37.1 0.0 collective-permute-start.14
  37.1 1.0 %collective-permute-start.13 = (bf16[272,128]{1,0:T(8,128)(2,1)S(1)}, bf16[272,128]{1,0:T(8,128)(2,1)S(1)}, u32[]{:S(2)}, u32[]{:S(2)}) collective-permute-start(bf16[272,128]{1,0:T(8,128)(2,1)S(1)} %add.2.refs_0_), channel_id=1, source_target_pairs={{0,8},{4,12},{8,0},{12,4},{16,24},{20,28},{24,16},{28,20},{1,9},{5... | collective-permute-start | bytes 208904 | tf_op jit(solution)/shard_map/ppermute | solution.py:355
  38.2 0.4 collective-permute-start.8
  38.5 0.1 collective-permute-done.15.refs_3_
  38.7 1.6 %collective-permute-start.9 = (bf16[2,128,256]{2,1,0:T(8,128)(2,1)S(1)}, bf16[2,128,256]{2,1,0:T(8,128)(2,1)S(1)}, u32[]{:S(2)}, u32[]{:S(2)}) collective-permute-start(bf16[2,128,256]{2,1,0:T(8,128)(2,1)S(1)} %get-tuple-element.80), channel_id=1, source_target_pairs={{0,3},{1,2},{2,1},{3,0},{4,7},{5,6},{6,5},{7,4},{8,11},{9,10},{10,... | collective-permute-start | bytes 393224 | tf_op jit(solution)/shard_map/ppermute | solution.py:347
  40.3 2.0 %collective-permute-done.14.refs_2_ = bf16[272,128]{1,0:T(8,128)(2,1)S(1)} collective-permute-done((bf16[272,128]{1,0:T(8,128)(2,1)S(1)}, bf16[272,128]{1,0:T(8,128)(2,1)S(1)}, u32[]{:S(2)}, u32[]{:S(2)}) %collective-permute-start.14) | collective-permute-done | bytes 69664 | tf_op jit(solution)/shard_map/ppermute | solution.py:355
  42.3 0.0 collective-permute-done.13.refs_1_
  42.4 1.2 %collective-permute-start.18 = (bf16[272,128]{1,0:T(8,128)(2,1)S(1)}, bf16[272,128]{1,0:T(8,128)(2,1)S(1)}, u32[]{:S(2)}, u32[]{:S(2)}) collective-permute-start(bf16[272,128]{1,0:T(8,128)(2,1)S(1)} %add.3.own), channel_id=1, source_target_pairs={{0,3},{1,2},{2,1},{3,0},{4,7},{5,6},{6,5},{7,4},{8,11},{9,10},{10,... | collective-permute-start | bytes 208904 | tf_op jit(solution)/shard_map/ppermute | solution.py:347
  43.6 0.8 %collective-permute-start.17 = (bf16[272,128]{1,0:T(8,128)(2,1)S(1)}, bf16[272,128]{1,0:T(8,128)(2,1)S(1)}, u32[]{:S(2)}, u32[]{:S(2)}) collective-permute-start(bf16[272,128]{1,0:T(8,128)(2,1)S(1)} %add.3.own), channel_id=1, source_target_pairs={{0,2},{1,3},{2,0},{3,1},{4,6},{5,7},{6,4},{7,5},{8,10},{9,11},{10,... | collective-permute-start | bytes 208904 | tf_op jit(solution)/shard_map/ppermute | solution.py:347
  44.4 0.0 collective-permute-done.7.refs_0_
  44.4 1.5 %collective-permute-start.16 = (bf16[272,128]{1,0:T(8,128)(2,1)S(1)}, bf16[272,128]{1,0:T(8,128)(2,1)S(1)}, u32[]{:S(2)}, u32[]{:S(2)}) collective-permute-start(bf16[272,128]{1,0:T(8,128)(2,1)S(1)} %add.3.own), channel_id=1, source_target_pairs={{0,1},{1,0},{2,3},{3,2},{4,5},{5,4},{6,7},{7,6},{8,9},{9,8},{10,11... | collective-permute-start | bytes 208904 | tf_op jit(solution)/shard_map/ppermute | solution.py:347
  45.9 0.0 collective-permute-done.8.refs_1_
  45.9 0.0 collective-permute-done.9.refs_2_
  45.9 1.5 %aux.1 = (bf16[8,128,256]{2,1,0:T(8,128)(2,1)}, f32[8,128]{1,0:T(8,128)S(1)}) custom-call(s32[2,4]{1,0:T(2,128)S(1)} %bitcast.37, bf16[2,128,256]{2,1,0:T(8,128)(2,1)S(1)} %collective-permute-done.7.refs_0_, bf16[2,128,256]{2,1,0:T(8,128)(2,1)S(1)} %collective-permute-done.8.refs_1_, bf16[2,128,256]{2,1,0:T(8,128)(2,1)S(1)} %collective-permute-done.9.refs_2_), custom_call_target="tpu_custom_call" | custom-call | flops 1000000 | bytes 1000000 | tf_op jit(solution)/shard_map/aux/pallas_call | solution.py:515
  47.4 0.3 collective-permute-done.18.refs_2_
  47.7 0.7 %collective-permute-done.17.refs_1_ = bf16[272,128]{1,0:T(8,128)(2,1)S(1)} collective-permute-done((bf16[272,128]{1,0:T(8,128)(2,1)S(1)}, bf16[272,128]{1,0:T(8,128)(2,1)S(1)}, u32[]{:S(2)}, u32[]{:S(2)}) %collective-permute-start.17) | collective-permute-done | bytes 69664 | tf_op jit(solution)/shard_map/ppermute | solution.py:347
  48.4 0.4 collective-permute-done.16.refs_0_
  48.8 0.1 collective-permute-start.19
  48.9 1.5 %collective-permute-done.19.other = bf16[1088,128]{1,0:T(8,128)(2,1)S(1)} collective-permute-done((bf16[1088,128]{1,0:T(8,128)(2,1)S(1)}, bf16[1088,128]{1,0:T(8,128)(2,1)S(1)}, u32[]{:S(2)}, u32[]{:S(2)}) %collective-permute-start.19) | collective-permute-done | bytes 278560 | tf_op jit(solution)/shard_map/ppermute | solution.py:358
  50.4 1.0 %finish.1 = (f32[256,256]{1,0:T(8,128)}, f32[256,256]{1,0:T(8,128)}, f32[256,256]{1,0:T(8,128)}, f32[256,256]{1,0:T(8,128)}, f32[32,256]{1,0:T(8,128)}, /*index=5*/f32[1,1]{1,0:T(1,128)}) custom-call(bf16[1088,128]{1,0:T(8,128)(2,1)S(1)} %bitcast.25, bf16[1088,128]{1,0:T(8,128)(2,1)S(1)} %collective-permute-done.19.other), custom_call_target="tpu_custom_call" | custom-call | tf_op jit(solution)/shard_map/finish/pallas_call | solution.py:540
  (12 shorter events, 0.1 us)
Async XLA Ops:
  0.6 12.4 %copy-start = (bf16[1,1,8,4,128,128]{5,4,3,2,1,0:T(8,128)(2,1)S(1)}, bf16[1,1,8,4,128,128]{5,4,3,2,1,0:T(8,128)(2,1)}, u32[]{:S(2)}) copy-start(bf16[1,1,8,4,128,128]{5,4,3,2,1,0:T(8,128)(2,1)} %param.16) | copy-start | bytes 3145732
  0.7 0.8 %copy-start.11 = (s32[1,1,4,2]{2,3,1,0:T(2,128)S(1)}, s32[1,1,4,2]{2,3,1,0:T(2,128)}, u32[]{:S(2)}) copy-start(s32[1,1,4,2]{2,3,1,0:T(2,128)} %param.18) | copy-start | bytes 100
  2.7 8.0 %collective-permute-start = (bf16[2,128,256]{2,1,0:T(8,128)(2,1)S(1)}, bf16[2,128,256]{2,1,0:T(8,128)(2,1)S(1)}, u32[]{:S(2)}, u32[]{:S(2)}) collective-permute-start(bf16[2,128,256]{2,1,0:T(8,128)(2,1)S(1)} %get-tuple-element.53), channel_id=1, source_target_pairs={{0,1},{1,0},{2,3},{3,2},{4,5},{5,4},{6,7},{7,6},{8,9},{9,8},{10,11... | collective-permute-start | bytes 393224 | tf_op jit(solution)/shard_map/ppermute | solution.py:347
  5.7 9.2 %collective-permute-start.1 = (bf16[2,128,256]{2,1,0:T(8,128)(2,1)S(1)}, bf16[2,128,256]{2,1,0:T(8,128)(2,1)S(1)}, u32[]{:S(2)}, u32[]{:S(2)}) collective-permute-start(bf16[2,128,256]{2,1,0:T(8,128)(2,1)S(1)} %get-tuple-element.54), channel_id=1, source_target_pairs={{0,2},{1,3},{2,0},{3,1},{4,6},{5,7},{6,4},{7,5},{8,10},{9,11},{10,... | collective-permute-start | bytes 393224 | tf_op jit(solution)/shard_map/ppermute | solution.py:347
  7.2 7.7 %collective-permute-start.2 = (bf16[2,128,256]{2,1,0:T(8,128)(2,1)S(1)}, bf16[2,128,256]{2,1,0:T(8,128)(2,1)S(1)}, u32[]{:S(2)}, u32[]{:S(2)}) collective-permute-start(bf16[2,128,256]{2,1,0:T(8,128)(2,1)S(1)} %get-tuple-element.55), channel_id=1, source_target_pairs={{0,3},{1,2},{2,1},{3,0},{4,7},{5,6},{6,5},{7,4},{8,11},{9,10},{10,... | collective-permute-start | bytes 393224 | tf_op jit(solution)/shard_map/ppermute | solution.py:347
  7.2 10.7 %collective-permute-start.3 = (bf16[2,128,256]{2,1,0:T(8,128)(2,1)S(1)}, bf16[2,128,256]{2,1,0:T(8,128)(2,1)S(1)}, u32[]{:S(2)}, u32[]{:S(2)}) collective-permute-start(bf16[2,128,256]{2,1,0:T(8,128)(2,1)S(1)} %get-tuple-element.68), channel_id=1, source_target_pairs={{0,1},{1,0},{2,3},{3,2},{4,5},{5,4},{6,7},{7,6},{8,9},{9,8},{10,11... | collective-permute-start | bytes 393224 | tf_op jit(solution)/shard_map/ppermute | solution.py:347
  9.2 9.9 %collective-permute-start.4 = (bf16[2,128,256]{2,1,0:T(8,128)(2,1)S(1)}, bf16[2,128,256]{2,1,0:T(8,128)(2,1)S(1)}, u32[]{:S(2)}, u32[]{:S(2)}) collective-permute-start(bf16[2,128,256]{2,1,0:T(8,128)(2,1)S(1)} %get-tuple-element.69), channel_id=1, source_target_pairs={{0,2},{1,3},{2,0},{3,1},{4,6},{5,7},{6,4},{7,5},{8,10},{9,11},{10,... | collective-permute-start | bytes 393224 | tf_op jit(solution)/shard_map/ppermute | solution.py:347
  10.7 8.4 %collective-permute-start.5 = (bf16[2,128,256]{2,1,0:T(8,128)(2,1)S(1)}, bf16[2,128,256]{2,1,0:T(8,128)(2,1)S(1)}, u32[]{:S(2)}, u32[]{:S(2)}) collective-permute-start(bf16[2,128,256]{2,1,0:T(8,128)(2,1)S(1)} %get-tuple-element.70), channel_id=1, source_target_pairs={{0,3},{1,2},{2,1},{3,0},{4,7},{5,6},{6,5},{7,4},{8,11},{9,10},{10,... | collective-permute-start | bytes 393224 | tf_op jit(solution)/shard_map/ppermute | solution.py:347
  13.0 1.0 %copy-start.2 = (bf16[1,1,1024,256]{3,2,1,0:T(8,128)(2,1)S(1)}, bf16[1,1,1024,256]{3,2,1,0:T(8,128)(2,1)}, u32[]{:S(2)}) copy-start(bf16[1,1,1024,256]{3,2,1,0:T(8,128)(2,1)} %param.13) | copy-start | bytes 1572868
  14.1 0.9 %copy-start.3 = (bf16[256,256]{1,0:T(8,128)(2,1)S(1)}, bf16[256,256]{1,0:T(8,128)(2,1)}, u32[]{:S(2)}) copy-start(bf16[256,256]{1,0:T(8,128)(2,1)} %wn.1) | copy-start | bytes 393220
  14.1 1.0 %copy-start.4 = (bf16[256,256]{1,0:T(8,128)(2,1)S(1)}, bf16[256,256]{1,0:T(8,128)(2,1)}, u32[]{:S(2)}) copy-start(bf16[256,256]{1,0:T(8,128)(2,1)} %ws.1) | copy-start | bytes 393220
  14.1 1.0 %copy-start.5 = (bf16[256,256]{1,0:T(8,128)(2,1)S(1)}, bf16[256,256]{1,0:T(8,128)(2,1)}, u32[]{:S(2)}) copy-start(bf16[256,256]{1,0:T(8,128)(2,1)} %wn_next.1) | copy-start | bytes 393220
  14.1 1.1 %copy-start.6 = (bf16[256,256]{1,0:T(8,128)(2,1)S(1)}, bf16[256,256]{1,0:T(8,128)(2,1)}, u32[]{:S(2)}) copy-start(bf16[256,256]{1,0:T(8,128)(2,1)} %ws_next.1) | copy-start | bytes 393220
  14.1 1.1 %copy-start.7 = (bf16[256,32]{0,1:T(8,128)(2,1)S(1)}, bf16[256,32]{0,1:T(8,128)(2,1)}, u32[]{:S(2)}) copy-start(bf16[256,32]{0,1:T(8,128)(2,1)} %param.25) | copy-start | bytes 49156
  14.1 1.1 %copy-start.10 = (s32[1,1,1024]{2,1,0:T(1,128)S(1)}, s32[1,1,1024]{2,1,0:T(1,128)}, u32[]{:S(2)}) copy-start(s32[1,1,1024]{2,1,0:T(1,128)} %param.20) | copy-start | bytes 12292
  14.9 0.7 %copy-start.9 = (s32[1,1,1024]{2,1,0:T(1,128)S(1)}, s32[1,1,1024]{2,1,0:T(1,128)}, u32[]{:S(2)}) copy-start(s32[1,1,1024]{2,1,0:T(1,128)} %param.19) | copy-start | bytes 12292
  14.9 0.8 %copy-start.8 = (s32[1,1,8,4]{2,3,1,0:T(4,128)S(1)}, s32[1,1,8,4]{2,3,1,0:T(4,128)}, u32[]{:S(2)}) copy-start(s32[1,1,8,4]{2,3,1,0:T(4,128)} %param.17) | copy-start | bytes 388
  15.7 3.4 %copy-start.1 = (bf16[1,1,1024,256]{3,2,1,0:T(8,128)(2,1)S(1)}, bf16[1,1,1024,256]{3,2,1,0:T(8,128)(2,1)}, u32[]{:S(2)}) copy-start(bf16[1,1,1024,256]{3,2,1,0:T(8,128)(2,1)} %param.15) | copy-start | bytes 1572868
  22.8 1.6 %collective-permute-start.6 = (bf16[1088,128]{1,0:T(8,128)(2,1)S(1)}, bf16[1088,128]{1,0:T(8,128)(2,1)S(1)}, u32[]{:S(2)}, u32[]{:S(2)}) collective-permute-start(bf16[1088,128]{1,0:T(8,128)(2,1)S(1)} %get-tuple-element.73), channel_id=1, source_target_pairs={{0,4},{4,0},{8,12},{12,8},{16,20},{20,16},{24,28},{28,24},{1,5},{5... | collective-permute-start | bytes 835592 | tf_op jit(solution)/shard_map/ppermute | solution.py:358
  24.5 4.5 %collective-permute-start.10 = (bf16[272,128]{1,0:T(8,128)(2,1)S(1)}, bf16[272,128]{1,0:T(8,128)(2,1)S(1)}, u32[]{:S(2)}, u32[]{:S(2)}) collective-permute-start(bf16[272,128]{1,0:T(8,128)(2,1)S(1)} %get-tuple-element.82), channel_id=1, source_target_pairs={{0,1},{1,0},{2,3},{3,2},{4,5},{5,4},{6,7},{7,6},{8,9},{9,8},{10,11... | collective-permute-start | bytes 208904 | tf_op jit(solution)/shard_map/ppermute | solution.py:347
  25.8 4.9 %collective-permute-start.11 = (bf16[272,128]{1,0:T(8,128)(2,1)S(1)}, bf16[272,128]{1,0:T(8,128)(2,1)S(1)}, u32[]{:S(2)}, u32[]{:S(2)}) collective-permute-start(bf16[272,128]{1,0:T(8,128)(2,1)S(1)} %get-tuple-element.83), channel_id=1, source_target_pairs={{0,2},{1,3},{2,0},{3,1},{4,6},{5,7},{6,4},{7,5},{8,10},{9,11},{10,... | collective-permute-start | bytes 208904 | tf_op jit(solution)/shard_map/ppermute | solution.py:347
  26.6 5.2 %collective-permute-start.12 = (bf16[272,128]{1,0:T(8,128)(2,1)S(1)}, bf16[272,128]{1,0:T(8,128)(2,1)S(1)}, u32[]{:S(2)}, u32[]{:S(2)}) collective-permute-start(bf16[272,128]{1,0:T(8,128)(2,1)S(1)} %get-tuple-element.84), channel_id=1, source_target_pairs={{0,3},{1,2},{2,1},{3,0},{4,7},{5,6},{6,5},{7,4},{8,11},{9,10},{10,... | collective-permute-start | bytes 208904 | tf_op jit(solution)/shard_map/ppermute | solution.py:347
  31.9 6.8 %collective-permute-start.15 = (bf16[272,128]{1,0:T(8,128)(2,1)S(1)}, bf16[272,128]{1,0:T(8,128)(2,1)S(1)}, u32[]{:S(2)}, u32[]{:S(2)}) collective-permute-start(bf16[272,128]{1,0:T(8,128)(2,1)S(1)} %add.2.refs_0_), channel_id=1, source_target_pairs={{0,24},{4,28},{8,16},{12,20},{16,8},{20,12},{24,0},{28,4},{1,25},{... | collective-permute-start | bytes 208904 | tf_op jit(solution)/shard_map/ppermute | solution.py:355
  35.6 8.9 %collective-permute-start.7 = (bf16[2,128,256]{2,1,0:T(8,128)(2,1)S(1)}, bf16[2,128,256]{2,1,0:T(8,128)(2,1)S(1)}, u32[]{:S(2)}, u32[]{:S(2)}) collective-permute-start(bf16[2,128,256]{2,1,0:T(8,128)(2,1)S(1)} %get-tuple-element.78), channel_id=1, source_target_pairs={{0,1},{1,0},{2,3},{3,2},{4,5},{5,4},{6,7},{7,6},{8,9},{9,8},{10,11... | collective-permute-start | bytes 393224 | tf_op jit(solution)/shard_map/ppermute | solution.py:347
  37.1 5.2 %collective-permute-start.14 = (bf16[272,128]{1,0:T(8,128)(2,1)S(1)}, bf16[272,128]{1,0:T(8,128)(2,1)S(1)}, u32[]{:S(2)}, u32[]{:S(2)}) collective-permute-start(bf16[272,128]{1,0:T(8,128)(2,1)S(1)} %add.2.refs_0_), channel_id=1, source_target_pairs={{0,16},{4,20},{8,24},{12,28},{16,0},{20,4},{24,8},{28,12},{1,17},{... | collective-permute-start | bytes 208904 | tf_op jit(solution)/shard_map/ppermute | solution.py:355
  37.1 5.2 %collective-permute-start.13 = (bf16[272,128]{1,0:T(8,128)(2,1)S(1)}, bf16[272,128]{1,0:T(8,128)(2,1)S(1)}, u32[]{:S(2)}, u32[]{:S(2)}) collective-permute-start(bf16[272,128]{1,0:T(8,128)(2,1)S(1)} %add.2.refs_0_), channel_id=1, source_target_pairs={{0,8},{4,12},{8,0},{12,4},{16,24},{20,28},{24,16},{28,20},{1,9},{5... | collective-permute-start | bytes 208904 | tf_op jit(solution)/shard_map/ppermute | solution.py:355
  38.2 7.8 %collective-permute-start.8 = (bf16[2,128,256]{2,1,0:T(8,128)(2,1)S(1)}, bf16[2,128,256]{2,1,0:T(8,128)(2,1)S(1)}, u32[]{:S(2)}, u32[]{:S(2)}) collective-permute-start(bf16[2,128,256]{2,1,0:T(8,128)(2,1)S(1)} %get-tuple-element.79), channel_id=1, source_target_pairs={{0,2},{1,3},{2,0},{3,1},{4,6},{5,7},{6,4},{7,5},{8,10},{9,11},{10,... | collective-permute-start | bytes 393224 | tf_op jit(solution)/shard_map/ppermute | solution.py:347
  38.7 7.3 %collective-permute-start.9 = (bf16[2,128,256]{2,1,0:T(8,128)(2,1)S(1)}, bf16[2,128,256]{2,1,0:T(8,128)(2,1)S(1)}, u32[]{:S(2)}, u32[]{:S(2)}) collective-permute-start(bf16[2,128,256]{2,1,0:T(8,128)(2,1)S(1)} %get-tuple-element.80), channel_id=1, source_target_pairs={{0,3},{1,2},{2,1},{3,0},{4,7},{5,6},{6,5},{7,4},{8,11},{9,10},{10,... | collective-permute-start | bytes 393224 | tf_op jit(solution)/shard_map/ppermute | solution.py:347
  42.4 5.3 %collective-permute-start.18 = (bf16[272,128]{1,0:T(8,128)(2,1)S(1)}, bf16[272,128]{1,0:T(8,128)(2,1)S(1)}, u32[]{:S(2)}, u32[]{:S(2)}) collective-permute-start(bf16[272,128]{1,0:T(8,128)(2,1)S(1)} %add.3.own), channel_id=1, source_target_pairs={{0,3},{1,2},{2,1},{3,0},{4,7},{5,6},{6,5},{7,4},{8,11},{9,10},{10,... | collective-permute-start | bytes 208904 | tf_op jit(solution)/shard_map/ppermute | solution.py:347
  43.6 4.8 %collective-permute-start.17 = (bf16[272,128]{1,0:T(8,128)(2,1)S(1)}, bf16[272,128]{1,0:T(8,128)(2,1)S(1)}, u32[]{:S(2)}, u32[]{:S(2)}) collective-permute-start(bf16[272,128]{1,0:T(8,128)(2,1)S(1)} %add.3.own), channel_id=1, source_target_pairs={{0,2},{1,3},{2,0},{3,1},{4,6},{5,7},{6,4},{7,5},{8,10},{9,11},{10,... | collective-permute-start | bytes 208904 | tf_op jit(solution)/shard_map/ppermute | solution.py:347
  44.4 4.3 %collective-permute-start.16 = (bf16[272,128]{1,0:T(8,128)(2,1)S(1)}, bf16[272,128]{1,0:T(8,128)(2,1)S(1)}, u32[]{:S(2)}, u32[]{:S(2)}) collective-permute-start(bf16[272,128]{1,0:T(8,128)(2,1)S(1)} %add.3.own), channel_id=1, source_target_pairs={{0,1},{1,0},{2,3},{3,2},{4,5},{5,4},{6,7},{7,6},{8,9},{9,8},{10,11... | collective-permute-start | bytes 208904 | tf_op jit(solution)/shard_map/ppermute | solution.py:347
  48.8 1.6 %collective-permute-start.19 = (bf16[1088,128]{1,0:T(8,128)(2,1)S(1)}, bf16[1088,128]{1,0:T(8,128)(2,1)S(1)}, u32[]{:S(2)}, u32[]{:S(2)}) collective-permute-start(bf16[1088,128]{1,0:T(8,128)(2,1)S(1)} %bitcast.24), channel_id=1, source_target_pairs={{0,4},{4,0},{8,12},{12,8},{16,20},{20,16},{24,28},{28,24},{1,5},{5... | collective-permute-start | bytes 835592 | tf_op jit(solution)/shard_map/ppermute | solution.py:358
